TPU v7x, 512 devices: a whole 4x4x16 slice. The times are simulated.
512 devices in a mesh: ta: 16 (over z), gz: 4 (over x_hi, core), gy: 8 (over y, x_lo).
Axes of the slice: x: 4 (x_hi: 2, x_lo: 2; x = x_hi * 2 + x_lo), y: 4, z: 16, core: 2. Of those that a mesh axis runs over, the one named last changes fastest.
Arguments:
- sources: float32 [4, 2, 4, 3, 32, 8, 1024], P(None, None, None, None, 'ta', 'gz', 'gy'), may hold values from -10 to 10
- gauge_links: float32 [2, 4, 2, 3, 3, 32, 8, 1024], P(None, None, None, None, None, 'ta', 'gz', 'gy'), may hold values from -2.5 to 2.5
Outputs:
- solution: float32 [4, 2, 4, 3, 32, 8, 1024], P(None, None, None, None, 'ta', 'gz', 'gy')
- residual: float32 [4, 2, 4, 3, 32, 8, 1024], P(None, None, None, None, 'ta', 'gz', 'gy')
All inputs are finite; a program needn't handle non-finite values.
Results may differ from a plain program's by a relative error of at most 0.0003.
Values sent between devices are 32-bit elements; how exact they have to be, the bound alone decides.
No kernel may reach another device: no remote copies, remote signals or barrier semaphores. Data moves between devices by JAX's collectives and lax.ppermute only.
A program may use at most 128 MiB of HBM per device.

v0:
```python
import jax
import jax.numpy as jnp
from jax import lax
from jax.sharding import PartitionSpec as P

NX = 64
ITERS = 2


kappa_square = 0.0196
gamma_columns = ((3, 2, 1, 0), (3, 2, 1, 0), (2, 3, 0, 1), (2, 3, 0, 1))
gamma_phases = (
    ((0, 1), (0, 1), (0, -1), (0, -1)),
    ((1, 0), (-1, 0), (-1, 0), (1, 0)),
    ((0, 1), (0, -1), (0, -1), (0, 1)),
    ((1, 0), (1, 0), (1, 0), (1, 0)),
)


def with_halo(block, sides, width):
    for axis, dim in sides:
        count = lax.axis_size(axis)
        forward = [(i, i + 1) for i in range(count - 1)]
        forward.append((count - 1, 0))
        backward = [(target, source) for source, target in forward]
        low = lax.ppermute(
            lax.slice_in_dim(block, block.shape[dim] - width, None, axis=dim), axis, forward
        )
        high = lax.ppermute(lax.slice_in_dim(block, 0, width, axis=dim), axis, backward)
        block = jnp.concatenate([low, block, high], axis=dim)
    return block


def phase_times(phase, real_part, imag_part):
    if phase[1] == 0:
        if phase[0] == 1:
            return (real_part, imag_part)
        return (-real_part, -imag_part)
    if phase[1] == 1:
        return (-imag_part, real_part)
    return (imag_part, -real_part)


def project(spinor, direction, hop_sign, row_count):
    real_rows = []
    imag_rows = []
    for spin_row in range(row_count):
        partner = gamma_columns[direction][spin_row]
        moved_real, moved_imag = phase_times(
            gamma_phases[direction][spin_row], spinor[:, 0, partner], spinor[:, 1, partner]
        )
        if hop_sign > 0:
            real_rows.append(spinor[:, 0, spin_row] + moved_real)
            imag_rows.append(spinor[:, 1, spin_row] + moved_imag)
        else:
            real_rows.append(spinor[:, 0, spin_row] - moved_real)
            imag_rows.append(spinor[:, 1, spin_row] - moved_imag)
    return jnp.stack([jnp.stack(real_rows, 1), jnp.stack(imag_rows, 1)], 1)


def rebuild(half_rows, direction, hop_sign):
    real_rows = [half_rows[:, 0, 0], half_rows[:, 0, 1]]
    imag_rows = [half_rows[:, 1, 0], half_rows[:, 1, 1]]
    for spin_row in (2, 3):
        partner = gamma_columns[direction][spin_row]
        moved_real, moved_imag = phase_times(
            gamma_phases[direction][spin_row], half_rows[:, 0, partner], half_rows[:, 1, partner]
        )
        if hop_sign < 0:
            moved_real, moved_imag = (-moved_real, -moved_imag)
        real_rows.append(moved_real)
        imag_rows.append(moved_imag)
    return jnp.stack([jnp.stack(real_rows, 1), jnp.stack(imag_rows, 1)], 1)


def color_times(link, spinor, adjoint):
    link_real = link[0]
    link_imag = link[1]
    if adjoint:
        link_real = jnp.swapaxes(link_real, 0, 1)
        link_imag = -jnp.swapaxes(link_imag, 0, 1)
    spin_real = spinor[:, 0]
    spin_imag = spinor[:, 1]
    out_real = None
    out_imag = None
    for column in range(3):
        entry_real = link_real[:, column]
        entry_imag = link_imag[:, column]
        part_real = (
            entry_real * spin_real[:, :, column : column + 1]
            - entry_imag * spin_imag[:, :, column : column + 1]
        )
        part_imag = (
            entry_real * spin_imag[:, :, column : column + 1]
            + entry_imag * spin_real[:, :, column : column + 1]
        )
        if out_real is None:
            out_real, out_imag = (part_real, part_imag)
        else:
            out_real = out_real + part_real
            out_imag = out_imag + part_imag
    return jnp.stack([out_real, out_imag], 1)


def next_cell(values, half_x, cell_x):
    return jnp.where(
        cell_x == half_x - 1, jnp.roll(values, half_x - 1, -1), jnp.roll(values, -1, -1)
    )


def prior_cell(values, half_x, cell_x):
    return jnp.where(cell_x == 0, jnp.roll(values, 1 - half_x, -1), jnp.roll(values, 1, -1))


def move_time(forward, backward, top_sign, bottom_sign):
    slab = forward.shape[4]
    rims = jnp.concatenate([forward[:, :, :, :, 0:1], backward[:, :, :, :, slab - 1 : slab]], 4)
    padded = with_halo(rims, (("ta", 4),), 1)
    from_above = padded[:, :, :, :, 3:4] * top_sign
    from_below = padded[:, :, :, :, 0:1] * bottom_sign
    forward = jnp.concatenate([forward[:, :, :, :, 1:], from_above], 4)
    backward = jnp.concatenate([from_below, backward[:, :, :, :, : slab - 1]], 4)
    return (forward, backward)


def move_depth(forward, backward):
    slab = forward.shape[5]
    rims = jnp.concatenate(
        [forward[:, :, :, :, :, 0:1], backward[:, :, :, :, :, slab - 1 : slab]], 5
    )
    padded = with_halo(rims, (("gz", 5),), 1)
    forward = jnp.concatenate([forward[:, :, :, :, :, 1:], padded[:, :, :, :, :, 3:4]], 5)
    backward = jnp.concatenate([padded[:, :, :, :, :, 0:1], backward[:, :, :, :, :, : slab - 1]], 5)
    return (forward, backward)


def move_row(forward, backward, half_x):
    slab = forward.shape[6]
    rims = jnp.concatenate([forward[..., :half_x], backward[..., slab - half_x :]], 6)
    padded = with_halo(rims, (("gy", 6),), half_x)
    forward = jnp.concatenate([forward[..., half_x:], padded[..., 3 * half_x :]], 6)
    backward = jnp.concatenate([padded[..., :half_x], backward[..., : slab - half_x]], 6)
    return (forward, backward)


def hopping(spinor, gauge_links, out_parity, context, row_count):
    row_parity, cell_x, half_x, top_sign, bottom_sign = context
    shift_odd = (row_parity + out_parity) % 2
    summed = jnp.zeros_like(spinor)
    for direction in range(4):
        forward = project(spinor, direction, -1, row_count)
        backward = color_times(
            gauge_links[1 - out_parity, direction], project(spinor, direction, 1, row_count), True
        )
        if direction == 0:
            forward = jnp.where(shift_odd == 1, next_cell(forward, half_x, cell_x), forward)
            backward = jnp.where(shift_odd == 0, prior_cell(backward, half_x, cell_x), backward)
        elif direction == 1:
            forward, backward = move_row(forward, backward, half_x)
        elif direction == 2:
            forward, backward = move_depth(forward, backward)
        else:
            forward, backward = move_time(forward, backward, top_sign, bottom_sign)
        forward = color_times(gauge_links[out_parity, direction], forward, False)
        forward = rebuild(forward, direction, -1)
        backward = rebuild(backward, direction, 1)
        summed = summed + forward + backward
    return summed


def wilson_even(spinor, gauge_links, context, row_count):
    return spinor - kappa_square * hopping(
        hopping(spinor, gauge_links, 1, context, row_count), gauge_links, 0, context, row_count
    )


def normal_operator(spinor, gauge_links, context, row_count):
    gamma_five = jnp.array([1.0, 1.0, -1.0, -1.0], jnp.float32).reshape(1, 1, 4, 1, 1, 1, 1)
    once = gamma_five * wilson_even(spinor, gauge_links, context, row_count)
    return gamma_five * wilson_even(once, gauge_links, context, row_count)


def contract(left_flat, right_flat):
    return lax.dot_general(
        left_flat,
        right_flat,
        (((1,), (1,)), ((), ())),
        precision=lax.Precision.HIGHEST,
        preferred_element_type=jnp.float32,
    )


def matmul(left_mat, right_mat):
    return jnp.dot(
        left_mat, right_mat, precision=lax.Precision.HIGHEST, preferred_element_type=jnp.float32
    )


def gram(left, right):
    source_count = left.shape[0]
    left_real = left[:, 0].reshape(source_count, -1)
    left_imag = left[:, 1].reshape(source_count, -1)
    right_real = right[:, 0].reshape(source_count, -1)
    right_imag = right[:, 1].reshape(source_count, -1)
    real_part = contract(left_real, right_real) + contract(left_imag, right_imag)
    imag_part = contract(left_real, right_imag) - contract(left_imag, right_real)
    return jnp.stack([real_part, imag_part])


def combine(spinors, coeffs):
    source_count = spinors.shape[0]
    real_flat = spinors[:, 0].reshape(source_count, -1)
    imag_flat = spinors[:, 1].reshape(source_count, -1)
    real_new = matmul(coeffs[0].T, real_flat) - matmul(coeffs[1].T, imag_flat)
    imag_new = matmul(coeffs[0].T, imag_flat) + matmul(coeffs[1].T, real_flat)
    return jnp.stack([real_new, imag_new], 1).reshape(spinors.shape)


def cholesky_solve(factor, rhs_rows):
    order_size = factor.shape[0]
    forward_rows = []
    for row_index in range(order_size):
        running = rhs_rows[row_index]
        for col_index in range(row_index):
            running = running - factor[row_index, col_index] * forward_rows[col_index]
        forward_rows.append(running / factor[row_index, row_index])
    back_rows = [None] * order_size
    for row_index in reversed(range(order_size)):
        running = forward_rows[row_index]
        for col_index in range(row_index + 1, order_size):
            running = running - factor[col_index, row_index] * back_rows[col_index]
        back_rows[row_index] = running / factor[row_index, row_index]
    return jnp.stack(back_rows)


def complex_solve(matrix, rhs):
    upper = jnp.concatenate([matrix[0], -matrix[1]], 1)
    lower = jnp.concatenate([matrix[1], matrix[0]], 1)
    embedded = jnp.concatenate([upper, lower], 0)
    embedded = 0.5 * (embedded + embedded.T)
    factor = jnp.linalg.cholesky(embedded)
    stacked = jnp.concatenate([rhs[0], rhs[1]], 0)
    solved = cholesky_solve(factor, stacked)
    half_count = rhs.shape[1]
    return jnp.stack([solved[:half_count], solved[half_count:]])


def residual_total(residual):
    return lax.psum(gram(residual, residual), ("ta", "gz", "gy"))


def local(sources, gauge_links):
    slab_time = sources.shape[4]
    slab_depth = sources.shape[5]
    slab_flat = sources.shape[6]
    half_x = NX // 2
    time_iota = lax.broadcasted_iota(jnp.int32, (slab_time, slab_depth, slab_flat), 0)
    depth_iota = lax.broadcasted_iota(jnp.int32, (slab_time, slab_depth, slab_flat), 1)
    flat_iota = lax.broadcasted_iota(jnp.int32, (slab_time, slab_depth, slab_flat), 2)
    row_parity = (time_iota + depth_iota + flat_iota // half_x) % 2
    cell_x = flat_iota % half_x
    time_place = lax.axis_index("ta")
    top_sign = jnp.where(time_place == lax.axis_size("ta") - 1, -1.0, 1.0).astype(jnp.float32)
    bottom_sign = jnp.where(time_place == 0, -1.0, 1.0).astype(jnp.float32)
    context = (row_parity, cell_x, half_x, top_sign, bottom_sign)
    row_count = 2
    solution = jnp.zeros_like(sources)
    residual = sources
    search = sources
    residual_gram = residual_total(residual)
    for iteration in range(ITERS):
        images = normal_operator(search, gauge_links, context, row_count)
        curvature = lax.psum(gram(search, images), ("ta", "gz", "gy"))
        step_coeffs = complex_solve(curvature, residual_gram)
        solution = solution + combine(search, step_coeffs)
        residual = residual - combine(images, step_coeffs)
        if iteration + 1 < ITERS:
            next_gram = residual_total(residual)
            mixing = complex_solve(residual_gram, next_gram)
            search = residual + combine(search, mixing)
            residual_gram = next_gram
    return (solution, residual)


def solution(mesh):
    in_specs = (
        P(None, None, None, None, "ta", "gz", "gy"),
        P(None, None, None, None, None, "ta", "gz", "gy"),
    )
    out_specs = (
        P(None, None, None, None, "ta", "gz", "gy"),
        P(None, None, None, None, "ta", "gz", "gy"),
    )
    return jax.shard_map(local, mesh=mesh, in_specs=in_specs, out_specs=out_specs, check_vma=False)
```

profile of v0, /device:TPU:1, one launch (start us, length us, event | category | flops | bytes accessed | tf_op | source)
XLA Modules:
  0.0 688.9 jit_solution(7735612875795705263)
XLA Ops:
  1.9 6.5 collective-permute-start
  8.9 1.9 collective-permute-start.1
  10.9 6.3 collective-permute-start.2
  17.4 1.9 collective-permute-start.3
  19.4 10.0 %collective-permute-start.4 = (f32[4,2,2,3,1,2,128]{6,0,5,4,3,2,1:T(4,128)S(1)}, f32[4,2,2,3,1,2,128]{6,0,5,4,3,2,1:T(4,128)S(1)}, u32[]{:S(2)}, u32[]{:S(2)}) collective-permute-start(f32[4,2,2,3,1,2,128]{6,0,5,4,3,2,1:T(4,128)S(1)} %get-tuple-element.723), channel_id=1, source_target_pairs={{32,0},{64,32},{96,64},{128,96},{160,128},{192,160},{224,192},{256... | collective-permute-start | bytes 147464 | tf_op jit(solution)/shard_map/ppermute | solution.py:29
  33.6 1.9 collective-permute-start.5
  36.7 3.5 collective-permute-done.5
  42.6 1.9 collective-permute-start.11
  44.6 4.6 collective-permute-start.10
  49.3 3.9 collective-permute-start.9
  53.3 1.9 collective-permute-start.8
  55.4 1.9 collective-permute-start.7
  57.5 5.9 collective-permute-done.7
  63.4 2.5 collective-permute-start.6
  66.1 2.6 collective-permute-done.6
  73.0 4.7 collective-permute-start.12
  77.9 1.9 collective-permute-start.13
  79.9 6.8 collective-permute-start.14
  86.8 3.5 collective-permute-start.15
  90.4 1.9 collective-permute-start.16
  92.6 3.8 collective-permute-start.17
  97.5 1.6 collective-permute-done.17
  101.4 2.4 collective-permute-start.23
  103.9 4.4 collective-permute-start.21
  108.4 1.9 collective-permute-start.20
  110.6 1.9 collective-permute-start.19
  112.7 3.9 collective-permute-start.22
  116.6 1.7 collective-permute-done.19
  118.3 3.8 collective-permute-start.18
  128.0 103.3 %all-reduce = (f32[2,4,4]{2,1,0:T(4,128)S(1)}, f32[2,4,4]{2,1,0:T(4,128)S(1)}) all-reduce(f32[2,4,4]{2,1,0:T(4,128)S(1)} %pad_maximum_fusion.152, f32[2,4,4]{2,1,0:T(4,128)S(1)} %pad_maximum_fusion.153), channel_id=1, replica_groups=mesh['ta'=16,'gz'=4,'gy'=8] {'ta','gz','gy'}, use_global_device_ids=true, to_apply=%region_0.1 | all-reduce | flops 64 | bytes 512 | tf_op jit(solution)/shard_map/psum | solution.py:249
  236.5 17.1 %subtract_divide_fusion.30 = (f32[1,4]{1,0:T(1,128)S(1)}, f32[1,4]{1,0:T(1,128)S(1)}, f32[1,4]{1,0:T(1,128)S(1)}, f32[1,4]{1,0:T(1,128)S(1)}, f32[1,4]{1,0:T(1,1...) fusion(f32[2,4,4]{2,1,0:T(4,128)S(1)} %get-tuple-element.5, f32[]{:T(128)} %bitcast.680, f32[]{:T(128)} %bitcast.679, ...), kind=kLoop, calls=%fused_computation.2792 | loop fusion | flops 196 | bytes 336 | tf_op jit(solution)/shard_map/div | solution.py:226
  253.6 21.7 %subtract_divide_fusion.22 = (f32[1,4]{1,0:T(1,128)S(1)}, f32[1,4]{1,0:T(1,128)S(1)}, f32[1,4]{1,0:T(1,128)S(1)}, f32[1,4]{1,0:T(1,128)S(1)}, f32[1,4]{1,0:T(1,1...) fusion(f32[1,4]{1,0:T(1,128)S(1)} %get-tuple-element.51, f32[]{:T(128)} %bitcast.646, ...), kind=kLoop, calls=%fused_computation.2784 | loop fusion | flops 312 | bytes 400 | tf_op jit(solution)/shard_map/div | solution.py:232
  283.9 99.8 %psum.30 = f32[2,4,4]{2,1,0:T(4,128)S(1)} all-reduce(f32[2,4,4]{2,1,0:T(4,128)S(1)} %pad_maximum_fusion.154), channel_id=1, replica_groups=mesh['ta'=16,'gz'=4,'gy'=8] {'ta','gz','gy'}, use_global_device_ids=true, to_apply=%region_4.6 | all-reduce | flops 32 | bytes 256 | tf_op jit(solution)/shard_map/psum | solution.py:249
  384.9 17.1 %subtract_divide_fusion.19 = (f32[1,4]{1,0:T(1,128)S(1)}, f32[1,4]{1,0:T(1,128)S(1)}, f32[1,4]{1,0:T(1,128)S(1)}, f32[1,4]{1,0:T(1,128)S(1)}, f32[1,4]{1,0:T(1,1...) fusion(f32[2,4,4]{2,1,0:T(4,128)S(1)} %psum.30, f32[]{:T(128)} %bitcast.748, f32[]{:T(128)} %bitcast.747, ...), kind=kLoop, calls=%fused_computation.2781 | loop fusion | flops 196 | bytes 336 | tf_op jit(solution)/shard_map/div | solution.py:226
  402.1 21.7 %subtract_divide_fusion.11 = (f32[1,4]{1,0:T(1,128)S(1)}, f32[1,4]{1,0:T(1,128)S(1)}, f32[1,4]{1,0:T(1,128)S(1)}, f32[1,4]{1,0:T(1,128)S(1)}, f32[1,4]{1,0:T(1,1...) fusion(f32[1,1,4]{2,1,0:T(1,128)S(1)} %get-tuple-element.36, f32[]{:T(128)} %bitcast.714, ...), kind=kLoop, calls=%fused_computation.2773 | loop fusion | flops 312 | bytes 400 | tf_op jit(solution)/shard_map/div | solution.py:232
  428.1 3.1 collective-permute-start.24
  431.5 2.2 collective-permute-start.25
  433.8 3.1 collective-permute-start.26
  437.1 3.9 collective-permute-start.27
  441.1 3.7 collective-permute-start.28
  445.0 1.9 collective-permute-start.29
  448.1 3.8 collective-permute-done.29
  454.3 1.9 collective-permute-start.35
  456.3 2.7 collective-permute-start.33
  459.2 1.9 collective-permute-start.32
  461.3 3.9 collective-permute-start.31
  465.5 4.9 collective-permute-start.34
  470.3 3.7 collective-permute-start.30
  479.1 5.6 collective-permute-start.36
  484.9 1.9 collective-permute-start.37
  486.9 6.7 collective-permute-start.38
  493.8 2.4 collective-permute-start.39
  496.2 4.1 collective-permute-start.40
  500.6 1.9 collective-permute-start.41
  503.6 3.0 collective-permute-done.41
  509.0 1.9 collective-permute-start.47
  511.1 3.8 collective-permute-start.45
  515.0 1.9 collective-permute-start.44
  517.2 1.9 collective-permute-start.43
  519.3 4.9 collective-permute-start.46
  524.7 5.0 collective-permute-start.42
  535.6 103.7 %psum.31 = f32[2,4,4]{2,1,0:T(4,128)S(1)} all-reduce(f32[2,4,4]{2,1,0:T(4,128)S(1)} %pad_maximum_fusion.155), channel_id=1, replica_groups=mesh['ta'=16,'gz'=4,'gy'=8] {'ta','gz','gy'}, use_global_device_ids=true, to_apply=%region_5.7 | all-reduce | flops 32 | bytes 256 | tf_op jit(solution)/shard_map/psum | solution.py:273
  644.5 17.1 %subtract_divide_fusion.8 = (f32[1,4]{1,0:T(1,128)S(1)}, f32[1,4]{1,0:T(1,128)S(1)}, f32[1,4]{1,0:T(1,128)S(1)}, f32[1,4]{1,0:T(1,128)S(1)}, f32[1,4]{1,0:T(1,12...) fusion(f32[2,4,4]{2,1,0:T(4,128)S(1)} %psum.30, f32[]{:T(128)} %bitcast.1286, f32[]{:T(128)} %bitcast.1285, ...), kind=kLoop, calls=%fused_computation.2770 | loop fusion | flops 196 | bytes 336 | tf_op jit(solution)/shard_map/div | solution.py:226
  661.6 21.7 %subtract_divide_fusion = (f32[1,4]{1,0:T(1,128)S(1)}, f32[1,4]{1,0:T(1,128)S(1)}, f32[1,4]{1,0:T(1,128)S(1)}, f32[1,4]{1,0:T(1,128)S(1)}, f32[1,4]{1,0:T(1,128)...) fusion(f32[1,1,4]{2,1,0:T(1,128)S(1)} %get-tuple-element.21, f32[]{:T(128)} %bitcast.1258, ...), kind=kLoop, calls=%fused_computation.2762 | loop fusion | flops 312 | bytes 400 | tf_op jit(solution)/shard_map/div | solution.py:232
  (940 shorter events, 66.6 us)
Async XLA Ops:
  1.9 6.6 copy-start.1
  1.9 31.7 %collective-permute-start = (f32[4,2,2,3,2,2,32]{6,0,5,4,3,2,1:T(4,128)S(1)}, f32[4,2,2,3,2,2,32]{6,0,5,4,3,2,1:T(4,128)S(1)}, u32[]{:S(2)}, u32[]{:S(2)}) collective-permute-start(f32[4,2,2,3,2,2,32]{6,0,5,4,3,2,1:T(4,128)S(1)} %pad_maximum_fusion.47), channel_id=1, source_target_pairs={{1,0},{2,1},{3,2},{4,3},{5,4},{6,5},{7,6},{0,7},{9,8},{10,9},{11,1... | collective-permute-start | bytes 73736 | tf_op jit(solution)/shard_map/ppermute | solution.py:29
  8.9 26.9 %collective-permute-start.1 = (f32[4,2,2,3,2,2,32]{6,0,5,4,3,2,1:T(4,128)S(1)}, f32[4,2,2,3,2,2,32]{6,0,5,4,3,2,1:T(4,128)S(1)}, u32[]{:S(2)}, u32[]{:S(2)}) collective-permute-start(f32[4,2,2,3,2,2,32]{6,0,5,4,3,2,1:T(4,128)S(1)} %slice_maximum_fusion.14), channel_id=1, source_target_pairs={{0,1},{1,2},{2,3},{3,4},{4,5},{5,6},{6,7},{7,0},{8,9},{9,10},{10,1... | collective-permute-start | bytes 73736 | tf_op jit(solution)/shard_map/ppermute | solution.py:26
  10.9 25.3 %collective-permute-start.2 = (f32[4,2,2,3,2,1,128]{6,0,5,4,3,2,1:T(4,128)S(1)}, f32[4,2,2,3,2,1,128]{6,0,5,4,3,2,1:T(4,128)S(1)}, u32[]{:S(2)}, u32[]{:S(2)}) collective-permute-start(f32[4,2,2,3,2,1,128]{6,0,5,4,3,2,1:T(4,128)S(1)} %get-tuple-element.733), channel_id=1, source_target_pairs={{8,0},{16,8},{24,16},{0,24},{9,1},{17,9},{25,17},{1,25},{10,2},{18... | collective-permute-start | bytes 147464 | tf_op jit(solution)/shard_map/ppermute | solution.py:29
  17.4 18.7 %collective-permute-start.3 = (f32[4,2,2,3,2,1,128]{6,0,5,4,3,2,1:T(4,128)S(1)}, f32[4,2,2,3,2,1,128]{6,0,5,4,3,2,1:T(4,128)S(1)}, u32[]{:S(2)}, u32[]{:S(2)}) collective-permute-start(f32[4,2,2,3,2,1,128]{6,0,5,4,3,2,1:T(4,128)S(1)} %fusion.276), channel_id=1, source_target_pairs={{0,8},{8,16},{16,24},{24,0},{1,9},{9,17},{17,25},{25,1},{2,10},{10... | collective-permute-start | bytes 147464 | tf_op jit(solution)/shard_map/ppermute | solution.py:26
  19.4 17.0 %collective-permute-start.4 = (f32[4,2,2,3,1,2,128]{6,0,5,4,3,2,1:T(4,128)S(1)}, f32[4,2,2,3,1,2,128]{6,0,5,4,3,2,1:T(4,128)S(1)}, u32[]{:S(2)}, u32[]{:S(2)}) collective-permute-start(f32[4,2,2,3,1,2,128]{6,0,5,4,3,2,1:T(4,128)S(1)} %get-tuple-element.723), channel_id=1, source_target_pairs={{32,0},{64,32},{96,64},{128,96},{160,128},{192,160},{224,192},{256... | collective-permute-start | bytes 147464 | tf_op jit(solution)/shard_map/ppermute | solution.py:29
  33.6 6.6 collective-permute-start.5
  42.6 27.1 %collective-permute-start.11 = (f32[4,2,2,3,1,2,128]{6,0,5,4,3,2,1:T(4,128)S(1)}, f32[4,2,2,3,1,2,128]{6,0,5,4,3,2,1:T(4,128)S(1)}, u32[]{:S(2)}, u32[]{:S(2)}) collective-permute-start(f32[4,2,2,3,1,2,128]{6,0,5,4,3,2,1:T(4,128)S(1)} %fusion.262), channel_id=1, source_target_pairs={{0,32},{32,64},{64,96},{96,128},{128,160},{160,192},{192,224},{224... | collective-permute-start | bytes 147464 | tf_op jit(solution)/shard_map/ppermute | solution.py:26
  44.6 24.6 %collective-permute-start.10 = (f32[4,2,2,3,1,2,128]{6,0,5,4,3,2,1:T(4,128)S(1)}, f32[4,2,2,3,1,2,128]{6,0,5,4,3,2,1:T(4,128)S(1)}, u32[]{:S(2)}, u32[]{:S(2)}) collective-permute-start(f32[4,2,2,3,1,2,128]{6,0,5,4,3,2,1:T(4,128)S(1)} %get-tuple-element.711), channel_id=1, source_target_pairs={{32,0},{64,32},{96,64},{128,96},{160,128},{192,160},{224,192},{256... | collective-permute-start | bytes 147464 | tf_op jit(solution)/shard_map/ppermute | solution.py:29
  49.3 20.1 %collective-permute-start.9 = (f32[4,2,2,3,2,1,128]{6,0,5,4,3,2,1:T(4,128)S(1)}, f32[4,2,2,3,2,1,128]{6,0,5,4,3,2,1:T(4,128)S(1)}, u32[]{:S(2)}, u32[]{:S(2)}) collective-permute-start(f32[4,2,2,3,2,1,128]{6,0,5,4,3,2,1:T(4,128)S(1)} %fusion.266), channel_id=1, source_target_pairs={{0,8},{8,16},{16,24},{24,0},{1,9},{9,17},{17,25},{25,1},{2,10},{10... | collective-permute-start | bytes 147464 | tf_op jit(solution)/shard_map/ppermute | solution.py:26
  53.3 16.2 %collective-permute-start.8 = (f32[4,2,2,3,2,1,128]{6,0,5,4,3,2,1:T(4,128)S(1)}, f32[4,2,2,3,2,1,128]{6,0,5,4,3,2,1:T(4,128)S(1)}, u32[]{:S(2)}, u32[]{:S(2)}) collective-permute-start(f32[4,2,2,3,2,1,128]{6,0,5,4,3,2,1:T(4,128)S(1)} %get-tuple-element.701), channel_id=1, source_target_pairs={{8,0},{16,8},{24,16},{0,24},{9,1},{17,9},{25,17},{1,25},{10,2},{18... | collective-permute-start | bytes 147464 | tf_op jit(solution)/shard_map/ppermute | solution.py:29
  55.4 8.0 %collective-permute-start.7 = (f32[4,2,2,3,2,2,32]{6,0,5,4,3,2,1:T(4,128)S(1)}, f32[4,2,2,3,2,2,32]{6,0,5,4,3,2,1:T(4,128)S(1)}, u32[]{:S(2)}, u32[]{:S(2)}) collective-permute-start(f32[4,2,2,3,2,2,32]{6,0,5,4,3,2,1:T(4,128)S(1)} %slice_maximum_fusion.12), channel_id=1, source_target_pairs={{0,1},{1,2},{2,3},{3,4},{4,5},{5,6},{6,7},{7,0},{8,9},{9,10},{10,1... | collective-permute-start | bytes 73736 | tf_op jit(solution)/shard_map/ppermute | solution.py:26
  63.4 5.3 collective-permute-start.6
  69.9 0.9 copy-start
  70.0 0.9 copy-start.2
  73.0 19.6 %collective-permute-start.12 = (f32[4,2,2,3,2,2,32]{6,0,5,4,3,2,1:T(4,128)S(1)}, f32[4,2,2,3,2,2,32]{6,0,5,4,3,2,1:T(4,128)S(1)}, u32[]{:S(2)}, u32[]{:S(2)}) collective-permute-start(f32[4,2,2,3,2,2,32]{6,0,5,4,3,2,1:T(4,128)S(1)} %pad_maximum_fusion.39), channel_id=1, source_target_pairs={{1,0},{2,1},{3,2},{4,3},{5,4},{6,5},{7,6},{0,7},{9,8},{10,9},{11,1... | collective-permute-start | bytes 73736 | tf_op jit(solution)/shard_map/ppermute | solution.py:29
  77.9 18.8 %collective-permute-start.13 = (f32[4,2,2,3,2,2,32]{6,0,5,4,3,2,1:T(4,128)S(1)}, f32[4,2,2,3,2,2,32]{6,0,5,4,3,2,1:T(4,128)S(1)}, u32[]{:S(2)}, u32[]{:S(2)}) collective-permute-start(f32[4,2,2,3,2,2,32]{6,0,5,4,3,2,1:T(4,128)S(1)} %slice_maximum_fusion.10), channel_id=1, source_target_pairs={{0,1},{1,2},{2,3},{3,4},{4,5},{5,6},{6,7},{7,0},{8,9},{9,10},{10,1... | collective-permute-start | bytes 73736 | tf_op jit(solution)/shard_map/ppermute | solution.py:26
  79.9 17.2 %collective-permute-start.14 = (f32[4,2,2,3,2,1,128]{6,0,5,4,3,2,1:T(4,128)S(1)}, f32[4,2,2,3,2,1,128]{6,0,5,4,3,2,1:T(4,128)S(1)}, u32[]{:S(2)}, u32[]{:S(2)}) collective-permute-start(f32[4,2,2,3,2,1,128]{6,0,5,4,3,2,1:T(4,128)S(1)} %get-tuple-element.669), channel_id=1, source_target_pairs={{8,0},{16,8},{24,16},{0,24},{9,1},{17,9},{25,17},{1,25},{10,2},{18... | collective-permute-start | bytes 147464 | tf_op jit(solution)/shard_map/ppermute | solution.py:29
  86.8 10.2 %collective-permute-start.15 = (f32[4,2,2,3,2,1,128]{6,0,5,4,3,2,1:T(4,128)S(1)}, f32[4,2,2,3,2,1,128]{6,0,5,4,3,2,1:T(4,128)S(1)}, u32[]{:S(2)}, u32[]{:S(2)}) collective-permute-start(f32[4,2,2,3,2,1,128]{6,0,5,4,3,2,1:T(4,128)S(1)} %fusion.256), channel_id=1, source_target_pairs={{0,8},{8,16},{16,24},{24,0},{1,9},{9,17},{17,25},{25,1},{2,10},{10... | collective-permute-start | bytes 147464 | tf_op jit(solution)/shard_map/ppermute | solution.py:26
  90.4 6.9 collective-permute-start.16
  92.6 6.5 collective-permute-start.17
  101.4 23.2 %collective-permute-start.23 = (f32[4,2,2,3,1,2,128]{6,0,5,4,3,2,1:T(4,128)S(1)}, f32[4,2,2,3,1,2,128]{6,0,5,4,3,2,1:T(4,128)S(1)}, u32[]{:S(2)}, u32[]{:S(2)}) collective-permute-start(f32[4,2,2,3,1,2,128]{6,0,5,4,3,2,1:T(4,128)S(1)} %fusion.242), channel_id=1, source_target_pairs={{0,32},{32,64},{64,96},{96,128},{128,160},{160,192},{192,224},{224... | collective-permute-start | bytes 147464 | tf_op jit(solution)/shard_map/ppermute | solution.py:26
  103.9 20.4 %collective-permute-start.21 = (f32[4,2,2,3,2,1,128]{6,0,5,4,3,2,1:T(4,128)S(1)}, f32[4,2,2,3,2,1,128]{6,0,5,4,3,2,1:T(4,128)S(1)}, u32[]{:S(2)}, u32[]{:S(2)}) collective-permute-start(f32[4,2,2,3,2,1,128]{6,0,5,4,3,2,1:T(4,128)S(1)} %fusion.246), channel_id=1, source_target_pairs={{0,8},{8,16},{16,24},{24,0},{1,9},{9,17},{17,25},{25,1},{2,10},{10... | collective-permute-start | bytes 147464 | tf_op jit(solution)/shard_map/ppermute | solution.py:26
  108.4 16.0 %collective-permute-start.20 = (f32[4,2,2,3,2,1,128]{6,0,5,4,3,2,1:T(4,128)S(1)}, f32[4,2,2,3,2,1,128]{6,0,5,4,3,2,1:T(4,128)S(1)}, u32[]{:S(2)}, u32[]{:S(2)}) collective-permute-start(f32[4,2,2,3,2,1,128]{6,0,5,4,3,2,1:T(4,128)S(1)} %get-tuple-element.637), channel_id=1, source_target_pairs={{8,0},{16,8},{24,16},{0,24},{9,1},{17,9},{25,17},{1,25},{10,2},{18... | collective-permute-start | bytes 147464 | tf_op jit(solution)/shard_map/ppermute | solution.py:29
  110.6 7.7 %collective-permute-start.19 = (f32[4,2,2,3,2,2,32]{6,0,5,4,3,2,1:T(4,128)S(1)}, f32[4,2,2,3,2,2,32]{6,0,5,4,3,2,1:T(4,128)S(1)}, u32[]{:S(2)}, u32[]{:S(2)}) collective-permute-start(f32[4,2,2,3,2,2,32]{6,0,5,4,3,2,1:T(4,128)S(1)} %slice_maximum_fusion.8), channel_id=1, source_target_pairs={{0,1},{1,2},{2,3},{3,4},{4,5},{5,6},{6,7},{7,0},{8,9},{9,10},{10,1... | collective-permute-start | bytes 73736 | tf_op jit(solution)/shard_map/ppermute | solution.py:26
  112.7 11.4 %collective-permute-start.22 = (f32[4,2,2,3,1,2,128]{6,0,5,4,3,2,1:T(4,128)S(1)}, f32[4,2,2,3,1,2,128]{6,0,5,4,3,2,1:T(4,128)S(1)}, u32[]{:S(2)}, u32[]{:S(2)}) collective-permute-start(f32[4,2,2,3,1,2,128]{6,0,5,4,3,2,1:T(4,128)S(1)} %get-tuple-element.647), channel_id=1, source_target_pairs={{32,0},{64,32},{96,64},{128,96},{160,128},{192,160},{224,192},{256... | collective-permute-start | bytes 147464 | tf_op jit(solution)/shard_map/ppermute | solution.py:29
  118.3 5.4 collective-permute-start.18
  428.1 16.9 %collective-permute-start.24 = (f32[4,2,2,3,2,2,32]{6,0,5,4,3,2,1:T(4,128)S(1)}, f32[4,2,2,3,2,2,32]{6,0,5,4,3,2,1:T(4,128)S(1)}, u32[]{:S(2)}, u32[]{:S(2)}) collective-permute-start(f32[4,2,2,3,2,2,32]{6,0,5,4,3,2,1:T(4,128)S(1)} %pad_maximum_fusion.31), channel_id=1, source_target_pairs={{1,0},{2,1},{3,2},{4,3},{5,4},{6,5},{7,6},{0,7},{9,8},{10,9},{11,1... | collective-permute-start | bytes 73736 | tf_op jit(solution)/shard_map/ppermute | solution.py:29
  431.5 15.8 %collective-permute-start.25 = (f32[4,2,2,3,2,2,32]{6,0,5,4,3,2,1:T(4,128)S(1)}, f32[4,2,2,3,2,2,32]{6,0,5,4,3,2,1:T(4,128)S(1)}, u32[]{:S(2)}, u32[]{:S(2)}) collective-permute-start(f32[4,2,2,3,2,2,32]{6,0,5,4,3,2,1:T(4,128)S(1)} %slice_maximum_fusion.6), channel_id=1, source_target_pairs={{0,1},{1,2},{2,3},{3,4},{4,5},{5,6},{6,7},{7,0},{8,9},{9,10},{10,1... | collective-permute-start | bytes 73736 | tf_op jit(solution)/shard_map/ppermute | solution.py:26
  433.8 13.9 %collective-permute-start.26 = (f32[4,2,2,3,2,1,128]{6,0,5,4,3,2,1:T(4,128)S(1)}, f32[4,2,2,3,2,1,128]{6,0,5,4,3,2,1:T(4,128)S(1)}, u32[]{:S(2)}, u32[]{:S(2)}) collective-permute-start(f32[4,2,2,3,2,1,128]{6,0,5,4,3,2,1:T(4,128)S(1)} %get-tuple-element.605), channel_id=1, source_target_pairs={{8,0},{16,8},{24,16},{0,24},{9,1},{17,9},{25,17},{1,25},{10,2},{18... | collective-permute-start | bytes 147464 | tf_op jit(solution)/shard_map/ppermute | solution.py:29
  437.1 10.5 %collective-permute-start.27 = (f32[4,2,2,3,2,1,128]{6,0,5,4,3,2,1:T(4,128)S(1)}, f32[4,2,2,3,2,1,128]{6,0,5,4,3,2,1:T(4,128)S(1)}, u32[]{:S(2)}, u32[]{:S(2)}) collective-permute-start(f32[4,2,2,3,2,1,128]{6,0,5,4,3,2,1:T(4,128)S(1)} %fusion.236), channel_id=1, source_target_pairs={{0,8},{8,16},{16,24},{24,0},{1,9},{9,17},{17,25},{25,1},{2,10},{10... | collective-permute-start | bytes 147464 | tf_op jit(solution)/shard_map/ppermute | solution.py:26
  441.1 6.7 collective-permute-start.28
  445.0 6.9 collective-permute-start.29
  454.3 22.4 %collective-permute-start.35 = (f32[4,2,2,3,1,2,128]{6,0,5,4,3,2,1:T(4,128)S(1)}, f32[4,2,2,3,1,2,128]{6,0,5,4,3,2,1:T(4,128)S(1)}, u32[]{:S(2)}, u32[]{:S(2)}) collective-permute-start(f32[4,2,2,3,1,2,128]{6,0,5,4,3,2,1:T(4,128)S(1)} %fusion.222), channel_id=1, source_target_pairs={{0,32},{32,64},{64,96},{96,128},{128,160},{160,192},{192,224},{224... | collective-permute-start | bytes 147464 | tf_op jit(solution)/shard_map/ppermute | solution.py:26
  456.3 20.0 %collective-permute-start.33 = (f32[4,2,2,3,2,1,128]{6,0,5,4,3,2,1:T(4,128)S(1)}, f32[4,2,2,3,2,1,128]{6,0,5,4,3,2,1:T(4,128)S(1)}, u32[]{:S(2)}, u32[]{:S(2)}) collective-permute-start(f32[4,2,2,3,2,1,128]{6,0,5,4,3,2,1:T(4,128)S(1)} %fusion.226), channel_id=1, source_target_pairs={{0,8},{8,16},{16,24},{24,0},{1,9},{9,17},{17,25},{25,1},{2,10},{10... | collective-permute-start | bytes 147464 | tf_op jit(solution)/shard_map/ppermute | solution.py:26
  459.2 17.3 %collective-permute-start.32 = (f32[4,2,2,3,2,1,128]{6,0,5,4,3,2,1:T(4,128)S(1)}, f32[4,2,2,3,2,1,128]{6,0,5,4,3,2,1:T(4,128)S(1)}, u32[]{:S(2)}, u32[]{:S(2)}) collective-permute-start(f32[4,2,2,3,2,1,128]{6,0,5,4,3,2,1:T(4,128)S(1)} %get-tuple-element.573), channel_id=1, source_target_pairs={{8,0},{16,8},{24,16},{0,24},{9,1},{17,9},{25,17},{1,25},{10,2},{18... | collective-permute-start | bytes 147464 | tf_op jit(solution)/shard_map/ppermute | solution.py:29
  461.3 9.0 %collective-permute-start.31 = (f32[4,2,2,3,2,2,32]{6,0,5,4,3,2,1:T(4,128)S(1)}, f32[4,2,2,3,2,2,32]{6,0,5,4,3,2,1:T(4,128)S(1)}, u32[]{:S(2)}, u32[]{:S(2)}) collective-permute-start(f32[4,2,2,3,2,2,32]{6,0,5,4,3,2,1:T(4,128)S(1)} %slice_maximum_fusion.4), channel_id=1, source_target_pairs={{0,1},{1,2},{2,3},{3,4},{4,5},{5,6},{6,7},{7,0},{8,9},{9,10},{10,1... | collective-permute-start | bytes 73736 | tf_op jit(solution)/shard_map/ppermute | solution.py:26
  465.5 10.6 %collective-permute-start.34 = (f32[4,2,2,3,1,2,128]{6,0,5,4,3,2,1:T(4,128)S(1)}, f32[4,2,2,3,1,2,128]{6,0,5,4,3,2,1:T(4,128)S(1)}, u32[]{:S(2)}, u32[]{:S(2)}) collective-permute-start(f32[4,2,2,3,1,2,128]{6,0,5,4,3,2,1:T(4,128)S(1)} %get-tuple-element.583), channel_id=1, source_target_pairs={{32,0},{64,32},{96,64},{128,96},{160,128},{192,160},{224,192},{256... | collective-permute-start | bytes 147464 | tf_op jit(solution)/shard_map/ppermute | solution.py:29
  470.3 5.4 collective-permute-start.30
  479.1 21.5 %collective-permute-start.36 = (f32[4,2,2,3,2,2,32]{6,0,5,4,3,2,1:T(4,128)S(1)}, f32[4,2,2,3,2,2,32]{6,0,5,4,3,2,1:T(4,128)S(1)}, u32[]{:S(2)}, u32[]{:S(2)}) collective-permute-start(f32[4,2,2,3,2,2,32]{6,0,5,4,3,2,1:T(4,128)S(1)} %pad_maximum_fusion.23), channel_id=1, source_target_pairs={{1,0},{2,1},{3,2},{4,3},{5,4},{6,5},{7,6},{0,7},{9,8},{10,9},{11,1... | collective-permute-start | bytes 73736 | tf_op jit(solution)/shard_map/ppermute | solution.py:29
  484.9 17.9 %collective-permute-start.37 = (f32[4,2,2,3,2,2,32]{6,0,5,4,3,2,1:T(4,128)S(1)}, f32[4,2,2,3,2,2,32]{6,0,5,4,3,2,1:T(4,128)S(1)}, u32[]{:S(2)}, u32[]{:S(2)}) collective-permute-start(f32[4,2,2,3,2,2,32]{6,0,5,4,3,2,1:T(4,128)S(1)} %slice_maximum_fusion.2), channel_id=1, source_target_pairs={{0,1},{1,2},{2,3},{3,4},{4,5},{5,6},{6,7},{7,0},{8,9},{9,10},{10,1... | collective-permute-start | bytes 73736 | tf_op jit(solution)/shard_map/ppermute | solution.py:26
  486.9 16.3 %collective-permute-start.38 = (f32[4,2,2,3,2,1,128]{6,0,5,4,3,2,1:T(4,128)S(1)}, f32[4,2,2,3,2,1,128]{6,0,5,4,3,2,1:T(4,128)S(1)}, u32[]{:S(2)}, u32[]{:S(2)}) collective-permute-start(f32[4,2,2,3,2,1,128]{6,0,5,4,3,2,1:T(4,128)S(1)} %get-tuple-element.541), channel_id=1, source_target_pairs={{8,0},{16,8},{24,16},{0,24},{9,1},{17,9},{25,17},{1,25},{10,2},{18... | collective-permute-start | bytes 147464 | tf_op jit(solution)/shard_map/ppermute | solution.py:29
  493.8 9.3 %collective-permute-start.39 = (f32[4,2,2,3,2,1,128]{6,0,5,4,3,2,1:T(4,128)S(1)}, f32[4,2,2,3,2,1,128]{6,0,5,4,3,2,1:T(4,128)S(1)}, u32[]{:S(2)}, u32[]{:S(2)}) collective-permute-start(f32[4,2,2,3,2,1,128]{6,0,5,4,3,2,1:T(4,128)S(1)} %fusion.216), channel_id=1, source_target_pairs={{0,8},{8,16},{16,24},{24,0},{1,9},{9,17},{17,25},{25,1},{2,10},{10... | collective-permute-start | bytes 147464 | tf_op jit(solution)/shard_map/ppermute | solution.py:26
  496.2 7.1 %collective-permute-start.40 = (f32[4,2,2,3,1,2,128]{6,0,5,4,3,2,1:T(4,128)S(1)}, f32[4,2,2,3,1,2,128]{6,0,5,4,3,2,1:T(4,128)S(1)}, u32[]{:S(2)}, u32[]{:S(2)}) collective-permute-start(f32[4,2,2,3,1,2,128]{6,0,5,4,3,2,1:T(4,128)S(1)} %get-tuple-element.531), channel_id=1, source_target_pairs={{32,0},{64,32},{96,64},{128,96},{160,128},{192,160},{224,192},{256... | collective-permute-start | bytes 147464 | tf_op jit(solution)/shard_map/ppermute | solution.py:29
  500.6 6.0 collective-permute-start.41
  509.0 23.2 %collective-permute-start.47 = (f32[4,2,2,3,1,2,128]{6,0,5,4,3,2,1:T(4,128)S(1)}, f32[4,2,2,3,1,2,128]{6,0,5,4,3,2,1:T(4,128)S(1)}, u32[]{:S(2)}, u32[]{:S(2)}) collective-permute-start(f32[4,2,2,3,1,2,128]{6,0,5,4,3,2,1:T(4,128)S(1)} %fusion.202), channel_id=1, source_target_pairs={{0,32},{32,64},{64,96},{96,128},{128,160},{160,192},{192,224},{224... | collective-permute-start | bytes 147464 | tf_op jit(solution)/shard_map/ppermute | solution.py:26
  511.1 20.9 %collective-permute-start.45 = (f32[4,2,2,3,2,1,128]{6,0,5,4,3,2,1:T(4,128)S(1)}, f32[4,2,2,3,2,1,128]{6,0,5,4,3,2,1:T(4,128)S(1)}, u32[]{:S(2)}, u32[]{:S(2)}) collective-permute-start(f32[4,2,2,3,2,1,128]{6,0,5,4,3,2,1:T(4,128)S(1)} %fusion.206), channel_id=1, source_target_pairs={{0,8},{8,16},{16,24},{24,0},{1,9},{9,17},{17,25},{25,1},{2,10},{10... | collective-permute-start | bytes 147464 | tf_op jit(solution)/shard_map/ppermute | solution.py:26
  515.0 17.0 %collective-permute-start.44 = (f32[4,2,2,3,2,1,128]{6,0,5,4,3,2,1:T(4,128)S(1)}, f32[4,2,2,3,2,1,128]{6,0,5,4,3,2,1:T(4,128)S(1)}, u32[]{:S(2)}, u32[]{:S(2)}) collective-permute-start(f32[4,2,2,3,2,1,128]{6,0,5,4,3,2,1:T(4,128)S(1)} %get-tuple-element.509), channel_id=1, source_target_pairs={{8,0},{16,8},{24,16},{0,24},{9,1},{17,9},{25,17},{1,25},{10,2},{18... | collective-permute-start | bytes 147464 | tf_op jit(solution)/shard_map/ppermute | solution.py:29
  517.2 7.5 %collective-permute-start.43 = (f32[4,2,2,3,2,2,32]{6,0,5,4,3,2,1:T(4,128)S(1)}, f32[4,2,2,3,2,2,32]{6,0,5,4,3,2,1:T(4,128)S(1)}, u32[]{:S(2)}, u32[]{:S(2)}) collective-permute-start(f32[4,2,2,3,2,2,32]{6,0,5,4,3,2,1:T(4,128)S(1)} %slice_maximum_fusion), channel_id=1, source_target_pairs={{0,1},{1,2},{2,3},{3,4},{4,5},{5,6},{6,7},{7,0},{8,9},{9,10},{10,1... | collective-permute-start | bytes 73736 | tf_op jit(solution)/shard_map/ppermute | solution.py:26
  519.3 12.4 %collective-permute-start.46 = (f32[4,2,2,3,1,2,128]{6,0,5,4,3,2,1:T(4,128)S(1)}, f32[4,2,2,3,1,2,128]{6,0,5,4,3,2,1:T(4,128)S(1)}, u32[]{:S(2)}, u32[]{:S(2)}) collective-permute-start(f32[4,2,2,3,1,2,128]{6,0,5,4,3,2,1:T(4,128)S(1)} %get-tuple-element.519), channel_id=1, source_target_pairs={{32,0},{64,32},{96,64},{128,96},{160,128},{192,160},{224,192},{256... | collective-permute-start | bytes 147464 | tf_op jit(solution)/shard_map/ppermute | solution.py:29
  524.7 6.6 collective-permute-start.42
where the time goes:
time: 700 us; the launch traced here: 689 us
  blocking collectives  307 us (44%)
  starting transfers between devices  165 us (24%)
  other arithmetic  152 us (22%)
  waiting for transfers between devices  27.2 us (4%)
  matrix products  16.3 us (2%)
  between operations  11.7 us (2%)
  local copies, waits for them, and re-layouts  9.51 us (1%)
    psum x2, blocking collectives, residual_total(): return lax.psum(gram(residual, residual), ('ta', 'gz', 'gy'))  203 us
    psum x1, blocking collectives, local(): curvature = lax.psum(gram(search, images), ('ta', 'gz', 'gy'))  104 us
    ppermute x24, starting transfers between devices, with_halo(): lax.ppermute(lax.slice_in_dim(block, 0, width, axis=dim), axis, backward)  103 us
    div x3, other arithmetic, cholesky_solve(): back_rows[row_index] = running / factor[row_index, row_index]  65.1 us
    ppermute x24, starting transfers between devices, with_halo(): lax.ppermute(lax.slice_in_dim(block, block.shape[dim] - width, None, axis...  61.8 us
    div x3, other arithmetic, cholesky_solve(): forward_rows.append(running / factor[row_index, row_index])  51.4 us
    ppermute x24, waiting for transfers between devices, with_halo(): lax.ppermute(lax.slice_in_dim(block, block.shape[dim] - width, None, axis...  20.1 us
  transfers between devices with their start and end apart: 48, of which 11 were waited for; matrix products, arithmetic and copies ran while one was open for 2% of the time, Pallas kernels for 0%

commit v1 on v0

v1 whole, which is shorter than its diff:
```python
import jax
import jax.numpy as jnp
from jax import lax
from jax.experimental import pallas as pl
from jax.experimental.pallas import tpu as pltpu
from jax.sharding import PartitionSpec as P

SRC = 4
KAPPA_SQUARE = 0.0196
GAMMA_COLUMNS = ((3, 2, 1, 0), (3, 2, 1, 0), (2, 3, 0, 1), (2, 3, 0, 1))
GAMMA_PHASES = (
    ((0, 1), (0, 1), (0, -1), (0, -1)),
    ((1, 0), (-1, 0), (-1, 0), (1, 0)),
    ((0, 1), (0, -1), (0, -1), (0, 1)),
    ((1, 0), (1, 0), (1, 0), (1, 0)),
)
F32 = jnp.float32
TILE = (8, 128)
ROW_OWNER = ((0, 1, 3, 2), (2, 3, 1, 0))
GUARD = 0.005
PIVOT_GUARD = 1e-3
VMEM = pl.BlockSpec(memory_space=pltpu.VMEM)
SMEM = pl.BlockSpec(memory_space=pltpu.SMEM)


def call(body, outs, args, flops=10**6):
    in_specs = [SMEM if a.dtype == jnp.int32 else VMEM for a in args]
    shapes = [jax.ShapeDtypeStruct(s, F32) for s in outs]
    moved = 4 * sum(a.size for a in args)
    return pl.pallas_call(
        body,
        out_shape=shapes,
        in_specs=in_specs,
        out_specs=[VMEM] * len(shapes),
        compiler_params=pltpu.CompilerParams(vmem_limit_bytes=32 * 2**20),
        cost_estimate=pl.CostEstimate(flops=flops, bytes_accessed=moved, transcendentals=0),
    )(*args)


def lanes():
    return lax.broadcasted_iota(jnp.int32, TILE, 1)


def sublanes():
    return lax.broadcasted_iota(jnp.int32, TILE, 0)


def roll_lanes(x, shift):
    return pltpu.roll(x, shift % 128, 1)


def swap_groups(tiles):
    low = lanes() < 64
    even = (lanes() // 32) % 2 == 0
    a = [None] * 4
    for i in (0, 1):
        a[i] = jnp.where(low, tiles[i], roll_lanes(tiles[i + 2], 64))
        a[i + 2] = jnp.where(low, roll_lanes(tiles[i], 64), tiles[i + 2])
    out = []
    for i in (0, 2):
        out.append(jnp.where(even, a[i], roll_lanes(a[i + 1], 32)))
        out.append(jnp.where(even, roll_lanes(a[i], -32), a[i + 1]))
    return out


def owner(info, row):
    return jnp.where(info[4] == 1, ROW_OWNER[1][row], ROW_OWNER[0][row])


def pack_body(info, sources, links, out):
    for ref, base, chunks in ((sources, 0, 6), (links, 48, 9)):
        for z in range(2):
            for i in range(chunks):
                tiles = [ref[s, pl.ds(16 * i + z, 8, stride=2), :] for s in range(4)]
                for row, tile in enumerate(swap_groups(tiles)):
                    out[owner(info, row), z, base + 8 * i : base + 8 * i + 8, :] = tile


def unpack_body(info, received, links, spinor, *faces):
    for c in range(24):
        for t in range(2):
            spinor[c, t] = received[pl.ds(2 * c + t, 8, stride=120), :]
    low = lanes() < 64
    even = (lanes() // 32) % 2 == 0
    for l in range(36):
        for t in range(2):
            x = received[pl.ds(48 + 2 * l + t, 8, stride=120), :]
            half = roll_lanes(x, 64)
            for q, pair in ((0, jnp.where(low, x, half)), (2, jnp.where(low, half, x))):
                turned = roll_lanes(pair, 32)
                links[q * 36 + l, t] = jnp.where(even, pair, turned)
                links[(q + 1) * 36 + l, t] = jnp.where(even, turned, pair)
    write_faces(info, spinor, links, 1, faces)


def load_spinor(ref, t):
    return [[[ref[(p * 4 + s) * 3 + c, t] for c in range(3)] for s in range(4)] for p in range(2)]


def signed_add(a, b, sign):
    return a + b if sign > 0 else a - b


def turn(phase, part):
    if phase[1] == 0:
        return part, phase[0]
    return 1 - part, -phase[1] if part == 0 else phase[1]


def project(v, direction, hop):
    out = [[None, None], [None, None]]
    for part in range(2):
        for k in range(2):
            partner = GAMMA_COLUMNS[direction][k]
            other, sign = turn(GAMMA_PHASES[direction][k], part)
            out[part][k] = [
                signed_add(v[part][k][c], v[other][partner][c], sign * hop) for c in range(3)
            ]
    return out


def rebuild_add(acc, half, direction, hop):
    for part in range(2):
        for s in range(4):
            if s < 2:
                source, sign = half[part][s], 1
            else:
                other, sign = turn(GAMMA_PHASES[direction][s], part)
                source, sign = half[other][GAMMA_COLUMNS[direction][s]], sign * hop
            for c in range(3):
                old = acc[part][s][c]
                if old is None:
                    acc[part][s][c] = source[c] if sign > 0 else -source[c]
                else:
                    acc[part][s][c] = signed_add(old, source[c], sign)


def color_times(links, parity, direction, t, half, adjoint):
    base = (parity * 4 + direction) * 18
    out = [[[None] * 3 for _ in range(2)] for _ in range(2)]
    for row in range(3):
        for column in range(3):
            entry = 3 * column + row if adjoint else 3 * row + column
            re, im = links[base + entry, t], links[base + 9 + entry, t]
            for k in range(2):
                x, y = half[0][k][column], half[1][k][column]
                if adjoint:
                    a, b = re * x + im * y, re * y - im * x
                else:
                    a, b = re * x - im * y, re * y + im * x
                if out[0][k][row] is None:
                    out[0][k][row], out[1][k][row] = a, b
                else:
                    out[0][k][row] += a
                    out[1][k][row] += b
    return out


def map_half(f, half):
    return [[[f(x) for x in row] for row in part] for part in half]


def halves(half):
    return [half[p][k][c] for p in range(2) for k in range(2) for c in range(3)]


def write_faces(info, spinor, links, parity, faces):
    time_a, time_b, row_a, row_b = faces
    time_odd, row_odd = info[0] == 1, info[1] == 1
    for t in range(2):
        v = load_spinor(spinor, t)
        down = halves(project(v, 1, -1))
        up = halves(color_times(links, 1 - parity, 1, t, project(v, 1, 1), True))
        for i in range(12):
            row_a[i, t] = jnp.where(row_odd, down[i], up[i])
            row_b[i, t] = jnp.where(row_odd, up[i], down[i])
        if t == 0:
            time_down = halves(project(v, 3, -1))
        else:
            time_up = halves(color_times(links, 1 - parity, 3, t, project(v, 3, 1), True))
    for i in range(12):
        time_a[i] = jnp.where(time_odd, time_down[i], time_up[i])
        time_b[i] = jnp.where(time_odd, time_up[i], time_down[i])


def inner_body(parity, with_moments, info, spinor, links, out, *moments):
    cell = lanes() % 32
    site = sublanes() + info[1] + parity
    vs = [load_spinor(spinor, t) for t in range(2)]
    for t in range(2):
        odd = (site + t) % 2 == 1
        v = vs[t]
        acc = [[[None] * 3 for _ in range(4)] for _ in range(2)]

        def next_cell(x):
            moved = jnp.where(cell == 31, roll_lanes(x, 31), roll_lanes(x, -1))
            return jnp.where(odd, moved, x)

        def prior_cell(x):
            moved = jnp.where(cell == 0, roll_lanes(x, -31), roll_lanes(x, 1))
            return jnp.where(odd, x, moved)

        half = map_half(next_cell, project(v, 0, -1))
        rebuild_add(acc, color_times(links, parity, 0, t, half, False), 0, -1)
        half = color_times(links, 1 - parity, 0, t, project(v, 0, 1), True)
        rebuild_add(acc, map_half(prior_cell, half), 0, 1)
        half = map_half(lambda x: pltpu.roll(x, 7, 0), project(v, 2, -1))
        rebuild_add(acc, color_times(links, parity, 2, t, half, False), 2, -1)
        half = color_times(links, 1 - parity, 2, t, project(v, 2, 1), True)
        rebuild_add(acc, map_half(lambda x: pltpu.roll(x, 1, 0), half), 2, 1)
        if t == 0:
            half = project(vs[1], 3, -1)
            rebuild_add(acc, color_times(links, parity, 3, 0, half, False), 3, -1)
        else:
            half = color_times(links, 1 - parity, 3, 0, project(vs[0], 3, 1), True)
            rebuild_add(acc, half, 3, 1)
        for p in range(2):
            for s in range(4):
                for c in range(3):
                    out[(p * 4 + s) * 3 + c, t] = acc[p][s][c]
    if with_moments:
        for i, total in enumerate(moment_tiles(spinor)):
            moments[0][i] = total


def moment_tiles(spinor):
    totals = [jnp.zeros(TILE, F32) for _ in range(5)]
    for t in range(2):
        for c in range(12):
            re, im = spinor[c, t], spinor[12 + c, t]
            totals[0] = totals[0] + (re * re + im * im)
            for d in (1, 2):
                re_d, im_d = roll_lanes(re, -32 * d), roll_lanes(im, -32 * d)
                totals[2 * d - 1] = totals[2 * d - 1] + (re * re_d + im * im_d)
                totals[2 * d] = totals[2 * d] + (re * im_d - im * re_d)
    return totals


def add_received(info, acc, links, parity, t, recv):
    time_a, time_b, row_a, row_b = recv
    time_odd, row_odd = info[0] == 1, info[1] == 1

    def pick(flag, first, second):
        flat = [jnp.where(flag, first[i], second[i]) for i in range(12)]
        return [[flat[6 * p + 3 * k : 6 * p + 3 * k + 3] for k in range(2)] for p in range(2)]

    half = pick(row_odd, [row_b[i, t] for i in range(12)], [row_a[i, t] for i in range(12)])
    rebuild_add(acc, color_times(links, parity, 1, t, half, False), 1, -1)
    half = pick(row_odd, [row_a[i, t] for i in range(12)], [row_b[i, t] for i in range(12)])
    rebuild_add(acc, half, 1, 1)
    a, b = [time_a[i] for i in range(12)], [time_b[i] for i in range(12)]
    if t == 1:
        sign = jnp.where(info[2] == 1, -1.0, 1.0)
        half = map_half(lambda x: x * sign, pick(time_odd, b, a))
        rebuild_add(acc, color_times(links, parity, 3, t, half, False), 3, -1)
    else:
        sign = jnp.where(info[3] == 1, -1.0, 1.0)
        half = map_half(lambda x: x * sign, pick(time_odd, a, b))
        rebuild_add(acc, half, 3, 1)


def finished_spinor(info, partial, links, parity, t, recv, base):
    acc = load_spinor(partial, t)
    add_received(info, acc, links, parity, t, recv)
    if base is None:
        return acc
    old = load_spinor(base, t)
    for p in range(2):
        for s in range(4):
            for c in range(3):
                hopped = KAPPA_SQUARE * acc[p][s][c]
                acc[p][s][c] = old[p][s][c] - hopped if s < 2 else hopped - old[p][s][c]
    return acc


def outer_body(parity, with_base, with_faces, *refs):
    info, partial, links = refs[:3]
    recv = refs[3:7]
    base = refs[7] if with_base else None
    out = refs[8] if with_base else refs[7]
    faces = refs[-4:]
    for t in range(2):
        acc = finished_spinor(info, partial, links, parity, t, recv, base)
        for p in range(2):
            for s in range(4):
                for c in range(3):
                    out[(p * 4 + s) * 3 + c, t] = acc[p][s][c]
    if with_faces:
        write_faces(info, out, links, 1 - parity, faces)


def group_sum(x):
    cell = lax.broadcasted_iota(jnp.int32, x.shape, 1) % 32
    for step in (16, 8, 4, 2, 1):
        x = x + jnp.where(cell < 32 - step, roll_lanes(x, -step), roll_lanes(x, 32 - step))
    return x


def pick_cells(scratch, out):
    rows = group_sum(scratch[...])
    cell = lax.broadcasted_iota(jnp.int32, rows.shape, 1) % 32
    line = lax.broadcasted_iota(jnp.int32, rows.shape, 0)
    packed = jnp.sum(jnp.where(cell == line, rows, 0.0), axis=0, keepdims=True)
    out[...] = jnp.broadcast_to(packed, out.shape)


def moments_body(spinor, *refs):
    given, out, scratch = refs[:-2], refs[-2], refs[-1]
    scratch[...] = jnp.zeros(scratch.shape, F32)
    at = 0
    for total in [[m[i] for i in range(5)] for m in given] + [moment_tiles(spinor)]:
        for tile in total:
            scratch[at : at + 1, :] = jnp.sum(tile, axis=0, keepdims=True)
            at += 1
    pick_cells(scratch, out)


def moments_call(spinor, given):
    args = (spinor, *given)
    return pl.pallas_call(
        moments_body,
        out_shape=jax.ShapeDtypeStruct((32, 128), F32),
        in_specs=[VMEM] * len(args),
        out_specs=VMEM,
        scratch_shapes=[pltpu.VMEM((24, 128), F32)],
        cost_estimate=pl.CostEstimate(flops=10**5, bytes_accessed=10**5, transcendentals=0),
    )(*args)


def row_sum_body(rows, out):
    out[...] = jnp.broadcast_to(jnp.sum(rows[...], axis=0, keepdims=True), out.shape)


def reduce_devices(rows):
    rows = lax.all_to_all(rows, ("gz", "gy"), 0, 0, tiled=True)
    (rows,) = call(row_sum_body, [(16, 128)], (rows,), 10**4)
    return lax.all_to_all(rows, "ta", 0, 0, tiled=True)


def group_of_lane():
    return lanes() // 32


def read_matrix(total, field):
    line, group = sublanes(), group_of_lane()
    re, im = jnp.zeros(TILE, F32), jnp.zeros(TILE, F32)

    def value(q, g):
        lane = 32 * g + 5 * field + q
        return jnp.broadcast_to(total[:, lane : lane + 1], TILE)

    for i in range(4):
        re = jnp.where((line == i) & (group == i), value(0, i), re)
        for d in (1, 2):
            if d == 2 and i >= 2:
                continue
            j = (i + d) % 4
            x, y = value(2 * d - 1, i), value(2 * d, i)
            here, there = (line == i) & (group == j), (line == j) & (group == i)
            re = jnp.where(here | there, x, re)
            im = jnp.where(here, y, jnp.where(there, -y, im))
    return re, im


def column(x, k):
    return jnp.broadcast_to(x[:, 32 * k : 32 * k + 1], TILE)


def line_of(x, k):
    return jnp.broadcast_to(x[k : k + 1, :], TILE)


def matmul(a, b):
    re, im = jnp.zeros(TILE, F32), jnp.zeros(TILE, F32)
    for k in range(4):
        ar, ai, br, bi = column(a[0], k), column(a[1], k), line_of(b[0], k), line_of(b[1], k)
        re = re + (ar * br - ai * bi)
        im = im + (ar * bi + ai * br)
    return re, im


def adjoint_matmul(a, b):
    line, group = sublanes(), group_of_lane()
    re, im = jnp.zeros(TILE, F32), jnp.zeros(TILE, F32)
    for k in range(4):
        ar, ai = jnp.zeros(TILE, F32), jnp.zeros(TILE, F32)
        for i in range(4):
            here = line == i
            ar = jnp.where(here, jnp.broadcast_to(a[0][k : k + 1, 32 * i : 32 * i + 1], TILE), ar)
            ai = jnp.where(here, jnp.broadcast_to(a[1][k : k + 1, 32 * i : 32 * i + 1], TILE), ai)
        br, bi = line_of(b[0], k), line_of(b[1], k)
        re = re + (ar * br + ai * bi)
        im = im + (ar * bi - ai * br)
    return re, im


def solve(c, e, lowest):
    line = sublanes()
    cr, ci, er, ei = c[0], c[1], e[0], e[1]
    good = None
    for k in range(4):
        pivot = jnp.broadcast_to(cr[k : k + 1, 32 * k : 32 * k + 1], TILE)
        floor = jnp.broadcast_to(lowest[k : k + 1, 32 * k : 32 * k + 1], TILE)
        here = pivot > floor
        good = here if good is None else good & here
        inverse = 1.0 / pivot
        rows = [line_of(x, k) * inverse for x in (cr, ci, er, ei)]
        fr, fi = column(cr, k), column(ci, k)
        at = line == k
        cr, ci = (
            jnp.where(at, rows[0], cr - (fr * rows[0] - fi * rows[1])),
            jnp.where(at, rows[1], ci - (fr * rows[1] + fi * rows[0])),
        )
        er, ei = (
            jnp.where(at, rows[2], er - (fr * rows[2] - fi * rows[3])),
            jnp.where(at, rows[3], ei - (fr * rows[3] + fi * rows[2])),
        )
    return (er, ei), good


def add(a, b):
    return a[0] + b[0], a[1] + b[1]


def sub(a, b):
    return a[0] - b[0], a[1] - b[1]


def write_coefficients(out, base, c):
    line, group = sublanes(), group_of_lane()
    for d in range(4):
        here = line == (group + d) % 4
        for part in range(2):
            row = jnp.sum(jnp.where(here, c[part], 0.0), axis=0, keepdims=True)
            out[base + 2 * d + part : base + 2 * d + part + 1, :] = row


def coefficients_body(rows, out, good_out):
    total = jnp.sum(rows[...], axis=0, keepdims=True)
    mu = [read_matrix(total, f) for f in range(4)]
    line, group = sublanes(), group_of_lane()
    diagonal = (line == group) & (line < 4)
    unit = jnp.where(diagonal, 1.0, 0.0)
    alpha, good1 = solve(mu[1], mu[0], PIVOT_GUARD * mu[1][0])
    quad = adjoint_matmul(alpha, matmul(mu[2], alpha))
    right = matmul(mu[1], alpha)
    left = adjoint_matmul(alpha, mu[1])
    rho = add(sub(quad, add(left, right)), mu[0])
    rho_size = jnp.abs(quad[0]) + jnp.abs(left[0]) + jnp.abs(right[0]) + jnp.abs(mu[0][0])
    beta, good0 = solve(mu[0], rho, PIVOT_GUARD * mu[0][0])
    p = (beta[0] + unit, beta[1])
    first = adjoint_matmul(p, matmul(mu[1], p))
    cross = adjoint_matmul(p, matmul(mu[2], alpha))
    cross2 = adjoint_matmul(alpha, matmul(mu[2], p))
    last = adjoint_matmul(alpha, matmul(mu[3], alpha))
    c = add(sub(first, add(cross, cross2)), last)
    c_size = jnp.abs(first[0]) + jnp.abs(cross[0]) + jnp.abs(cross2[0]) + jnp.abs(last[0])
    alpha1, good2 = solve(c, rho, GUARD * c_size)
    _, good3 = solve(rho, unit_pair(unit), GUARD * rho_size)
    q = matmul(alpha, alpha1)
    k = add(alpha, matmul(p, alpha1))
    write_coefficients(out, 0, k)
    write_coefficients(out, 8, q)
    good = good0 & good1 & good2 & good3
    good_out[...] = jnp.where(good, 1.0, 0.0)


def unit_pair(unit):
    return unit, jnp.zeros(TILE, F32)


def solve_body(which, c_rows, e_rows, out):
    c = read_matrix(jnp.sum(c_rows[...], axis=0, keepdims=True), which[0])
    e = read_matrix(jnp.sum(e_rows[...], axis=0, keepdims=True), which[1])
    solved, _ = solve(c, e, jnp.zeros(TILE, F32))
    write_coefficients(out, 0, solved)


def mix(re, im, coefficients, base):
    total_re = total_im = None
    for d in range(4):
        x, y = (re, im) if d == 0 else (roll_lanes(re, -32 * d), roll_lanes(im, -32 * d))
        cr = coefficients[base + 2 * d : base + 2 * d + 1, :]
        ci = coefficients[base + 2 * d + 1 : base + 2 * d + 2, :]
        a, b = x * cr - y * ci, x * ci + y * cr
        total_re = a if total_re is None else total_re + a
        total_im = b if total_im is None else total_im + b
    return total_re, total_im


def combine_body(sign, x, y, coefficients, out):
    for t in range(2):
        for c in range(12):
            re, im = mix(y[c, t], y[12 + c, t], coefficients, 0)
            out[c, t] = signed_add(x[c, t], re, sign)
            out[12 + c, t] = signed_add(x[12 + c, t], im, sign)


def final_body(info, partial, links, time_a, time_b, row_a, row_b, base, first, image, rows, out):
    recv = (time_a, time_b, row_a, row_b)
    for t in range(2):
        b = finished_spinor(info, partial, links, 0, t, recv, base)
        for s in range(4):
            for c in range(3):
                at = s * 3 + c
                re, im = first[at, t], first[12 + at, t]
                image_re, image_im = image[at, t], image[12 + at, t]
                rk = mix(re, im, rows, 0)
                ak = mix(image_re, image_im, rows, 0)
                aq = mix(image_re, image_im, rows, 8)
                bq = mix(b[0][s][c], b[1][s][c], rows, 8)
                out[pl.ds(2 * at + t, 8, stride=96), :] = rk[0] - aq[0]
                out[pl.ds(2 * (12 + at) + t, 8, stride=96), :] = rk[1] - aq[1]
                out[pl.ds(48 + 2 * at + t, 8, stride=96), :] = re - ak[0] + bq[0]
                out[pl.ds(48 + 2 * (12 + at) + t, 8, stride=96), :] = im - ak[1] + bq[1]


def send_order_body(solution_ref, residual_ref, out):
    for i, ref in enumerate((solution_ref, residual_ref)):
        for c in range(24):
            for t in range(2):
                out[pl.ds(48 * i + 2 * c + t, 8, stride=96), :] = ref[c, t]


def deliver_body(info, received, solution_ref, residual_ref):
    for i, ref in enumerate((solution_ref, residual_ref)):
        for z in range(2):
            for n in range(6):
                at = 48 * i + 8 * n
                tiles = [received[owner(info, row), z, at : at + 8, :] for row in range(4)]
                for s, tile in enumerate(swap_groups(tiles)):
                    ref[s, pl.ds(16 * n + z, 8, stride=2), :] = tile


SPINOR = (24, 2, 8, 128)
FACES = [(12, 8, 128), (12, 8, 128), (12, 2, 8, 128), (12, 2, 8, 128)]


def make_pairs(order, start):
    count = len(order)
    out = []
    for i in range(start, start + count, 2):
        a, b = order[i % count], order[(i + 1) % count]
        out += [(a, b), (b, a)]
    return out


def exchange(faces):
    times = list(range(lax.axis_size("ta")))
    blocks = lax.axis_size("gy")
    rows = [gz * blocks + gy for gy in range(blocks) for gz in ROW_OWNER[gy % 2]]
    time_a, time_b, row_a, row_b = faces
    return (
        lax.ppermute(time_a, "ta", make_pairs(times, 0)),
        lax.ppermute(time_b, "ta", make_pairs(times, 1)),
        lax.ppermute(row_a, ("gz", "gy"), make_pairs(rows, 0)),
        lax.ppermute(row_b, ("gz", "gy"), make_pairs(rows, 1)),
    )


def hop_inner(info, spinor, links, parity, with_moments=False):
    outs = [SPINOR] + ([(5, 8, 128)] if with_moments else [])

    def body(*refs):
        inner_body(parity, with_moments, *refs)

    return call(body, outs, (info, spinor, links), 8 * 10**6)


def hop_outer(info, partial, links, recv, parity, base=None, with_faces=True):
    args = (info, partial, links, *recv) + (() if base is None else (base,))

    def body(*refs):
        outer_body(parity, base is not None, with_faces, *refs)

    outs = call(body, [SPINOR] + (FACES if with_faces else []), args, 4 * 10**6)
    return outs[0], outs[1:]


def half_normal(info, spinor, faces, links, with_moments=False, with_faces=True):
    recv = exchange(faces)
    partial, *moments = hop_inner(info, spinor, links, 1, with_moments)
    odd, faces = hop_outer(info, partial, links, recv, 1)
    recv = exchange(faces)
    (partial,) = hop_inner(info, odd, links, 0)
    out, faces = hop_outer(info, partial, links, recv, 0, spinor, with_faces)
    return out, faces, moments


def faces_only(info, spinor, links):
    def body(info, spinor, links, *faces):
        write_faces(info, spinor, links, 1, faces)

    return call(body, FACES, (info, spinor, links))


def direct_branch(info, links, first, image, rows):
    def solve_call(c_rows, e_rows, c_field, e_field):
        def body(*refs):
            solve_body((c_field, e_field), *refs)

        return call(body, [(8, 128)], (c_rows, e_rows), 10**4)[0]

    def combine(sign, x, y, coefficients):
        def body(*refs):
            combine_body(sign, *refs)

        return call(body, [SPINOR], (x, y, coefficients))[0]

    alpha = solve_call(rows, rows, 1, 0)
    residual = combine(-1, first, image, alpha)
    rho = reduce_devices(moments_call(residual, ()))
    beta = solve_call(rows, rho, 0, 0)
    search = combine(1, residual, first, beta)
    faces = faces_only(info, search, links)
    halfway, faces, _ = half_normal(info, search, faces, links)
    curvature = reduce_devices(moments_call(halfway, ()))
    images, _, _ = half_normal(info, halfway, faces, links, with_faces=False)
    alpha1 = solve_call(curvature, rho, 0, 0)
    zero = jnp.zeros(SPINOR, F32)
    solution_field = combine(1, combine(1, zero, first, alpha), search, alpha1)
    residual = combine(-1, residual, images, alpha1)
    return call(send_order_body, [(768, 128)], (solution_field, residual))[0]


def local(sources, gauge_links):
    ta, gz, gy = (lax.axis_index(name) for name in ("ta", "gz", "gy"))
    odd_block = gy % 2
    position = jnp.where(odd_block == 1, jnp.array([3, 2, 0, 1])[gz], jnp.array([0, 1, 3, 2])[gz])
    info = jnp.stack(
        [ta % 2, position % 2, ta == lax.axis_size("ta") - 1, ta == 0, odd_block]
    ).astype(jnp.int32)

    args = (info, sources.reshape(4, 96, 128), gauge_links.reshape(4, 144, 128))
    (packed,) = call(pack_body, [(4, 2, 120, 128)], args)
    received = lax.all_to_all(packed, "gz", 0, 0).reshape(960, 128)
    links, first, *faces = call(
        unpack_body, [(144, 2, 8, 128), SPINOR] + FACES, (info, received)
    )
    half1, faces, moments0 = half_normal(info, first, faces, links, True)
    image, faces, moments1 = half_normal(info, half1, faces, links, True)
    half2, faces, moments2 = half_normal(info, image, faces, links, True)
    rows = reduce_devices(moments_call(half2, (*moments0, *moments1, *moments2)))
    table, good = call(coefficients_body, [(16, 128), TILE], (rows,), 10**5)

    recv = exchange(faces)
    (partial,) = hop_inner(info, half2, links, 1)
    odd, faces = hop_outer(info, partial, links, recv, 1)
    recv = exchange(faces)
    (partial,) = hop_inner(info, odd, links, 0)

    def moment_branch():
        given = (info, partial, links, *recv, half2, first, image, table)
        return call(final_body, [(768, 128)], given, 10**7)[0]

    out = lax.cond(
        good[0, 0] > 0.5,
        moment_branch,
        lambda: direct_branch(info, links, first, image, rows),
    )
    received = lax.all_to_all(out.reshape(4, 2, 96, 128), "gz", 0, 0)
    done = call(deliver_body, [(4, 96, 128)] * 2, (info, received))
    return tuple(x.reshape(sources.shape) for x in done)


def solution(mesh):
    spinor_spec = P(None, None, None, None, "ta", "gz", "gy")
    link_spec = P(None, None, None, None, None, "ta", "gz", "gy")
    return jax.shard_map(
        local,
        mesh=mesh,
        in_specs=(spinor_spec, link_spec),
        out_specs=(spinor_spec, spinor_spec),
        check_vma=False,
    )
```

time: 700 us -> 212 us (0.30); the launches traced: 689 us -> 211 us
  blocking collectives: 307 us -> 61.6 us
  other arithmetic: 152 us -> 0 us
  starting transfers between devices: 165 us -> 113 us
  Pallas kernels: 0 us -> 23.5 us
  waiting for transfers between devices: 27.2 us -> 4.13 us
  matrix products: 16.3 us -> 0 us
  between operations: 11.7 us -> 3.11 us
    psum x3 -> x0, blocking collectives: 307 us -> none  [the longest x2 203 us: residual_total(): return lax.psum(gram(residual, residual), ('ta', 'gz', 'gy'))]
    div x10 -> x0, other arithmetic: 116 us -> none  [the longest x3 65.1 us: cholesky_solve(): back_rows[row_index] = running / factor[row_index, row_index]]
    all_to_all x0 -> x4, blocking collectives: none -> 61.6 us  [the longest x1 18.3 us: local(): received = lax.all_to_all(packed, 'gz', 0, 0).reshape(960, 128)]
    ppermute x48 -> x32, starting transfers between devices: 165 us -> 113 us  [the longest x8 42 us: exchange(): lax.ppermute(time_b, 'ta', make_pairs(times, 1))]
    pallas_call x0 -> x22, Pallas kernels: none -> 23.5 us  [the longest x21 21.6 us: call(): pl.pallas_call(body, out_shape=shapes, in_specs=in_specs, out_specs=[VMEM...]
    ppermute x48 -> x32, waiting for transfers between devices: 27.2 us -> 4.13 us  [the longest x8 4.06 us: exchange(): lax.ppermute(time_b, 'ta', make_pairs(times, 1))]
    dot_general x36 -> x0, matrix products: 16.3 us -> none  [the longest x16 8.7 us: contract(): lax.dot_general(left_flat, right_flat, (((1,), (1,)), ((), ())), precisio...]
    another operation x290 -> x0, other arithmetic: 14.7 us -> none  [the longest x125 4.53 us: project(): return jnp.stack([jnp.stack(real_rows, 1), jnp.stack(imag_rows, 1)], 1)]
  transfers between devices with their start and end apart: 48 -> 32, of which waited for: 11 -> 7; matrix products, arithmetic and copies ran while one was open for 2% -> 0% of each run, Pallas kernels for 0% -> 5%
where the time goes in v1:
time: 212 us; the launch traced here: 211 us
  starting transfers between devices  113 us (53%)
  blocking collectives  61.6 us (29%)
  Pallas kernels  23.5 us (11%)
  local copies, waits for them, and re-layouts  5.02 us (2%)
  waiting for transfers between devices  4.13 us (2%)
  between operations  3.11 us (1%)
    ppermute x8, starting transfers between devices, exchange(): lax.ppermute(time_b, 'ta', make_pairs(times, 1))  42 us
    ppermute x8, starting transfers between devices, exchange(): lax.ppermute(row_a, ('gz', 'gy'), make_pairs(rows, 0))  37.5 us
    pallas_call x21, Pallas kernels, call(): pl.pallas_call(body, out_shape=shapes, in_specs=in_specs, out_specs=[VMEM...  21.6 us
    ppermute x8, starting transfers between devices, exchange(): lax.ppermute(row_b, ('gz', 'gy'), make_pairs(rows, 1))  18.4 us
    all_to_all x1, blocking collectives, local(): received = lax.all_to_all(packed, 'gz', 0, 0).reshape(960, 128)  18.3 us
    all_to_all x1, blocking collectives, reduce_devices(): return lax.all_to_all(rows, 'ta', 0, 0, tiled=True)  18.1 us
    ppermute x8, starting transfers between devices, exchange(): lax.ppermute(time_a, 'ta', make_pairs(times, 0))  15.4 us
    all_to_all x1, blocking collectives, reduce_devices(): rows = lax.all_to_all(rows, ('gz', 'gy'), 0, 0, tiled=True)  12.8 us
  transfers between devices with their start and end apart: 32, of which 7 were waited for; matrix products, arithmetic and copies ran while one was open for 0% of the time, Pallas kernels for 5%

profile of v1, /device:TPU:1, one launch (start us, length us, event | category | flops | bytes accessed | tf_op | source)
XLA Modules:
  0.0 210.8 jit_solution(8794649488708620570)
XLA Ops:
  0.7 1.3 dynamic_slice.7
  1.9 1.2 dynamic_slice.6
  4.6 1.0 copy-done.5
  5.5 0.9 copy-done.6
  6.5 1.8 shard_map.59
  8.3 18.3 %all_to_all.67 = f32[4,2,120,128]{3,2,1,0:T(8,128)S(1)} all-to-all(f32[4,2,120,128]{3,2,1,0:T(8,128)S(1)} %shard_map.59), channel_id=1, replica_groups=mesh['ta'=16,'gz'=4,'gy'=8] {'gz'}, dimensions={0} | all-to-all | bytes 983040 | tf_op jit(solution)/shard_map/all_to_all | solution.py:636
  26.6 2.6 %shard_map.60 = (f32[144,2,8,128]{3,2,1,0:T(8,128)S(1)}, f32[24,2,8,128]{3,2,1,0:T(8,128)S(1)}, f32[12,8,128]{2,1,0:T(8,128)S(1)}, f32[12,8,128]{2,1,0:T(8,128)S...) custom-call(s32[5]{0:T(128)S(1)} %stack.31.info.refs_0_, f32[960,128]{1,0:T(8,128)S(1)} %bitcast.38), custom_call_target="tpu_custom_call" | custom-call | flops 1000000 | bytes 491540 | tf_op jit(solution)/shard_map/pallas_call | solution.py:30
  29.2 2.9 %collective-permute-start.18 = (f32[12,2,8,128]{3,2,1,0:T(8,128)S(1)}, f32[12,2,8,128]{3,2,1,0:T(8,128)S(1)}, u32[]{:S(2)}, u32[]{:S(2)}) collective-permute-start(f32[12,2,8,128]{3,2,1,0:T(8,128)S(1)} %get-tuple-element.128), channel_id=1, source_target_pairs={{0,8},{8,0},{24,16},{16,24},{17,25},{25,17},{9,1},{1,9},{2,10},{10... | collective-permute-start | bytes 294920 | tf_op jit(solution)/shard_map/ppermute | solution.py:556
  32.1 2.0 collective-permute-start.19
  34.1 1.9 collective-permute-start.16
  36.0 8.2 %collective-permute-start.17 = (f32[12,8,128]{2,1,0:T(8,128)S(1)}, f32[12,8,128]{2,1,0:T(8,128)S(1)}, u32[]{:S(2)}, u32[]{:S(2)}) collective-permute-start(f32[12,8,128]{2,1,0:T(8,128)S(1)} %get-tuple-element.127), channel_id=1, source_target_pairs={{32,64},{64,32},{96,128},{128,96},{160,192},{192,160},{224,256},{2... | collective-permute-start | bytes 147464 | tf_op jit(solution)/shard_map/ppermute | solution.py:555
  44.2 0.9 shard_map.61
  45.7 0.7 shard_map.62
  46.4 6.0 %collective-permute-start.22 = (f32[12,2,8,128]{3,2,1,0:T(8,128)S(1)}, f32[12,2,8,128]{3,2,1,0:T(8,128)S(1)}, u32[]{:S(2)}, u32[]{:S(2)}) collective-permute-start(f32[12,2,8,128]{3,2,1,0:T(8,128)S(1)} %get-tuple-element.133), channel_id=1, source_target_pairs={{0,8},{8,0},{24,16},{16,24},{17,25},{25,17},{9,1},{1,9},{2,10},{10... | collective-permute-start | bytes 294920 | tf_op jit(solution)/shard_map/ppermute | solution.py:556
  52.4 1.9 collective-permute-start.23
  54.4 1.9 collective-permute-start.20
  56.3 4.9 %collective-permute-start.21 = (f32[12,8,128]{2,1,0:T(8,128)S(1)}, f32[12,8,128]{2,1,0:T(8,128)S(1)}, u32[]{:S(2)}, u32[]{:S(2)}) collective-permute-start(f32[12,8,128]{2,1,0:T(8,128)S(1)} %get-tuple-element.132), channel_id=1, source_target_pairs={{32,64},{64,32},{96,128},{128,96},{160,192},{192,160},{224,256},{2... | collective-permute-start | bytes 147464 | tf_op jit(solution)/shard_map/ppermute | solution.py:555
  61.2 0.8 shard_map.63.refs_1_
  62.0 0.6 collective-permute-done.21.refs_4_
  62.6 0.7 shard_map.64
  63.4 3.9 %collective-permute-start.26 = (f32[12,2,8,128]{3,2,1,0:T(8,128)S(1)}, f32[12,2,8,128]{3,2,1,0:T(8,128)S(1)}, u32[]{:S(2)}, u32[]{:S(2)}) collective-permute-start(f32[12,2,8,128]{3,2,1,0:T(8,128)S(1)} %get-tuple-element.139), channel_id=1, source_target_pairs={{0,8},{8,0},{24,16},{16,24},{17,25},{25,17},{9,1},{1,9},{2,10},{10... | collective-permute-start | bytes 294920 | tf_op jit(solution)/shard_map/ppermute | solution.py:556
  67.2 2.9 %collective-permute-start.27 = (f32[12,2,8,128]{3,2,1,0:T(8,128)S(1)}, f32[12,2,8,128]{3,2,1,0:T(8,128)S(1)}, u32[]{:S(2)}, u32[]{:S(2)}) collective-permute-start(f32[12,2,8,128]{3,2,1,0:T(8,128)S(1)} %get-tuple-element.140), channel_id=1, source_target_pairs={{8,24},{24,8},{16,17},{17,16},{25,9},{9,25},{1,2},{2,1},{10,26},{2... | collective-permute-start | bytes 294920 | tf_op jit(solution)/shard_map/ppermute | solution.py:557
  70.2 1.9 collective-permute-start.24
  72.1 4.8 %collective-permute-start.25 = (f32[12,8,128]{2,1,0:T(8,128)S(1)}, f32[12,8,128]{2,1,0:T(8,128)S(1)}, u32[]{:S(2)}, u32[]{:S(2)}) collective-permute-start(f32[12,8,128]{2,1,0:T(8,128)S(1)} %get-tuple-element.138), channel_id=1, source_target_pairs={{32,64},{64,32},{96,128},{128,96},{160,192},{192,160},{224,256},{2... | collective-permute-start | bytes 147464 | tf_op jit(solution)/shard_map/ppermute | solution.py:555
  76.9 0.9 shard_map.65
  78.4 0.7 shard_map.66
  79.1 5.7 %collective-permute-start.30 = (f32[12,2,8,128]{3,2,1,0:T(8,128)S(1)}, f32[12,2,8,128]{3,2,1,0:T(8,128)S(1)}, u32[]{:S(2)}, u32[]{:S(2)}) collective-permute-start(f32[12,2,8,128]{3,2,1,0:T(8,128)S(1)} %get-tuple-element.144), channel_id=1, source_target_pairs={{0,8},{8,0},{24,16},{16,24},{17,25},{25,17},{9,1},{1,9},{2,10},{10... | collective-permute-start | bytes 294920 | tf_op jit(solution)/shard_map/ppermute | solution.py:556
  84.8 1.9 collective-permute-start.31
  86.7 1.9 collective-permute-start.28
  88.7 4.9 %collective-permute-start.29 = (f32[12,8,128]{2,1,0:T(8,128)S(1)}, f32[12,8,128]{2,1,0:T(8,128)S(1)}, u32[]{:S(2)}, u32[]{:S(2)}) collective-permute-start(f32[12,8,128]{2,1,0:T(8,128)S(1)} %get-tuple-element.143), channel_id=1, source_target_pairs={{32,64},{64,32},{96,128},{128,96},{160,192},{192,160},{224,256},{2... | collective-permute-start | bytes 147464 | tf_op jit(solution)/shard_map/ppermute | solution.py:555
  93.5 0.8 shard_map.67.refs_1_
  95.0 0.7 shard_map.68
  95.7 3.9 %collective-permute-start.34 = (f32[12,2,8,128]{3,2,1,0:T(8,128)S(1)}, f32[12,2,8,128]{3,2,1,0:T(8,128)S(1)}, u32[]{:S(2)}, u32[]{:S(2)}) collective-permute-start(f32[12,2,8,128]{3,2,1,0:T(8,128)S(1)} %get-tuple-element.150), channel_id=1, source_target_pairs={{0,8},{8,0},{24,16},{16,24},{17,25},{25,17},{9,1},{1,9},{2,10},{10... | collective-permute-start | bytes 294920 | tf_op jit(solution)/shard_map/ppermute | solution.py:556
  99.6 2.9 %collective-permute-start.35 = (f32[12,2,8,128]{3,2,1,0:T(8,128)S(1)}, f32[12,2,8,128]{3,2,1,0:T(8,128)S(1)}, u32[]{:S(2)}, u32[]{:S(2)}) collective-permute-start(f32[12,2,8,128]{3,2,1,0:T(8,128)S(1)} %get-tuple-element.151), channel_id=1, source_target_pairs={{8,24},{24,8},{16,17},{17,16},{25,9},{9,25},{1,2},{2,1},{10,26},{2... | collective-permute-start | bytes 294920 | tf_op jit(solution)/shard_map/ppermute | solution.py:557
  102.5 1.9 collective-permute-start.32
  104.5 4.8 %collective-permute-start.33 = (f32[12,8,128]{2,1,0:T(8,128)S(1)}, f32[12,8,128]{2,1,0:T(8,128)S(1)}, u32[]{:S(2)}, u32[]{:S(2)}) collective-permute-start(f32[12,8,128]{2,1,0:T(8,128)S(1)} %get-tuple-element.149), channel_id=1, source_target_pairs={{32,64},{64,32},{96,128},{128,96},{160,192},{192,160},{224,256},{2... | collective-permute-start | bytes 147464 | tf_op jit(solution)/shard_map/ppermute | solution.py:555
  109.3 0.9 shard_map.69
  110.7 0.7 shard_map.70
  111.5 5.7 %collective-permute-start.38 = (f32[12,2,8,128]{3,2,1,0:T(8,128)S(1)}, f32[12,2,8,128]{3,2,1,0:T(8,128)S(1)}, u32[]{:S(2)}, u32[]{:S(2)}) collective-permute-start(f32[12,2,8,128]{3,2,1,0:T(8,128)S(1)} %get-tuple-element.155), channel_id=1, source_target_pairs={{0,8},{8,0},{24,16},{16,24},{17,25},{25,17},{9,1},{1,9},{2,10},{10... | collective-permute-start | bytes 294920 | tf_op jit(solution)/shard_map/ppermute | solution.py:556
  117.1 1.9 collective-permute-start.39
  119.1 1.9 collective-permute-start.36
  121.0 4.9 %collective-permute-start.37 = (f32[12,8,128]{2,1,0:T(8,128)S(1)}, f32[12,8,128]{2,1,0:T(8,128)S(1)}, u32[]{:S(2)}, u32[]{:S(2)}) collective-permute-start(f32[12,8,128]{2,1,0:T(8,128)S(1)} %get-tuple-element.154), channel_id=1, source_target_pairs={{32,64},{64,32},{96,128},{128,96},{160,192},{192,160},{224,256},{2... | collective-permute-start | bytes 147464 | tf_op jit(solution)/shard_map/ppermute | solution.py:555
  125.9 0.8 shard_map.71.refs_1_
  127.3 0.7 shard_map.72
  128.1 3.9 %collective-permute-start.42 = (f32[12,2,8,128]{3,2,1,0:T(8,128)S(1)}, f32[12,2,8,128]{3,2,1,0:T(8,128)S(1)}, u32[]{:S(2)}, u32[]{:S(2)}) collective-permute-start(f32[12,2,8,128]{3,2,1,0:T(8,128)S(1)} %get-tuple-element.164), channel_id=1, source_target_pairs={{0,8},{8,0},{24,16},{16,24},{17,25},{25,17},{9,1},{1,9},{2,10},{10... | collective-permute-start | bytes 294920 | tf_op jit(solution)/shard_map/ppermute | solution.py:556
  132.0 2.9 %collective-permute-start.43 = (f32[12,2,8,128]{3,2,1,0:T(8,128)S(1)}, f32[12,2,8,128]{3,2,1,0:T(8,128)S(1)}, u32[]{:S(2)}, u32[]{:S(2)}) collective-permute-start(f32[12,2,8,128]{3,2,1,0:T(8,128)S(1)} %get-tuple-element.165), channel_id=1, source_target_pairs={{8,24},{24,8},{16,17},{17,16},{25,9},{9,25},{1,2},{2,1},{10,26},{2... | collective-permute-start | bytes 294920 | tf_op jit(solution)/shard_map/ppermute | solution.py:557
  134.9 1.9 collective-permute-start.40
  136.8 4.8 %collective-permute-start.41 = (f32[12,8,128]{2,1,0:T(8,128)S(1)}, f32[12,8,128]{2,1,0:T(8,128)S(1)}, u32[]{:S(2)}, u32[]{:S(2)}) collective-permute-start(f32[12,8,128]{2,1,0:T(8,128)S(1)} %get-tuple-element.163), channel_id=1, source_target_pairs={{32,64},{64,32},{96,128},{128,96},{160,192},{192,160},{224,256},{2... | collective-permute-start | bytes 147464 | tf_op jit(solution)/shard_map/ppermute | solution.py:555
  141.6 0.8 shard_map.76.refs_1_
  142.5 0.6 collective-permute-done.41.refs_4_
  143.1 0.7 shard_map.77
  143.8 5.7 %collective-permute-start.46 = (f32[12,2,8,128]{3,2,1,0:T(8,128)S(1)}, f32[12,2,8,128]{3,2,1,0:T(8,128)S(1)}, u32[]{:S(2)}, u32[]{:S(2)}) collective-permute-start(f32[12,2,8,128]{3,2,1,0:T(8,128)S(1)} %get-tuple-element.169), channel_id=1, source_target_pairs={{0,8},{8,0},{24,16},{16,24},{17,25},{25,17},{9,1},{1,9},{2,10},{10... | collective-permute-start | bytes 294920 | tf_op jit(solution)/shard_map/ppermute | solution.py:556
  149.5 1.9 collective-permute-start.47
  151.4 1.9 collective-permute-start.44
  153.4 4.9 %collective-permute-start.45 = (f32[12,8,128]{2,1,0:T(8,128)S(1)}, f32[12,8,128]{2,1,0:T(8,128)S(1)}, u32[]{:S(2)}, u32[]{:S(2)}) collective-permute-start(f32[12,8,128]{2,1,0:T(8,128)S(1)} %get-tuple-element.168), channel_id=1, source_target_pairs={{32,64},{64,32},{96,128},{128,96},{160,192},{192,160},{224,256},{2... | collective-permute-start | bytes 147464 | tf_op jit(solution)/shard_map/ppermute | solution.py:555
  158.2 1.9 shard_map.73
  160.1 12.8 %all_to_all.68 = f32[32,1,128]{2,1,0:T(1,128)S(1)} all-to-all(f32[32,1,128]{2,1,0:T(1,128)} %bitcast.52), channel_id=1, replica_groups=mesh['ta'=16,'gz'=4,'gy'=8] {'gz','gy'}, dimensions={0} | all-to-all | bytes 32768 | tf_op jit(solution)/shard_map/all_to_all | solution.py:335
  172.9 18.1 %all_to_all.69 = f32[16,1,128]{2,1,0:T(1,128)S(1)} all-to-all(f32[16,1,128]{2,1,0:T(1,128)S(1)} %bitcast.46), channel_id=1, replica_groups=mesh['ta'=16,'gz'=4,'gy'=8] {'ta'}, dimensions={0} | all-to-all | bytes 16384 | tf_op jit(solution)/shard_map/all_to_all | solution.py:337
  191.0 1.9 shard_map.75
  194.0 0.8 shard_map.78
  194.9 1.5 conditional.1
  195.2 1.2 branch_1_fun.1
  196.4 12.4 %all_to_all.70.received = f32[4,2,96,128]{3,2,1,0:T(8,128)S(1)} all-to-all(f32[4,2,96,128]{3,2,1,0:T(8,128)S(1)} %bitcast.49), channel_id=1, replica_groups=mesh['ta'=16,'gz'=4,'gy'=8] {'gz'}, dimensions={0} | all-to-all | bytes 786432 | tf_op jit(solution)/shard_map/all_to_all | solution.py:661
  208.8 2.0 shard_map.79
  (41 shorter events, 3.5 us)
Async XLA Ops:
  4.6 1.0 copy-start.5
  5.5 0.9 copy-start.6
  29.2 16.4 %collective-permute-start.18 = (f32[12,2,8,128]{3,2,1,0:T(8,128)S(1)}, f32[12,2,8,128]{3,2,1,0:T(8,128)S(1)}, u32[]{:S(2)}, u32[]{:S(2)}) collective-permute-start(f32[12,2,8,128]{3,2,1,0:T(8,128)S(1)} %get-tuple-element.128), channel_id=1, source_target_pairs={{0,8},{8,0},{24,16},{16,24},{17,25},{25,17},{9,1},{1,9},{2,10},{10... | collective-permute-start | bytes 294920 | tf_op jit(solution)/shard_map/ppermute | solution.py:556
  32.1 13.6 %collective-permute-start.19 = (f32[12,2,8,128]{3,2,1,0:T(8,128)S(1)}, f32[12,2,8,128]{3,2,1,0:T(8,128)S(1)}, u32[]{:S(2)}, u32[]{:S(2)}) collective-permute-start(f32[12,2,8,128]{3,2,1,0:T(8,128)S(1)} %get-tuple-element.129), channel_id=1, source_target_pairs={{8,24},{24,8},{16,17},{17,16},{25,9},{9,25},{1,2},{2,1},{10,26},{2... | collective-permute-start | bytes 294920 | tf_op jit(solution)/shard_map/ppermute | solution.py:557
  34.1 11.0 %collective-permute-start.16 = (f32[12,8,128]{2,1,0:T(8,128)S(1)}, f32[12,8,128]{2,1,0:T(8,128)S(1)}, u32[]{:S(2)}, u32[]{:S(2)}) collective-permute-start(f32[12,8,128]{2,1,0:T(8,128)S(1)} %get-tuple-element.126), channel_id=1, source_target_pairs={{0,32},{32,0},{64,96},{96,64},{128,160},{160,128},{192,224},{224,1... | collective-permute-start | bytes 147464 | tf_op jit(solution)/shard_map/ppermute | solution.py:554
  36.0 9.6 %collective-permute-start.17 = (f32[12,8,128]{2,1,0:T(8,128)S(1)}, f32[12,8,128]{2,1,0:T(8,128)S(1)}, u32[]{:S(2)}, u32[]{:S(2)}) collective-permute-start(f32[12,8,128]{2,1,0:T(8,128)S(1)} %get-tuple-element.127), channel_id=1, source_target_pairs={{32,64},{64,32},{96,128},{128,96},{160,192},{192,160},{224,256},{2... | collective-permute-start | bytes 147464 | tf_op jit(solution)/shard_map/ppermute | solution.py:555
  45.1 11.2 %copy-start.7 = (f32[5,8,128]{2,1,0:T(8,128)}, f32[5,8,128]{2,1,0:T(8,128)S(1)}, u32[]{:S(2)}) copy-start(f32[5,8,128]{2,1,0:T(8,128)S(1)} %get-tuple-element.158.refs_0_) | copy-start | bytes 61444
  46.4 16.2 %collective-permute-start.22 = (f32[12,2,8,128]{3,2,1,0:T(8,128)S(1)}, f32[12,2,8,128]{3,2,1,0:T(8,128)S(1)}, u32[]{:S(2)}, u32[]{:S(2)}) collective-permute-start(f32[12,2,8,128]{3,2,1,0:T(8,128)S(1)} %get-tuple-element.133), channel_id=1, source_target_pairs={{0,8},{8,0},{24,16},{16,24},{17,25},{25,17},{9,1},{1,9},{2,10},{10... | collective-permute-start | bytes 294920 | tf_op jit(solution)/shard_map/ppermute | solution.py:556
  52.4 10.2 %collective-permute-start.23 = (f32[12,2,8,128]{3,2,1,0:T(8,128)S(1)}, f32[12,2,8,128]{3,2,1,0:T(8,128)S(1)}, u32[]{:S(2)}, u32[]{:S(2)}) collective-permute-start(f32[12,2,8,128]{3,2,1,0:T(8,128)S(1)} %get-tuple-element.134), channel_id=1, source_target_pairs={{8,24},{24,8},{16,17},{17,16},{25,9},{9,25},{1,2},{2,1},{10,26},{2... | collective-permute-start | bytes 294920 | tf_op jit(solution)/shard_map/ppermute | solution.py:557
  54.4 7.6 %collective-permute-start.20 = (f32[12,8,128]{2,1,0:T(8,128)S(1)}, f32[12,8,128]{2,1,0:T(8,128)S(1)}, u32[]{:S(2)}, u32[]{:S(2)}) collective-permute-start(f32[12,8,128]{2,1,0:T(8,128)S(1)} %get-tuple-element.131), channel_id=1, source_target_pairs={{0,32},{32,0},{64,96},{96,64},{128,160},{160,128},{192,224},{224,1... | collective-permute-start | bytes 147464 | tf_op jit(solution)/shard_map/ppermute | solution.py:554
  56.3 6.3 %collective-permute-start.21 = (f32[12,8,128]{2,1,0:T(8,128)S(1)}, f32[12,8,128]{2,1,0:T(8,128)S(1)}, u32[]{:S(2)}, u32[]{:S(2)}) collective-permute-start(f32[12,8,128]{2,1,0:T(8,128)S(1)} %get-tuple-element.132), channel_id=1, source_target_pairs={{32,64},{64,32},{96,128},{128,96},{160,192},{192,160},{224,256},{2... | collective-permute-start | bytes 147464 | tf_op jit(solution)/shard_map/ppermute | solution.py:555
  63.4 15.0 %collective-permute-start.26 = (f32[12,2,8,128]{3,2,1,0:T(8,128)S(1)}, f32[12,2,8,128]{3,2,1,0:T(8,128)S(1)}, u32[]{:S(2)}, u32[]{:S(2)}) collective-permute-start(f32[12,2,8,128]{3,2,1,0:T(8,128)S(1)} %get-tuple-element.139), channel_id=1, source_target_pairs={{0,8},{8,0},{24,16},{16,24},{17,25},{25,17},{9,1},{1,9},{2,10},{10... | collective-permute-start | bytes 294920 | tf_op jit(solution)/shard_map/ppermute | solution.py:556
  67.2 11.1 %collective-permute-start.27 = (f32[12,2,8,128]{3,2,1,0:T(8,128)S(1)}, f32[12,2,8,128]{3,2,1,0:T(8,128)S(1)}, u32[]{:S(2)}, u32[]{:S(2)}) collective-permute-start(f32[12,2,8,128]{3,2,1,0:T(8,128)S(1)} %get-tuple-element.140), channel_id=1, source_target_pairs={{8,24},{24,8},{16,17},{17,16},{25,9},{9,25},{1,2},{2,1},{10,26},{2... | collective-permute-start | bytes 294920 | tf_op jit(solution)/shard_map/ppermute | solution.py:557
  70.2 7.7 %collective-permute-start.24 = (f32[12,8,128]{2,1,0:T(8,128)S(1)}, f32[12,8,128]{2,1,0:T(8,128)S(1)}, u32[]{:S(2)}, u32[]{:S(2)}) collective-permute-start(f32[12,8,128]{2,1,0:T(8,128)S(1)} %get-tuple-element.137), channel_id=1, source_target_pairs={{0,32},{32,0},{64,96},{96,64},{128,160},{160,128},{192,224},{224,1... | collective-permute-start | bytes 147464 | tf_op jit(solution)/shard_map/ppermute | solution.py:554
  72.1 6.3 %collective-permute-start.25 = (f32[12,8,128]{2,1,0:T(8,128)S(1)}, f32[12,8,128]{2,1,0:T(8,128)S(1)}, u32[]{:S(2)}, u32[]{:S(2)}) collective-permute-start(f32[12,8,128]{2,1,0:T(8,128)S(1)} %get-tuple-element.138), channel_id=1, source_target_pairs={{32,64},{64,32},{96,128},{128,96},{160,192},{192,160},{224,256},{2... | collective-permute-start | bytes 147464 | tf_op jit(solution)/shard_map/ppermute | solution.py:555
  77.8 10.8 %copy-start.8 = (f32[5,8,128]{2,1,0:T(8,128)}, f32[5,8,128]{2,1,0:T(8,128)S(1)}, u32[]{:S(2)}) copy-start(f32[5,8,128]{2,1,0:T(8,128)S(1)} %get-tuple-element.159.refs_1_) | copy-start | bytes 61444
  79.1 15.9 %collective-permute-start.30 = (f32[12,2,8,128]{3,2,1,0:T(8,128)S(1)}, f32[12,2,8,128]{3,2,1,0:T(8,128)S(1)}, u32[]{:S(2)}, u32[]{:S(2)}) collective-permute-start(f32[12,2,8,128]{3,2,1,0:T(8,128)S(1)} %get-tuple-element.144), channel_id=1, source_target_pairs={{0,8},{8,0},{24,16},{16,24},{17,25},{25,17},{9,1},{1,9},{2,10},{10... | collective-permute-start | bytes 294920 | tf_op jit(solution)/shard_map/ppermute | solution.py:556
  84.8 10.2 %collective-permute-start.31 = (f32[12,2,8,128]{3,2,1,0:T(8,128)S(1)}, f32[12,2,8,128]{3,2,1,0:T(8,128)S(1)}, u32[]{:S(2)}, u32[]{:S(2)}) collective-permute-start(f32[12,2,8,128]{3,2,1,0:T(8,128)S(1)} %get-tuple-element.145), channel_id=1, source_target_pairs={{8,24},{24,8},{16,17},{17,16},{25,9},{9,25},{1,2},{2,1},{10,26},{2... | collective-permute-start | bytes 294920 | tf_op jit(solution)/shard_map/ppermute | solution.py:557
  86.7 7.6 %collective-permute-start.28 = (f32[12,8,128]{2,1,0:T(8,128)S(1)}, f32[12,8,128]{2,1,0:T(8,128)S(1)}, u32[]{:S(2)}, u32[]{:S(2)}) collective-permute-start(f32[12,8,128]{2,1,0:T(8,128)S(1)} %get-tuple-element.142), channel_id=1, source_target_pairs={{0,32},{32,0},{64,96},{96,64},{128,160},{160,128},{192,224},{224,1... | collective-permute-start | bytes 147464 | tf_op jit(solution)/shard_map/ppermute | solution.py:554
  88.7 6.3 %collective-permute-start.29 = (f32[12,8,128]{2,1,0:T(8,128)S(1)}, f32[12,8,128]{2,1,0:T(8,128)S(1)}, u32[]{:S(2)}, u32[]{:S(2)}) collective-permute-start(f32[12,8,128]{2,1,0:T(8,128)S(1)} %get-tuple-element.143), channel_id=1, source_target_pairs={{32,64},{64,32},{96,128},{128,96},{160,192},{192,160},{224,256},{2... | collective-permute-start | bytes 147464 | tf_op jit(solution)/shard_map/ppermute | solution.py:555
  95.7 15.0 %collective-permute-start.34 = (f32[12,2,8,128]{3,2,1,0:T(8,128)S(1)}, f32[12,2,8,128]{3,2,1,0:T(8,128)S(1)}, u32[]{:S(2)}, u32[]{:S(2)}) collective-permute-start(f32[12,2,8,128]{3,2,1,0:T(8,128)S(1)} %get-tuple-element.150), channel_id=1, source_target_pairs={{0,8},{8,0},{24,16},{16,24},{17,25},{25,17},{9,1},{1,9},{2,10},{10... | collective-permute-start | bytes 294920 | tf_op jit(solution)/shard_map/ppermute | solution.py:556
  99.6 11.1 %collective-permute-start.35 = (f32[12,2,8,128]{3,2,1,0:T(8,128)S(1)}, f32[12,2,8,128]{3,2,1,0:T(8,128)S(1)}, u32[]{:S(2)}, u32[]{:S(2)}) collective-permute-start(f32[12,2,8,128]{3,2,1,0:T(8,128)S(1)} %get-tuple-element.151), channel_id=1, source_target_pairs={{8,24},{24,8},{16,17},{17,16},{25,9},{9,25},{1,2},{2,1},{10,26},{2... | collective-permute-start | bytes 294920 | tf_op jit(solution)/shard_map/ppermute | solution.py:557
  102.5 7.7 %collective-permute-start.32 = (f32[12,8,128]{2,1,0:T(8,128)S(1)}, f32[12,8,128]{2,1,0:T(8,128)S(1)}, u32[]{:S(2)}, u32[]{:S(2)}) collective-permute-start(f32[12,8,128]{2,1,0:T(8,128)S(1)} %get-tuple-element.148), channel_id=1, source_target_pairs={{0,32},{32,0},{64,96},{96,64},{128,160},{160,128},{192,224},{224,1... | collective-permute-start | bytes 147464 | tf_op jit(solution)/shard_map/ppermute | solution.py:554
  104.5 6.3 %collective-permute-start.33 = (f32[12,8,128]{2,1,0:T(8,128)S(1)}, f32[12,8,128]{2,1,0:T(8,128)S(1)}, u32[]{:S(2)}, u32[]{:S(2)}) collective-permute-start(f32[12,8,128]{2,1,0:T(8,128)S(1)} %get-tuple-element.149), channel_id=1, source_target_pairs={{32,64},{64,32},{96,128},{128,96},{160,192},{192,160},{224,256},{2... | collective-permute-start | bytes 147464 | tf_op jit(solution)/shard_map/ppermute | solution.py:555
  110.2 10.8 %copy-start.9 = (f32[5,8,128]{2,1,0:T(8,128)}, f32[5,8,128]{2,1,0:T(8,128)S(1)}, u32[]{:S(2)}) copy-start(f32[5,8,128]{2,1,0:T(8,128)S(1)} %get-tuple-element.160.refs_2_) | copy-start | bytes 61444
  111.5 15.9 %collective-permute-start.38 = (f32[12,2,8,128]{3,2,1,0:T(8,128)S(1)}, f32[12,2,8,128]{3,2,1,0:T(8,128)S(1)}, u32[]{:S(2)}, u32[]{:S(2)}) collective-permute-start(f32[12,2,8,128]{3,2,1,0:T(8,128)S(1)} %get-tuple-element.155), channel_id=1, source_target_pairs={{0,8},{8,0},{24,16},{16,24},{17,25},{25,17},{9,1},{1,9},{2,10},{10... | collective-permute-start | bytes 294920 | tf_op jit(solution)/shard_map/ppermute | solution.py:556
  117.1 10.2 %collective-permute-start.39 = (f32[12,2,8,128]{3,2,1,0:T(8,128)S(1)}, f32[12,2,8,128]{3,2,1,0:T(8,128)S(1)}, u32[]{:S(2)}, u32[]{:S(2)}) collective-permute-start(f32[12,2,8,128]{3,2,1,0:T(8,128)S(1)} %get-tuple-element.156), channel_id=1, source_target_pairs={{8,24},{24,8},{16,17},{17,16},{25,9},{9,25},{1,2},{2,1},{10,26},{2... | collective-permute-start | bytes 294920 | tf_op jit(solution)/shard_map/ppermute | solution.py:557
  119.1 7.6 %collective-permute-start.36 = (f32[12,8,128]{2,1,0:T(8,128)S(1)}, f32[12,8,128]{2,1,0:T(8,128)S(1)}, u32[]{:S(2)}, u32[]{:S(2)}) collective-permute-start(f32[12,8,128]{2,1,0:T(8,128)S(1)} %get-tuple-element.153), channel_id=1, source_target_pairs={{0,32},{32,0},{64,96},{96,64},{128,160},{160,128},{192,224},{224,1... | collective-permute-start | bytes 147464 | tf_op jit(solution)/shard_map/ppermute | solution.py:554
  121.0 6.3 %collective-permute-start.37 = (f32[12,8,128]{2,1,0:T(8,128)S(1)}, f32[12,8,128]{2,1,0:T(8,128)S(1)}, u32[]{:S(2)}, u32[]{:S(2)}) collective-permute-start(f32[12,8,128]{2,1,0:T(8,128)S(1)} %get-tuple-element.154), channel_id=1, source_target_pairs={{32,64},{64,32},{96,128},{128,96},{160,192},{192,160},{224,256},{2... | collective-permute-start | bytes 147464 | tf_op jit(solution)/shard_map/ppermute | solution.py:555
  128.1 15.0 %collective-permute-start.42 = (f32[12,2,8,128]{3,2,1,0:T(8,128)S(1)}, f32[12,2,8,128]{3,2,1,0:T(8,128)S(1)}, u32[]{:S(2)}, u32[]{:S(2)}) collective-permute-start(f32[12,2,8,128]{3,2,1,0:T(8,128)S(1)} %get-tuple-element.164), channel_id=1, source_target_pairs={{0,8},{8,0},{24,16},{16,24},{17,25},{25,17},{9,1},{1,9},{2,10},{10... | collective-permute-start | bytes 294920 | tf_op jit(solution)/shard_map/ppermute | solution.py:556
  132.0 11.1 %collective-permute-start.43 = (f32[12,2,8,128]{3,2,1,0:T(8,128)S(1)}, f32[12,2,8,128]{3,2,1,0:T(8,128)S(1)}, u32[]{:S(2)}, u32[]{:S(2)}) collective-permute-start(f32[12,2,8,128]{3,2,1,0:T(8,128)S(1)} %get-tuple-element.165), channel_id=1, source_target_pairs={{8,24},{24,8},{16,17},{17,16},{25,9},{9,25},{1,2},{2,1},{10,26},{2... | collective-permute-start | bytes 294920 | tf_op jit(solution)/shard_map/ppermute | solution.py:557
  134.9 7.6 %collective-permute-start.40 = (f32[12,8,128]{2,1,0:T(8,128)S(1)}, f32[12,8,128]{2,1,0:T(8,128)S(1)}, u32[]{:S(2)}, u32[]{:S(2)}) collective-permute-start(f32[12,8,128]{2,1,0:T(8,128)S(1)} %get-tuple-element.162), channel_id=1, source_target_pairs={{0,32},{32,0},{64,96},{96,64},{128,160},{160,128},{192,224},{224,1... | collective-permute-start | bytes 147464 | tf_op jit(solution)/shard_map/ppermute | solution.py:554
  136.8 6.3 %collective-permute-start.41 = (f32[12,8,128]{2,1,0:T(8,128)S(1)}, f32[12,8,128]{2,1,0:T(8,128)S(1)}, u32[]{:S(2)}, u32[]{:S(2)}) collective-permute-start(f32[12,8,128]{2,1,0:T(8,128)S(1)} %get-tuple-element.163), channel_id=1, source_target_pairs={{32,64},{64,32},{96,128},{128,96},{160,192},{192,160},{224,256},{2... | collective-permute-start | bytes 147464 | tf_op jit(solution)/shard_map/ppermute | solution.py:555
  143.8 51.1 %collective-permute-start.46 = (f32[12,2,8,128]{3,2,1,0:T(8,128)S(1)}, f32[12,2,8,128]{3,2,1,0:T(8,128)S(1)}, u32[]{:S(2)}, u32[]{:S(2)}) collective-permute-start(f32[12,2,8,128]{3,2,1,0:T(8,128)S(1)} %get-tuple-element.169), channel_id=1, source_target_pairs={{0,8},{8,0},{24,16},{16,24},{17,25},{25,17},{9,1},{1,9},{2,10},{10... | collective-permute-start | bytes 294920 | tf_op jit(solution)/shard_map/ppermute | solution.py:556
  149.5 45.4 %collective-permute-start.47 = (f32[12,2,8,128]{3,2,1,0:T(8,128)S(1)}, f32[12,2,8,128]{3,2,1,0:T(8,128)S(1)}, u32[]{:S(2)}, u32[]{:S(2)}) collective-permute-start(f32[12,2,8,128]{3,2,1,0:T(8,128)S(1)} %get-tuple-element.170), channel_id=1, source_target_pairs={{8,24},{24,8},{16,17},{17,16},{25,9},{9,25},{1,2},{2,1},{10,26},{2... | collective-permute-start | bytes 294920 | tf_op jit(solution)/shard_map/ppermute | solution.py:557
  151.4 43.4 %collective-permute-start.44 = (f32[12,8,128]{2,1,0:T(8,128)S(1)}, f32[12,8,128]{2,1,0:T(8,128)S(1)}, u32[]{:S(2)}, u32[]{:S(2)}) collective-permute-start(f32[12,8,128]{2,1,0:T(8,128)S(1)} %get-tuple-element.167), channel_id=1, source_target_pairs={{0,32},{32,0},{64,96},{96,64},{128,160},{160,128},{192,224},{224,1... | collective-permute-start | bytes 147464 | tf_op jit(solution)/shard_map/ppermute | solution.py:554
  153.4 41.5 %collective-permute-start.45 = (f32[12,8,128]{2,1,0:T(8,128)S(1)}, f32[12,8,128]{2,1,0:T(8,128)S(1)}, u32[]{:S(2)}, u32[]{:S(2)}) collective-permute-start(f32[12,8,128]{2,1,0:T(8,128)S(1)} %get-tuple-element.168), channel_id=1, source_target_pairs={{32,64},{64,32},{96,128},{128,96},{160,192},{192,160},{224,256},{2... | collective-permute-start | bytes 147464 | tf_op jit(solution)/shard_map/ppermute | solution.py:555

commit v2 on v1

--- a/solution.py
+++ b/solution.py
@@ -21,20 +21,37 @@
 PIVOT_GUARD = 1e-3
 VMEM = pl.BlockSpec(memory_space=pltpu.VMEM)
 SMEM = pl.BlockSpec(memory_space=pltpu.SMEM)
-
-
-def call(body, outs, args, flops=10**6):
-    in_specs = [SMEM if a.dtype == jnp.int32 else VMEM for a in args]
+ANY = pl.BlockSpec(memory_space=pl.ANY)
+
+
+def call(body, outs, args, flops=10**6, after=(), scratch=(), flag=False):
+    count = len(args)
+
+    def without_after(*refs):
+        body(*refs[:count], *refs[count + len(after) :])
+
     shapes = [jax.ShapeDtypeStruct(s, F32) for s in outs]
+    out_specs = [VMEM] * len(shapes)
+    if flag:
+        shapes.append(jax.ShapeDtypeStruct((1,), jnp.int32))
+        out_specs.append(SMEM)
     moved = 4 * sum(a.size for a in args)
     return pl.pallas_call(
-        body,
+        without_after,
         out_shape=shapes,
-        in_specs=in_specs,
-        out_specs=[VMEM] * len(shapes),
-        compiler_params=pltpu.CompilerParams(vmem_limit_bytes=32 * 2**20),
+        in_specs=[VMEM] * count + [ANY] * len(after),
+        out_specs=out_specs,
+        scratch_shapes=scratch,
+        compiler_params=pltpu.CompilerParams(vmem_limit_bytes=16 * 2**20),
         cost_estimate=pl.CostEstimate(flops=flops, bytes_accessed=moved, transcendentals=0),
-    )(*args)
+    )(*args, *after)
+
+
+def place():
+    ta, gz, gy = (lax.axis_index(name) for name in ("ta", "gz", "gy"))
+    block_odd = gy % 2
+    row_odd = (gz + gz // 2 + block_odd) % 2
+    return ta % 2, row_odd, ta == lax.axis_size("ta") - 1, ta == 0, block_odd
 
 
 def lanes():
@@ -63,20 +80,21 @@
     return out
 
 
-def owner(info, row):
-    return jnp.where(info[4] == 1, ROW_OWNER[1][row], ROW_OWNER[0][row])
-
-
-def pack_body(info, sources, links, out):
+def owner(block_odd, row):
+    return jnp.where(block_odd == 1, ROW_OWNER[1][row], ROW_OWNER[0][row])
+
+
+def pack_body(sources, links, out):
+    block_odd = place()[4]
     for ref, base, chunks in ((sources, 0, 6), (links, 48, 9)):
         for z in range(2):
             for i in range(chunks):
                 tiles = [ref[s, pl.ds(16 * i + z, 8, stride=2), :] for s in range(4)]
                 for row, tile in enumerate(swap_groups(tiles)):
-                    out[owner(info, row), z, base + 8 * i : base + 8 * i + 8, :] = tile
-
-
-def unpack_body(info, received, links, spinor, *faces):
+                    out[owner(block_odd, row), z, base + 8 * i : base + 8 * i + 8, :] = tile
+
+
+def unpack_body(received, links, spinor, *faces):
     for c in range(24):
         for t in range(2):
             spinor[c, t] = received[pl.ds(2 * c + t, 8, stride=120), :]
@@ -90,7 +108,7 @@
                 turned = roll_lanes(pair, 32)
                 links[q * 36 + l, t] = jnp.where(even, pair, turned)
                 links[(q + 1) * 36 + l, t] = jnp.where(even, turned, pair)
-    write_faces(info, spinor, links, 1, faces)
+    write_faces(spinor, links, 1, faces)
 
 
 def load_spinor(ref, t):
@@ -164,9 +182,9 @@
     return [half[p][k][c] for p in range(2) for k in range(2) for c in range(3)]
 
 
-def write_faces(info, spinor, links, parity, faces):
+def write_faces(spinor, links, parity, faces):
     time_a, time_b, row_a, row_b = faces
-    time_odd, row_odd = info[0] == 1, info[1] == 1
+    time_odd, row_odd = (flag == 1 for flag in place()[:2])
     for t in range(2):
         v = load_spinor(spinor, t)
         down = halves(project(v, 1, -1))
@@ -183,9 +201,9 @@
         time_b[i] = jnp.where(time_odd, time_up[i], time_down[i])
 
 
-def inner_body(parity, with_moments, info, spinor, links, out, *moments):
+def inner_body(parity, with_moments, spinor, links, out, *moments):
     cell = lanes() % 32
-    site = sublanes() + info[1] + parity
+    site = sublanes() + place()[1] + parity
     vs = [load_spinor(spinor, t) for t in range(2)]
     for t in range(2):
         odd = (site + t) % 2 == 1
@@ -236,9 +254,10 @@
     return totals
 
 
-def add_received(info, acc, links, parity, t, recv):
+def add_received(acc, links, parity, t, recv):
     time_a, time_b, row_a, row_b = recv
-    time_odd, row_odd = info[0] == 1, info[1] == 1
+    time_odd, row_odd, last, first, _ = place()
+    time_odd, row_odd = time_odd == 1, row_odd == 1
 
     def pick(flag, first, second):
         flat = [jnp.where(flag, first[i], second[i]) for i in range(12)]
@@ -250,18 +269,18 @@
     rebuild_add(acc, half, 1, 1)
     a, b = [time_a[i] for i in range(12)], [time_b[i] for i in range(12)]
     if t == 1:
-        sign = jnp.where(info[2] == 1, -1.0, 1.0)
+        sign = jnp.where(last, -1.0, 1.0)
         half = map_half(lambda x: x * sign, pick(time_odd, b, a))
         rebuild_add(acc, color_times(links, parity, 3, t, half, False), 3, -1)
     else:
-        sign = jnp.where(info[3] == 1, -1.0, 1.0)
+        sign = jnp.where(first, -1.0, 1.0)
         half = map_half(lambda x: x * sign, pick(time_odd, a, b))
         rebuild_add(acc, half, 3, 1)
 
 
-def finished_spinor(info, partial, links, parity, t, recv, base):
+def finished_spinor(partial, links, parity, t, recv, base):
     acc = load_spinor(partial, t)
-    add_received(info, acc, links, parity, t, recv)
+    add_received(acc, links, parity, t, recv)
     if base is None:
         return acc
     old = load_spinor(base, t)
@@ -274,19 +293,19 @@
 
 
 def outer_body(parity, with_base, with_faces, *refs):
-    info, partial, links = refs[:3]
-    recv = refs[3:7]
-    base = refs[7] if with_base else None
-    out = refs[8] if with_base else refs[7]
+    partial, links = refs[:2]
+    recv = in_face_order(refs[2:6])
+    base = refs[6] if with_base else None
+    out = refs[7] if with_base else refs[6]
     faces = refs[-4:]
     for t in range(2):
-        acc = finished_spinor(info, partial, links, parity, t, recv, base)
+        acc = finished_spinor(partial, links, parity, t, recv, base)
         for p in range(2):
             for s in range(4):
                 for c in range(3):
                     out[(p * 4 + s) * 3 + c, t] = acc[p][s][c]
     if with_faces:
-        write_faces(info, out, links, 1 - parity, faces)
+        write_faces(out, links, 1 - parity, faces)
 
 
 def group_sum(x):
@@ -316,25 +335,21 @@
 
 
 def moments_call(spinor, given):
-    args = (spinor, *given)
-    return pl.pallas_call(
-        moments_body,
-        out_shape=jax.ShapeDtypeStruct((32, 128), F32),
-        in_specs=[VMEM] * len(args),
-        out_specs=VMEM,
-        scratch_shapes=[pltpu.VMEM((24, 128), F32)],
-        cost_estimate=pl.CostEstimate(flops=10**5, bytes_accessed=10**5, transcendentals=0),
-    )(*args)
+    scratch = [pltpu.VMEM((24, 128), F32)]
+    return call(moments_body, [(32, 128)], (spinor, *given), 10**5, scratch=scratch)[0]
 
 
 def row_sum_body(rows, out):
     out[...] = jnp.broadcast_to(jnp.sum(rows[...], axis=0, keepdims=True), out.shape)
 
 
+def reduce_rows(rows):
+    rows = lax.all_to_all(rows, ("gz", "gy"), 0, 0, tiled=True)
+    return call(row_sum_body, [(16, 128)], (rows,), 10**4)[0]
+
+
 def reduce_devices(rows):
-    rows = lax.all_to_all(rows, ("gz", "gy"), 0, 0, tiled=True)
-    (rows,) = call(row_sum_body, [(16, 128)], (rows,), 10**4)
-    return lax.all_to_all(rows, "ta", 0, 0, tiled=True)
+    return lax.all_to_all(reduce_rows(rows), "ta", 0, 0, tiled=True)
 
 
 def group_of_lane():
@@ -462,7 +477,7 @@
     write_coefficients(out, 0, k)
     write_coefficients(out, 8, q)
     good = good0 & good1 & good2 & good3
-    good_out[...] = jnp.where(good, 1.0, 0.0)
+    good_out[0] = jnp.min(jnp.where(good, 1, 0))
 
 
 def unit_pair(unit):
@@ -496,10 +511,11 @@
             out[12 + c, t] = signed_add(x[12 + c, t], im, sign)
 
 
-def final_body(info, partial, links, time_a, time_b, row_a, row_b, base, first, image, rows, out):
-    recv = (time_a, time_b, row_a, row_b)
+def final_body(partial, links, *refs):
+    recv = in_face_order(refs[:4])
+    base, first, image, rows, out = refs[4:]
     for t in range(2):
-        b = finished_spinor(info, partial, links, 0, t, recv, base)
+        b = finished_spinor(partial, links, 0, t, recv, base)
         for s in range(4):
             for c in range(3):
                 at = s * 3 + c
@@ -522,18 +538,28 @@
                 out[pl.ds(48 * i + 2 * c + t, 8, stride=96), :] = ref[c, t]
 
 
-def deliver_body(info, received, solution_ref, residual_ref):
+def deliver_body(received, solution_ref, residual_ref):
+    block_odd = place()[4]
     for i, ref in enumerate((solution_ref, residual_ref)):
         for z in range(2):
             for n in range(6):
                 at = 48 * i + 8 * n
-                tiles = [received[owner(info, row), z, at : at + 8, :] for row in range(4)]
+                tiles = [received[owner(block_odd, row), z, at : at + 8, :] for row in range(4)]
                 for s, tile in enumerate(swap_groups(tiles)):
                     ref[s, pl.ds(16 * n + z, 8, stride=2), :] = tile
 
 
 SPINOR = (24, 2, 8, 128)
-FACES = [(12, 8, 128), (12, 8, 128), (12, 2, 8, 128), (12, 2, 8, 128)]
+FACES = [(24, 8, 128), (24, 8, 128), (12, 2, 8, 128), (12, 2, 8, 128)]
+START_ORDER = (1, 3, 0, 2)
+
+
+def in_start_order(faces):
+    return [faces[i] for i in START_ORDER]
+
+
+def in_face_order(operands):
+    return [operands[START_ORDER.index(i)] for i in range(4)]
 
 
 def make_pairs(order, start):
@@ -558,43 +584,43 @@
     )
 
 
-def hop_inner(info, spinor, links, parity, with_moments=False):
+def hop_inner(spinor, links, parity, with_moments=False):
     outs = [SPINOR] + ([(5, 8, 128)] if with_moments else [])
 
     def body(*refs):
         inner_body(parity, with_moments, *refs)
 
-    return call(body, outs, (info, spinor, links), 8 * 10**6)
-
-
-def hop_outer(info, partial, links, recv, parity, base=None, with_faces=True):
-    args = (info, partial, links, *recv) + (() if base is None else (base,))
+    return call(body, outs, (spinor, links), 8 * 10**6)
+
+
+def hop_outer(partial, links, recv, parity, base=None, with_faces=True, after=()):
+    args = (partial, links, *in_start_order(recv)) + (() if base is None else (base,))
 
     def body(*refs):
         outer_body(parity, base is not None, with_faces, *refs)
 
-    outs = call(body, [SPINOR] + (FACES if with_faces else []), args, 4 * 10**6)
+    outs = call(body, [SPINOR] + (FACES if with_faces else []), args, 4 * 10**6, after)
     return outs[0], outs[1:]
 
 
-def half_normal(info, spinor, faces, links, with_moments=False, with_faces=True):
+def half_normal(spinor, faces, links, with_moments=False, with_faces=True):
     recv = exchange(faces)
-    partial, *moments = hop_inner(info, spinor, links, 1, with_moments)
-    odd, faces = hop_outer(info, partial, links, recv, 1)
+    partial, *moments = hop_inner(spinor, links, 1, with_moments)
+    odd, faces = hop_outer(partial, links, recv, 1)
     recv = exchange(faces)
-    (partial,) = hop_inner(info, odd, links, 0)
-    out, faces = hop_outer(info, partial, links, recv, 0, spinor, with_faces)
+    (partial,) = hop_inner(odd, links, 0)
+    out, faces = hop_outer(partial, links, recv, 0, spinor, with_faces)
     return out, faces, moments
 
 
-def faces_only(info, spinor, links):
-    def body(info, spinor, links, *faces):
-        write_faces(info, spinor, links, 1, faces)
-
-    return call(body, FACES, (info, spinor, links))
-
-
-def direct_branch(info, links, first, image, rows):
+def faces_only(spinor, links):
+    def body(spinor, links, *faces):
+        write_faces(spinor, links, 1, faces)
+
+    return call(body, FACES, (spinor, links))
+
+
+def direct_branch(links, first, image, rows):
     def solve_call(c_rows, e_rows, c_field, e_field):
         def body(*refs):
             solve_body((c_field, e_field), *refs)
@@ -612,10 +638,10 @@
     rho = reduce_devices(moments_call(residual, ()))
     beta = solve_call(rows, rho, 0, 0)
     search = combine(1, residual, first, beta)
-    faces = faces_only(info, search, links)
-    halfway, faces, _ = half_normal(info, search, faces, links)
+    faces = faces_only(search, links)
+    halfway, faces, _ = half_normal(search, faces, links)
     curvature = reduce_devices(moments_call(halfway, ()))
-    images, _, _ = half_normal(info, halfway, faces, links, with_faces=False)
+    images, _, _ = half_normal(halfway, faces, links, with_faces=False)
     alpha1 = solve_call(curvature, rho, 0, 0)
     zero = jnp.zeros(SPINOR, F32)
     solution_field = combine(1, combine(1, zero, first, alpha), search, alpha1)
@@ -624,42 +650,33 @@
 
 
 def local(sources, gauge_links):
-    ta, gz, gy = (lax.axis_index(name) for name in ("ta", "gz", "gy"))
-    odd_block = gy % 2
-    position = jnp.where(odd_block == 1, jnp.array([3, 2, 0, 1])[gz], jnp.array([0, 1, 3, 2])[gz])
-    info = jnp.stack(
-        [ta % 2, position % 2, ta == lax.axis_size("ta") - 1, ta == 0, odd_block]
-    ).astype(jnp.int32)
-
-    args = (info, sources.reshape(4, 96, 128), gauge_links.reshape(4, 144, 128))
+    args = (sources.reshape(4, 96, 128), gauge_links.reshape(4, 144, 128))
     (packed,) = call(pack_body, [(4, 2, 120, 128)], args)
     received = lax.all_to_all(packed, "gz", 0, 0).reshape(960, 128)
-    links, first, *faces = call(
-        unpack_body, [(144, 2, 8, 128), SPINOR] + FACES, (info, received)
-    )
-    half1, faces, moments0 = half_normal(info, first, faces, links, True)
-    image, faces, moments1 = half_normal(info, half1, faces, links, True)
-    half2, faces, moments2 = half_normal(info, image, faces, links, True)
-    rows = reduce_devices(moments_call(half2, (*moments0, *moments1, *moments2)))
-    table, good = call(coefficients_body, [(16, 128), TILE], (rows,), 10**5)
-
+    links, first, *faces = call(unpack_body, [(144, 2, 8, 128), SPINOR] + FACES, (received,))
+    half1, faces, moments0 = half_normal(first, faces, links, True)
+    image, faces, moments1 = half_normal(half1, faces, links, True)
+    half2, faces, moments2 = half_normal(image, faces, links, True)
+
+    rows = moments_call(half2, (*moments0, *moments1, *moments2))
     recv = exchange(faces)
-    (partial,) = hop_inner(info, half2, links, 1)
-    odd, faces = hop_outer(info, partial, links, recv, 1)
+    (partial,) = hop_inner(half2, links, 1)
+    rows = reduce_rows(rows)
+    odd, faces = hop_outer(partial, links, recv, 1, after=(rows,))
+    rows = lax.all_to_all(rows, "ta", 0, 0, tiled=True)
     recv = exchange(faces)
-    (partial,) = hop_inner(info, odd, links, 0)
+    (partial,) = hop_inner(odd, links, 0)
+    table, good = call(coefficients_body, [(16, 128)], (rows,), 10**5, flag=True)
 
     def moment_branch():
-        given = (info, partial, links, *recv, half2, first, image, table)
+        given = (partial, links, *in_start_order(recv), half2, first, image, table)
         return call(final_body, [(768, 128)], given, 10**7)[0]
 
     out = lax.cond(
-        good[0, 0] > 0.5,
-        moment_branch,
-        lambda: direct_branch(info, links, first, image, rows),
+        good[0] == 1, moment_branch, lambda: direct_branch(links, first, image, rows)
     )
     received = lax.all_to_all(out.reshape(4, 2, 96, 128), "gz", 0, 0)
-    done = call(deliver_body, [(4, 96, 128)] * 2, (info, received))
+    done = call(deliver_body, [(4, 96, 128)] * 2, (received,))
     return tuple(x.reshape(sources.shape) for x in done)
 
 

time: 212 us -> 188 us (0.89)
  blocking collectives: 61.6 us -> 48.5 us
  Pallas kernels: 23.5 us -> 12.8 us
  waiting for transfers between devices: 4.13 us -> 10.1 us
  local copies, waits for them, and re-layouts: 5.02 us -> 1.88 us
    all_to_all x2 -> x1, blocking collectives: 30.9 us -> 18.4 us  [local(): rows = lax.all_to_all(rows, 'ta', 0, 0, tiled=True)]
    pallas_call x22, Pallas kernels: 23.5 us -> 12.8 us  [call(): pl.pallas_call(without_after, out_shape=shapes, in_specs=[VMEM] * count +...]
    ppermute x8, starting transfers between devices: 42 us -> 34.9 us  [exchange(): lax.ppermute(time_b, 'ta', make_pairs(times, 1))]
    all_to_all x0 -> x1, waiting for transfers between devices: none -> 6.56 us  [reduce_rows(): rows = lax.all_to_all(rows, ('gz', 'gy'), 0, 0, tiled=True)]
    ppermute x8, waiting for transfers between devices: 4.06 us -> 0.02 us  [exchange(): lax.ppermute(time_b, 'ta', make_pairs(times, 1))]
    all_to_all x0 -> x1, starting transfers between devices: none -> 3.62 us  [reduce_rows(): rows = lax.all_to_all(rows, ('gz', 'gy'), 0, 0, tiled=True)]
    ppermute x8, waiting for transfers between devices: 0.02 us -> 3.51 us  [exchange(): lax.ppermute(row_a, ('gz', 'gy'), make_pairs(rows, 0))]
    dynamic_slice x2 -> x0, local copies, waits for them, and re-layouts: 2.52 us -> none  [the longest x1 1.28 us: local(): jnp.array([0, 1, 3, 2])[gz]]
  transfers between devices with their start and end apart: 32 -> 33, of which waited for: 7 -> 7; matrix products, arithmetic and copies ran while one was open for 0% -> 0% of each run, Pallas kernels for 5% -> 3%
where the time goes in v2:
time: 188 us; the launch traced here: 187 us
  starting transfers between devices  111 us (59%)
  blocking collectives  48.5 us (26%)
  Pallas kernels  12.8 us (7%)
  waiting for transfers between devices  10.1 us (5%)
    ppermute x8, starting transfers between devices, exchange(): lax.ppermute(row_a, ('gz', 'gy'), make_pairs(rows, 0))  35.5 us
    ppermute x8, starting transfers between devices, exchange(): lax.ppermute(time_b, 'ta', make_pairs(times, 1))  34.9 us
    ppermute x8, starting transfers between devices, exchange(): lax.ppermute(row_b, ('gz', 'gy'), make_pairs(rows, 1))  20.7 us
    all_to_all x1, blocking collectives, local(): rows = lax.all_to_all(rows, 'ta', 0, 0, tiled=True)  18.4 us
    all_to_all x1, blocking collectives, local(): received = lax.all_to_all(packed, 'gz', 0, 0).reshape(960, 128)  18.3 us
    ppermute x8, starting transfers between devices, exchange(): lax.ppermute(time_a, 'ta', make_pairs(times, 0))  16.6 us
    pallas_call x22, Pallas kernels, call(): pl.pallas_call(without_after, out_shape=shapes, in_specs=[VMEM] * count +...  12.8 us
    all_to_all x1, blocking collectives, local(): received = lax.all_to_all(out.reshape(4, 2, 96, 128), 'gz', 0, 0)  11.8 us
  transfers between devices with their start and end apart: 33, of which 7 were waited for; matrix products, arithmetic and copies ran while one was open for 0% of the time, Pallas kernels for 3%

profile of v2, /device:TPU:1, one launch (start us, length us, event | category | flops | bytes accessed | tf_op | source)
XLA Modules:
  0.0 186.6 jit_solution(3231700203462079338)
XLA Ops:
  0.6 1.0 copy-done
  1.6 0.9 copy-done.1
  2.5 1.3 shard_map.41
  3.8 18.3 %all_to_all.67 = f32[4,2,120,128]{3,2,1,0:T(8,128)S(1)} all-to-all(f32[4,2,120,128]{3,2,1,0:T(8,128)S(1)} %shard_map.41), channel_id=1, replica_groups=mesh['ta'=16,'gz'=4,'gy'=8] {'gz'}, dimensions={0} | all-to-all | bytes 983040 | tf_op jit(solution)/shard_map/all_to_all | solution.py:655
  22.1 2.0 %shard_map.42 = (f32[144,2,8,128]{3,2,1,0:T(8,128)S(1)}, f32[24,2,8,128]{3,2,1,0:T(8,128)S(1)}, f32[24,8,128]{2,1,0:T(8,128)S(1)}, f32[24,8,128]{2,1,0:T(8,128)S...) custom-call(f32[960,128]{1,0:T(8,128)S(1)} %bitcast.31), custom_call_target="tpu_custom_call" | custom-call | flops 1000000 | bytes 491520 | tf_op jit(solution)/shard_map/pallas_call | solution.py:39
  24.2 7.5 %collective-permute-start.16 = (f32[24,8,128]{2,1,0:T(8,128)S(1)}, f32[24,8,128]{2,1,0:T(8,128)S(1)}, u32[]{:S(2)}, u32[]{:S(2)}) collective-permute-start(f32[24,8,128]{2,1,0:T(8,128)S(1)} %get-tuple-element.120), channel_id=1, source_target_pairs={{32,64},{64,32},{96,128},{128,96},{160,192},{192,160},{224,256},{2... | collective-permute-start | bytes 294920 | tf_op jit(solution)/shard_map/ppermute | solution.py:581
  31.7 2.4 %collective-permute-start.17 = (f32[12,2,8,128]{3,2,1,0:T(8,128)S(1)}, f32[12,2,8,128]{3,2,1,0:T(8,128)S(1)}, u32[]{:S(2)}, u32[]{:S(2)}) collective-permute-start(f32[12,2,8,128]{3,2,1,0:T(8,128)S(1)} %get-tuple-element.121), channel_id=1, source_target_pairs={{8,24},{24,8},{16,17},{17,16},{25,9},{9,25},{1,2},{2,1},{10,26},{2... | collective-permute-start | bytes 294920 | tf_op jit(solution)/shard_map/ppermute | solution.py:583
  34.0 1.9 %collective-permute-start.18 = (f32[24,8,128]{2,1,0:T(8,128)S(1)}, f32[24,8,128]{2,1,0:T(8,128)S(1)}, u32[]{:S(2)}, u32[]{:S(2)}) collective-permute-start(f32[24,8,128]{2,1,0:T(8,128)S(1)} %get-tuple-element.122), channel_id=1, source_target_pairs={{0,32},{32,0},{64,96},{96,64},{128,160},{160,128},{192,224},{224,1... | collective-permute-start | bytes 294920 | tf_op jit(solution)/shard_map/ppermute | solution.py:580
  36.0 5.7 %collective-permute-start.19 = (f32[12,2,8,128]{3,2,1,0:T(8,128)S(1)}, f32[12,2,8,128]{3,2,1,0:T(8,128)S(1)}, u32[]{:S(2)}, u32[]{:S(2)}) collective-permute-start(f32[12,2,8,128]{3,2,1,0:T(8,128)S(1)} %get-tuple-element.123), channel_id=1, source_target_pairs={{0,8},{8,0},{24,16},{16,24},{17,25},{25,17},{9,1},{1,9},{2,10},{10... | collective-permute-start | bytes 294920 | tf_op jit(solution)/shard_map/ppermute | solution.py:582
  41.7 0.3 shard_map.43
  42.1 0.5 collective-permute-done.19.refs_5_
  42.8 3.6 %collective-permute-start.20 = (f32[24,8,128]{2,1,0:T(8,128)S(1)}, f32[24,8,128]{2,1,0:T(8,128)S(1)}, u32[]{:S(2)}, u32[]{:S(2)}) collective-permute-start(f32[24,8,128]{2,1,0:T(8,128)S(1)} %get-tuple-element.125), channel_id=1, source_target_pairs={{32,64},{64,32},{96,128},{128,96},{160,192},{192,160},{224,256},{2... | collective-permute-start | bytes 294920 | tf_op jit(solution)/shard_map/ppermute | solution.py:581
  46.5 1.9 %collective-permute-start.21 = (f32[12,2,8,128]{3,2,1,0:T(8,128)S(1)}, f32[12,2,8,128]{3,2,1,0:T(8,128)S(1)}, u32[]{:S(2)}, u32[]{:S(2)}) collective-permute-start(f32[12,2,8,128]{3,2,1,0:T(8,128)S(1)} %get-tuple-element.126), channel_id=1, source_target_pairs={{8,24},{24,8},{16,17},{17,16},{25,9},{9,25},{1,2},{2,1},{10,26},{2... | collective-permute-start | bytes 294920 | tf_op jit(solution)/shard_map/ppermute | solution.py:583
  48.4 1.9 %collective-permute-start.22 = (f32[24,8,128]{2,1,0:T(8,128)S(1)}, f32[24,8,128]{2,1,0:T(8,128)S(1)}, u32[]{:S(2)}, u32[]{:S(2)}) collective-permute-start(f32[24,8,128]{2,1,0:T(8,128)S(1)} %get-tuple-element.127), channel_id=1, source_target_pairs={{0,32},{32,0},{64,96},{96,64},{128,160},{160,128},{192,224},{224,1... | collective-permute-start | bytes 294920 | tf_op jit(solution)/shard_map/ppermute | solution.py:580
  50.3 3.6 %collective-permute-start.23 = (f32[12,2,8,128]{3,2,1,0:T(8,128)S(1)}, f32[12,2,8,128]{3,2,1,0:T(8,128)S(1)}, u32[]{:S(2)}, u32[]{:S(2)}) collective-permute-start(f32[12,2,8,128]{3,2,1,0:T(8,128)S(1)} %get-tuple-element.128), channel_id=1, source_target_pairs={{0,8},{8,0},{24,16},{16,24},{17,25},{25,17},{9,1},{1,9},{2,10},{10... | collective-permute-start | bytes 294920 | tf_op jit(solution)/shard_map/ppermute | solution.py:582
  54.0 0.3 shard_map.45.refs_0_
  54.3 0.6 collective-permute-done.23.refs_5_
  54.9 0.2 shard_map.46
  55.1 4.8 %collective-permute-start.24 = (f32[24,8,128]{2,1,0:T(8,128)S(1)}, f32[24,8,128]{2,1,0:T(8,128)S(1)}, u32[]{:S(2)}, u32[]{:S(2)}) collective-permute-start(f32[24,8,128]{2,1,0:T(8,128)S(1)} %get-tuple-element.131), channel_id=1, source_target_pairs={{32,64},{64,32},{96,128},{128,96},{160,192},{192,160},{224,256},{2... | collective-permute-start | bytes 294920 | tf_op jit(solution)/shard_map/ppermute | solution.py:581
  59.9 3.2 %collective-permute-start.25 = (f32[12,2,8,128]{3,2,1,0:T(8,128)S(1)}, f32[12,2,8,128]{3,2,1,0:T(8,128)S(1)}, u32[]{:S(2)}, u32[]{:S(2)}) collective-permute-start(f32[12,2,8,128]{3,2,1,0:T(8,128)S(1)} %get-tuple-element.132), channel_id=1, source_target_pairs={{8,24},{24,8},{16,17},{17,16},{25,9},{9,25},{1,2},{2,1},{10,26},{2... | collective-permute-start | bytes 294920 | tf_op jit(solution)/shard_map/ppermute | solution.py:583
  63.2 1.9 %collective-permute-start.26 = (f32[24,8,128]{2,1,0:T(8,128)S(1)}, f32[24,8,128]{2,1,0:T(8,128)S(1)}, u32[]{:S(2)}, u32[]{:S(2)}) collective-permute-start(f32[24,8,128]{2,1,0:T(8,128)S(1)} %get-tuple-element.133), channel_id=1, source_target_pairs={{0,32},{32,0},{64,96},{96,64},{128,160},{160,128},{192,224},{224,1... | collective-permute-start | bytes 294920 | tf_op jit(solution)/shard_map/ppermute | solution.py:580
  65.1 5.1 %collective-permute-start.27 = (f32[12,2,8,128]{3,2,1,0:T(8,128)S(1)}, f32[12,2,8,128]{3,2,1,0:T(8,128)S(1)}, u32[]{:S(2)}, u32[]{:S(2)}) collective-permute-start(f32[12,2,8,128]{3,2,1,0:T(8,128)S(1)} %get-tuple-element.134), channel_id=1, source_target_pairs={{0,8},{8,0},{24,16},{16,24},{17,25},{25,17},{9,1},{1,9},{2,10},{10... | collective-permute-start | bytes 294920 | tf_op jit(solution)/shard_map/ppermute | solution.py:582
  70.2 0.3 shard_map.47
  70.6 0.5 collective-permute-done.27.refs_5_
  71.3 3.2 %collective-permute-start.28 = (f32[24,8,128]{2,1,0:T(8,128)S(1)}, f32[24,8,128]{2,1,0:T(8,128)S(1)}, u32[]{:S(2)}, u32[]{:S(2)}) collective-permute-start(f32[24,8,128]{2,1,0:T(8,128)S(1)} %get-tuple-element.136), channel_id=1, source_target_pairs={{32,64},{64,32},{96,128},{128,96},{160,192},{192,160},{224,256},{2... | collective-permute-start | bytes 294920 | tf_op jit(solution)/shard_map/ppermute | solution.py:581
  74.6 1.9 %collective-permute-start.29 = (f32[12,2,8,128]{3,2,1,0:T(8,128)S(1)}, f32[12,2,8,128]{3,2,1,0:T(8,128)S(1)}, u32[]{:S(2)}, u32[]{:S(2)}) collective-permute-start(f32[12,2,8,128]{3,2,1,0:T(8,128)S(1)} %get-tuple-element.137), channel_id=1, source_target_pairs={{8,24},{24,8},{16,17},{17,16},{25,9},{9,25},{1,2},{2,1},{10,26},{2... | collective-permute-start | bytes 294920 | tf_op jit(solution)/shard_map/ppermute | solution.py:583
  76.5 2.3 %collective-permute-start.30 = (f32[24,8,128]{2,1,0:T(8,128)S(1)}, f32[24,8,128]{2,1,0:T(8,128)S(1)}, u32[]{:S(2)}, u32[]{:S(2)}) collective-permute-start(f32[24,8,128]{2,1,0:T(8,128)S(1)} %get-tuple-element.138), channel_id=1, source_target_pairs={{0,32},{32,0},{64,96},{96,64},{128,160},{160,128},{192,224},{224,1... | collective-permute-start | bytes 294920 | tf_op jit(solution)/shard_map/ppermute | solution.py:580
  78.8 3.8 %collective-permute-start.31 = (f32[12,2,8,128]{3,2,1,0:T(8,128)S(1)}, f32[12,2,8,128]{3,2,1,0:T(8,128)S(1)}, u32[]{:S(2)}, u32[]{:S(2)}) collective-permute-start(f32[12,2,8,128]{3,2,1,0:T(8,128)S(1)} %get-tuple-element.139), channel_id=1, source_target_pairs={{0,8},{8,0},{24,16},{16,24},{17,25},{25,17},{9,1},{1,9},{2,10},{10... | collective-permute-start | bytes 294920 | tf_op jit(solution)/shard_map/ppermute | solution.py:582
  82.6 0.3 shard_map.49.refs_0_
  82.9 0.6 collective-permute-done.31.refs_5_
  83.6 0.2 shard_map.50
  83.8 4.6 %collective-permute-start.32 = (f32[24,8,128]{2,1,0:T(8,128)S(1)}, f32[24,8,128]{2,1,0:T(8,128)S(1)}, u32[]{:S(2)}, u32[]{:S(2)}) collective-permute-start(f32[24,8,128]{2,1,0:T(8,128)S(1)} %get-tuple-element.142), channel_id=1, source_target_pairs={{32,64},{64,32},{96,128},{128,96},{160,192},{192,160},{224,256},{2... | collective-permute-start | bytes 294920 | tf_op jit(solution)/shard_map/ppermute | solution.py:581
  88.4 3.2 %collective-permute-start.33 = (f32[12,2,8,128]{3,2,1,0:T(8,128)S(1)}, f32[12,2,8,128]{3,2,1,0:T(8,128)S(1)}, u32[]{:S(2)}, u32[]{:S(2)}) collective-permute-start(f32[12,2,8,128]{3,2,1,0:T(8,128)S(1)} %get-tuple-element.143), channel_id=1, source_target_pairs={{8,24},{24,8},{16,17},{17,16},{25,9},{9,25},{1,2},{2,1},{10,26},{2... | collective-permute-start | bytes 294920 | tf_op jit(solution)/shard_map/ppermute | solution.py:583
  91.7 1.9 %collective-permute-start.34 = (f32[24,8,128]{2,1,0:T(8,128)S(1)}, f32[24,8,128]{2,1,0:T(8,128)S(1)}, u32[]{:S(2)}, u32[]{:S(2)}) collective-permute-start(f32[24,8,128]{2,1,0:T(8,128)S(1)} %get-tuple-element.144), channel_id=1, source_target_pairs={{0,32},{32,0},{64,96},{96,64},{128,160},{160,128},{192,224},{224,1... | collective-permute-start | bytes 294920 | tf_op jit(solution)/shard_map/ppermute | solution.py:580
  93.6 5.1 %collective-permute-start.35 = (f32[12,2,8,128]{3,2,1,0:T(8,128)S(1)}, f32[12,2,8,128]{3,2,1,0:T(8,128)S(1)}, u32[]{:S(2)}, u32[]{:S(2)}) collective-permute-start(f32[12,2,8,128]{3,2,1,0:T(8,128)S(1)} %get-tuple-element.145), channel_id=1, source_target_pairs={{0,8},{8,0},{24,16},{16,24},{17,25},{25,17},{9,1},{1,9},{2,10},{10... | collective-permute-start | bytes 294920 | tf_op jit(solution)/shard_map/ppermute | solution.py:582
  98.7 0.3 shard_map.51
  99.0 0.5 collective-permute-done.35.refs_5_
  99.8 3.2 %collective-permute-start.36 = (f32[24,8,128]{2,1,0:T(8,128)S(1)}, f32[24,8,128]{2,1,0:T(8,128)S(1)}, u32[]{:S(2)}, u32[]{:S(2)}) collective-permute-start(f32[24,8,128]{2,1,0:T(8,128)S(1)} %get-tuple-element.147), channel_id=1, source_target_pairs={{32,64},{64,32},{96,128},{128,96},{160,192},{192,160},{224,256},{2... | collective-permute-start | bytes 294920 | tf_op jit(solution)/shard_map/ppermute | solution.py:581
  103.0 1.9 %collective-permute-start.37 = (f32[12,2,8,128]{3,2,1,0:T(8,128)S(1)}, f32[12,2,8,128]{3,2,1,0:T(8,128)S(1)}, u32[]{:S(2)}, u32[]{:S(2)}) collective-permute-start(f32[12,2,8,128]{3,2,1,0:T(8,128)S(1)} %get-tuple-element.148), channel_id=1, source_target_pairs={{8,24},{24,8},{16,17},{17,16},{25,9},{9,25},{1,2},{2,1},{10,26},{2... | collective-permute-start | bytes 294920 | tf_op jit(solution)/shard_map/ppermute | solution.py:583
  105.0 2.3 %collective-permute-start.38 = (f32[24,8,128]{2,1,0:T(8,128)S(1)}, f32[24,8,128]{2,1,0:T(8,128)S(1)}, u32[]{:S(2)}, u32[]{:S(2)}) collective-permute-start(f32[24,8,128]{2,1,0:T(8,128)S(1)} %get-tuple-element.149), channel_id=1, source_target_pairs={{0,32},{32,0},{64,96},{96,64},{128,160},{160,128},{192,224},{224,1... | collective-permute-start | bytes 294920 | tf_op jit(solution)/shard_map/ppermute | solution.py:580
  107.3 3.8 %collective-permute-start.39 = (f32[12,2,8,128]{3,2,1,0:T(8,128)S(1)}, f32[12,2,8,128]{3,2,1,0:T(8,128)S(1)}, u32[]{:S(2)}, u32[]{:S(2)}) collective-permute-start(f32[12,2,8,128]{3,2,1,0:T(8,128)S(1)} %get-tuple-element.150), channel_id=1, source_target_pairs={{0,8},{8,0},{24,16},{16,24},{17,25},{25,17},{9,1},{1,9},{2,10},{10... | collective-permute-start | bytes 294920 | tf_op jit(solution)/shard_map/ppermute | solution.py:582
  111.1 0.3 shard_map.53.refs_0_
  111.4 0.6 collective-permute-done.39.refs_5_
  112.0 0.2 shard_map.54
  112.3 4.6 %collective-permute-start.40 = (f32[24,8,128]{2,1,0:T(8,128)S(1)}, f32[24,8,128]{2,1,0:T(8,128)S(1)}, u32[]{:S(2)}, u32[]{:S(2)}) collective-permute-start(f32[24,8,128]{2,1,0:T(8,128)S(1)} %get-tuple-element.156), channel_id=1, source_target_pairs={{32,64},{64,32},{96,128},{128,96},{160,192},{192,160},{224,256},{2... | collective-permute-start | bytes 294920 | tf_op jit(solution)/shard_map/ppermute | solution.py:581
  116.9 3.2 %collective-permute-start.41 = (f32[12,2,8,128]{3,2,1,0:T(8,128)S(1)}, f32[12,2,8,128]{3,2,1,0:T(8,128)S(1)}, u32[]{:S(2)}, u32[]{:S(2)}) collective-permute-start(f32[12,2,8,128]{3,2,1,0:T(8,128)S(1)} %get-tuple-element.157), channel_id=1, source_target_pairs={{8,24},{24,8},{16,17},{17,16},{25,9},{9,25},{1,2},{2,1},{10,26},{2... | collective-permute-start | bytes 294920 | tf_op jit(solution)/shard_map/ppermute | solution.py:583
  120.1 1.9 %collective-permute-start.42 = (f32[24,8,128]{2,1,0:T(8,128)S(1)}, f32[24,8,128]{2,1,0:T(8,128)S(1)}, u32[]{:S(2)}, u32[]{:S(2)}) collective-permute-start(f32[24,8,128]{2,1,0:T(8,128)S(1)} %get-tuple-element.158), channel_id=1, source_target_pairs={{0,32},{32,0},{64,96},{96,64},{128,160},{160,128},{192,224},{224,1... | collective-permute-start | bytes 294920 | tf_op jit(solution)/shard_map/ppermute | solution.py:580
  122.1 5.1 %collective-permute-start.43 = (f32[12,2,8,128]{3,2,1,0:T(8,128)S(1)}, f32[12,2,8,128]{3,2,1,0:T(8,128)S(1)}, u32[]{:S(2)}, u32[]{:S(2)}) collective-permute-start(f32[12,2,8,128]{3,2,1,0:T(8,128)S(1)} %get-tuple-element.159), channel_id=1, source_target_pairs={{0,8},{8,0},{24,16},{16,24},{17,25},{25,17},{9,1},{1,9},{2,10},{10... | collective-permute-start | bytes 294920 | tf_op jit(solution)/shard_map/ppermute | solution.py:582
  127.2 1.1 shard_map.55
  128.3 3.6 %all-to-all-start.5 = ((f32[32,1,128]{2,1,0:T(1,128)}), f32[32,1,128]{2,1,0:T(1,128)S(1)}, u32[]{:S(2)}, u32[]{:S(2)}) async-start(f32[32,1,128]{2,1,0:T(1,128)} %bitcast.20), calls=%async_computation.5 | async-start | bytes 32768 | tf_op jit(solution)/shard_map/all_to_all | solution.py:347
  131.9 0.3 shard_map.58.refs_0_
  132.2 6.6 %all-to-all-done.5 = f32[32,1,128]{2,1,0:T(1,128)S(1)} async-done(((f32[32,1,128]{2,1,0:T(1,128)}), f32[32,1,128]{2,1,0:T(1,128)S(1)}, u32[]{:S(2)}, u32[]{:S(2)}) %all-to-all-start.5) | async-done | bytes 16416 | tf_op jit(solution)/shard_map/all_to_all | solution.py:347
  138.8 0.2 shard_map.59
  139.0 3.2 %collective-permute-start.44 = (f32[24,8,128]{2,1,0:T(8,128)S(1)}, f32[24,8,128]{2,1,0:T(8,128)S(1)}, u32[]{:S(2)}, u32[]{:S(2)}) collective-permute-start(f32[24,8,128]{2,1,0:T(8,128)S(1)} %get-tuple-element.161), channel_id=1, source_target_pairs={{32,64},{64,32},{96,128},{128,96},{160,192},{192,160},{224,256},{2... | collective-permute-start | bytes 294920 | tf_op jit(solution)/shard_map/ppermute | solution.py:581
  142.3 2.9 %collective-permute-start.45 = (f32[12,2,8,128]{3,2,1,0:T(8,128)S(1)}, f32[12,2,8,128]{3,2,1,0:T(8,128)S(1)}, u32[]{:S(2)}, u32[]{:S(2)}) collective-permute-start(f32[12,2,8,128]{3,2,1,0:T(8,128)S(1)} %get-tuple-element.162), channel_id=1, source_target_pairs={{8,24},{24,8},{16,17},{17,16},{25,9},{9,25},{1,2},{2,1},{10,26},{2... | collective-permute-start | bytes 294920 | tf_op jit(solution)/shard_map/ppermute | solution.py:583
  145.1 2.3 %collective-permute-start.46 = (f32[24,8,128]{2,1,0:T(8,128)S(1)}, f32[24,8,128]{2,1,0:T(8,128)S(1)}, u32[]{:S(2)}, u32[]{:S(2)}) collective-permute-start(f32[24,8,128]{2,1,0:T(8,128)S(1)} %get-tuple-element.163), channel_id=1, source_target_pairs={{0,32},{32,0},{64,96},{96,64},{128,160},{160,128},{192,224},{224,1... | collective-permute-start | bytes 294920 | tf_op jit(solution)/shard_map/ppermute | solution.py:580
  147.5 3.3 %collective-permute-start.47 = (f32[12,2,8,128]{3,2,1,0:T(8,128)S(1)}, f32[12,2,8,128]{3,2,1,0:T(8,128)S(1)}, u32[]{:S(2)}, u32[]{:S(2)}) collective-permute-start(f32[12,2,8,128]{3,2,1,0:T(8,128)S(1)} %get-tuple-element.164), channel_id=1, source_target_pairs={{0,8},{8,0},{24,16},{16,24},{17,25},{25,17},{9,1},{1,9},{2,10},{10... | collective-permute-start | bytes 294920 | tf_op jit(solution)/shard_map/ppermute | solution.py:582
  150.7 18.4 %all_to_all.68 = f32[16,1,128]{2,1,0:T(1,128)S(1)} all-to-all(f32[16,1,128]{2,1,0:T(1,128)S(1)} %bitcast.34), channel_id=1, replica_groups=mesh['ta'=16,'gz'=4,'gy'=8] {'ta'}, dimensions={0} | all-to-all | bytes 16384 | tf_op jit(solution)/shard_map/all_to_all | solution.py:666
  169.1 2.4 %shard_map.57 = (f32[16,128]{1,0:T(8,128)S(1)}, s32[1]{0:T(128)}) custom-call(f32[16,128]{1,0:T(8,128)S(1)} %bitcast.45), custom_call_target="tpu_custom_call" | custom-call | flops 100000 | bytes 8192 | tf_op jit(solution)/shard_map/pallas_call | solution.py:39
  172.2 0.3 shard_map.60
  172.5 0.9 conditional.1
  172.8 0.7 branch_1_fun.1
  173.5 11.8 %all_to_all.69.refs_0_ = f32[4,2,96,128]{3,2,1,0:T(8,128)S(1)} all-to-all(f32[4,2,96,128]{3,2,1,0:T(8,128)S(1)} %bitcast.44), channel_id=1, replica_groups=mesh['ta'=16,'gz'=4,'gy'=8] {'gz'}, dimensions={0} | all-to-all | bytes 786432 | tf_op jit(solution)/shard_map/all_to_all | solution.py:678
  185.2 1.4 shard_map.61
  (32 shorter events, 0.7 us)
Async XLA Ops:
  0.6 1.0 copy-start
  1.6 0.9 copy-start.1
  24.2 17.8 %collective-permute-start.16 = (f32[24,8,128]{2,1,0:T(8,128)S(1)}, f32[24,8,128]{2,1,0:T(8,128)S(1)}, u32[]{:S(2)}, u32[]{:S(2)}) collective-permute-start(f32[24,8,128]{2,1,0:T(8,128)S(1)} %get-tuple-element.120), channel_id=1, source_target_pairs={{32,64},{64,32},{96,128},{128,96},{160,192},{192,160},{224,256},{2... | collective-permute-start | bytes 294920 | tf_op jit(solution)/shard_map/ppermute | solution.py:581
  31.7 10.4 %collective-permute-start.17 = (f32[12,2,8,128]{3,2,1,0:T(8,128)S(1)}, f32[12,2,8,128]{3,2,1,0:T(8,128)S(1)}, u32[]{:S(2)}, u32[]{:S(2)}) collective-permute-start(f32[12,2,8,128]{3,2,1,0:T(8,128)S(1)} %get-tuple-element.121), channel_id=1, source_target_pairs={{8,24},{24,8},{16,17},{17,16},{25,9},{9,25},{1,2},{2,1},{10,26},{2... | collective-permute-start | bytes 294920 | tf_op jit(solution)/shard_map/ppermute | solution.py:583
  34.0 8.0 %collective-permute-start.18 = (f32[24,8,128]{2,1,0:T(8,128)S(1)}, f32[24,8,128]{2,1,0:T(8,128)S(1)}, u32[]{:S(2)}, u32[]{:S(2)}) collective-permute-start(f32[24,8,128]{2,1,0:T(8,128)S(1)} %get-tuple-element.122), channel_id=1, source_target_pairs={{0,32},{32,0},{64,96},{96,64},{128,160},{160,128},{192,224},{224,1... | collective-permute-start | bytes 294920 | tf_op jit(solution)/shard_map/ppermute | solution.py:580
  36.0 6.7 %collective-permute-start.19 = (f32[12,2,8,128]{3,2,1,0:T(8,128)S(1)}, f32[12,2,8,128]{3,2,1,0:T(8,128)S(1)}, u32[]{:S(2)}, u32[]{:S(2)}) collective-permute-start(f32[12,2,8,128]{3,2,1,0:T(8,128)S(1)} %get-tuple-element.123), channel_id=1, source_target_pairs={{0,8},{8,0},{24,16},{16,24},{17,25},{25,17},{9,1},{1,9},{2,10},{10... | collective-permute-start | bytes 294920 | tf_op jit(solution)/shard_map/ppermute | solution.py:582
  42.8 11.4 %collective-permute-start.20 = (f32[24,8,128]{2,1,0:T(8,128)S(1)}, f32[24,8,128]{2,1,0:T(8,128)S(1)}, u32[]{:S(2)}, u32[]{:S(2)}) collective-permute-start(f32[24,8,128]{2,1,0:T(8,128)S(1)} %get-tuple-element.125), channel_id=1, source_target_pairs={{32,64},{64,32},{96,128},{128,96},{160,192},{192,160},{224,256},{2... | collective-permute-start | bytes 294920 | tf_op jit(solution)/shard_map/ppermute | solution.py:581
  46.5 7.8 %collective-permute-start.21 = (f32[12,2,8,128]{3,2,1,0:T(8,128)S(1)}, f32[12,2,8,128]{3,2,1,0:T(8,128)S(1)}, u32[]{:S(2)}, u32[]{:S(2)}) collective-permute-start(f32[12,2,8,128]{3,2,1,0:T(8,128)S(1)} %get-tuple-element.126), channel_id=1, source_target_pairs={{8,24},{24,8},{16,17},{17,16},{25,9},{9,25},{1,2},{2,1},{10,26},{2... | collective-permute-start | bytes 294920 | tf_op jit(solution)/shard_map/ppermute | solution.py:583
  48.4 5.9 %collective-permute-start.22 = (f32[24,8,128]{2,1,0:T(8,128)S(1)}, f32[24,8,128]{2,1,0:T(8,128)S(1)}, u32[]{:S(2)}, u32[]{:S(2)}) collective-permute-start(f32[24,8,128]{2,1,0:T(8,128)S(1)} %get-tuple-element.127), channel_id=1, source_target_pairs={{0,32},{32,0},{64,96},{96,64},{128,160},{160,128},{192,224},{224,1... | collective-permute-start | bytes 294920 | tf_op jit(solution)/shard_map/ppermute | solution.py:580
  50.3 4.6 %collective-permute-start.23 = (f32[12,2,8,128]{3,2,1,0:T(8,128)S(1)}, f32[12,2,8,128]{3,2,1,0:T(8,128)S(1)}, u32[]{:S(2)}, u32[]{:S(2)}) collective-permute-start(f32[12,2,8,128]{3,2,1,0:T(8,128)S(1)} %get-tuple-element.128), channel_id=1, source_target_pairs={{0,8},{8,0},{24,16},{16,24},{17,25},{25,17},{9,1},{1,9},{2,10},{10... | collective-permute-start | bytes 294920 | tf_op jit(solution)/shard_map/ppermute | solution.py:582
  55.1 15.4 %collective-permute-start.24 = (f32[24,8,128]{2,1,0:T(8,128)S(1)}, f32[24,8,128]{2,1,0:T(8,128)S(1)}, u32[]{:S(2)}, u32[]{:S(2)}) collective-permute-start(f32[24,8,128]{2,1,0:T(8,128)S(1)} %get-tuple-element.131), channel_id=1, source_target_pairs={{32,64},{64,32},{96,128},{128,96},{160,192},{192,160},{224,256},{2... | collective-permute-start | bytes 294920 | tf_op jit(solution)/shard_map/ppermute | solution.py:581
  59.9 10.6 %collective-permute-start.25 = (f32[12,2,8,128]{3,2,1,0:T(8,128)S(1)}, f32[12,2,8,128]{3,2,1,0:T(8,128)S(1)}, u32[]{:S(2)}, u32[]{:S(2)}) collective-permute-start(f32[12,2,8,128]{3,2,1,0:T(8,128)S(1)} %get-tuple-element.132), channel_id=1, source_target_pairs={{8,24},{24,8},{16,17},{17,16},{25,9},{9,25},{1,2},{2,1},{10,26},{2... | collective-permute-start | bytes 294920 | tf_op jit(solution)/shard_map/ppermute | solution.py:583
  63.2 7.4 %collective-permute-start.26 = (f32[24,8,128]{2,1,0:T(8,128)S(1)}, f32[24,8,128]{2,1,0:T(8,128)S(1)}, u32[]{:S(2)}, u32[]{:S(2)}) collective-permute-start(f32[24,8,128]{2,1,0:T(8,128)S(1)} %get-tuple-element.133), channel_id=1, source_target_pairs={{0,32},{32,0},{64,96},{96,64},{128,160},{160,128},{192,224},{224,1... | collective-permute-start | bytes 294920 | tf_op jit(solution)/shard_map/ppermute | solution.py:580
  65.1 6.0 %collective-permute-start.27 = (f32[12,2,8,128]{3,2,1,0:T(8,128)S(1)}, f32[12,2,8,128]{3,2,1,0:T(8,128)S(1)}, u32[]{:S(2)}, u32[]{:S(2)}) collective-permute-start(f32[12,2,8,128]{3,2,1,0:T(8,128)S(1)} %get-tuple-element.134), channel_id=1, source_target_pairs={{0,8},{8,0},{24,16},{16,24},{17,25},{25,17},{9,1},{1,9},{2,10},{10... | collective-permute-start | bytes 294920 | tf_op jit(solution)/shard_map/ppermute | solution.py:582
  71.3 11.6 %collective-permute-start.28 = (f32[24,8,128]{2,1,0:T(8,128)S(1)}, f32[24,8,128]{2,1,0:T(8,128)S(1)}, u32[]{:S(2)}, u32[]{:S(2)}) collective-permute-start(f32[24,8,128]{2,1,0:T(8,128)S(1)} %get-tuple-element.136), channel_id=1, source_target_pairs={{32,64},{64,32},{96,128},{128,96},{160,192},{192,160},{224,256},{2... | collective-permute-start | bytes 294920 | tf_op jit(solution)/shard_map/ppermute | solution.py:581
  74.6 8.4 %collective-permute-start.29 = (f32[12,2,8,128]{3,2,1,0:T(8,128)S(1)}, f32[12,2,8,128]{3,2,1,0:T(8,128)S(1)}, u32[]{:S(2)}, u32[]{:S(2)}) collective-permute-start(f32[12,2,8,128]{3,2,1,0:T(8,128)S(1)} %get-tuple-element.137), channel_id=1, source_target_pairs={{8,24},{24,8},{16,17},{17,16},{25,9},{9,25},{1,2},{2,1},{10,26},{2... | collective-permute-start | bytes 294920 | tf_op jit(solution)/shard_map/ppermute | solution.py:583
  76.5 6.5 %collective-permute-start.30 = (f32[24,8,128]{2,1,0:T(8,128)S(1)}, f32[24,8,128]{2,1,0:T(8,128)S(1)}, u32[]{:S(2)}, u32[]{:S(2)}) collective-permute-start(f32[24,8,128]{2,1,0:T(8,128)S(1)} %get-tuple-element.138), channel_id=1, source_target_pairs={{0,32},{32,0},{64,96},{96,64},{128,160},{160,128},{192,224},{224,1... | collective-permute-start | bytes 294920 | tf_op jit(solution)/shard_map/ppermute | solution.py:580
  78.8 4.7 %collective-permute-start.31 = (f32[12,2,8,128]{3,2,1,0:T(8,128)S(1)}, f32[12,2,8,128]{3,2,1,0:T(8,128)S(1)}, u32[]{:S(2)}, u32[]{:S(2)}) collective-permute-start(f32[12,2,8,128]{3,2,1,0:T(8,128)S(1)} %get-tuple-element.139), channel_id=1, source_target_pairs={{0,8},{8,0},{24,16},{16,24},{17,25},{25,17},{9,1},{1,9},{2,10},{10... | collective-permute-start | bytes 294920 | tf_op jit(solution)/shard_map/ppermute | solution.py:582
  83.8 15.2 %collective-permute-start.32 = (f32[24,8,128]{2,1,0:T(8,128)S(1)}, f32[24,8,128]{2,1,0:T(8,128)S(1)}, u32[]{:S(2)}, u32[]{:S(2)}) collective-permute-start(f32[24,8,128]{2,1,0:T(8,128)S(1)} %get-tuple-element.142), channel_id=1, source_target_pairs={{32,64},{64,32},{96,128},{128,96},{160,192},{192,160},{224,256},{2... | collective-permute-start | bytes 294920 | tf_op jit(solution)/shard_map/ppermute | solution.py:581
  88.4 10.6 %collective-permute-start.33 = (f32[12,2,8,128]{3,2,1,0:T(8,128)S(1)}, f32[12,2,8,128]{3,2,1,0:T(8,128)S(1)}, u32[]{:S(2)}, u32[]{:S(2)}) collective-permute-start(f32[12,2,8,128]{3,2,1,0:T(8,128)S(1)} %get-tuple-element.143), channel_id=1, source_target_pairs={{8,24},{24,8},{16,17},{17,16},{25,9},{9,25},{1,2},{2,1},{10,26},{2... | collective-permute-start | bytes 294920 | tf_op jit(solution)/shard_map/ppermute | solution.py:583
  91.7 7.4 %collective-permute-start.34 = (f32[24,8,128]{2,1,0:T(8,128)S(1)}, f32[24,8,128]{2,1,0:T(8,128)S(1)}, u32[]{:S(2)}, u32[]{:S(2)}) collective-permute-start(f32[24,8,128]{2,1,0:T(8,128)S(1)} %get-tuple-element.144), channel_id=1, source_target_pairs={{0,32},{32,0},{64,96},{96,64},{128,160},{160,128},{192,224},{224,1... | collective-permute-start | bytes 294920 | tf_op jit(solution)/shard_map/ppermute | solution.py:580
  93.6 6.0 %collective-permute-start.35 = (f32[12,2,8,128]{3,2,1,0:T(8,128)S(1)}, f32[12,2,8,128]{3,2,1,0:T(8,128)S(1)}, u32[]{:S(2)}, u32[]{:S(2)}) collective-permute-start(f32[12,2,8,128]{3,2,1,0:T(8,128)S(1)} %get-tuple-element.145), channel_id=1, source_target_pairs={{0,8},{8,0},{24,16},{16,24},{17,25},{25,17},{9,1},{1,9},{2,10},{10... | collective-permute-start | bytes 294920 | tf_op jit(solution)/shard_map/ppermute | solution.py:582
  99.8 11.6 %collective-permute-start.36 = (f32[24,8,128]{2,1,0:T(8,128)S(1)}, f32[24,8,128]{2,1,0:T(8,128)S(1)}, u32[]{:S(2)}, u32[]{:S(2)}) collective-permute-start(f32[24,8,128]{2,1,0:T(8,128)S(1)} %get-tuple-element.147), channel_id=1, source_target_pairs={{32,64},{64,32},{96,128},{128,96},{160,192},{192,160},{224,256},{2... | collective-permute-start | bytes 294920 | tf_op jit(solution)/shard_map/ppermute | solution.py:581
  103.0 8.4 %collective-permute-start.37 = (f32[12,2,8,128]{3,2,1,0:T(8,128)S(1)}, f32[12,2,8,128]{3,2,1,0:T(8,128)S(1)}, u32[]{:S(2)}, u32[]{:S(2)}) collective-permute-start(f32[12,2,8,128]{3,2,1,0:T(8,128)S(1)} %get-tuple-element.148), channel_id=1, source_target_pairs={{8,24},{24,8},{16,17},{17,16},{25,9},{9,25},{1,2},{2,1},{10,26},{2... | collective-permute-start | bytes 294920 | tf_op jit(solution)/shard_map/ppermute | solution.py:583
  105.0 6.5 %collective-permute-start.38 = (f32[24,8,128]{2,1,0:T(8,128)S(1)}, f32[24,8,128]{2,1,0:T(8,128)S(1)}, u32[]{:S(2)}, u32[]{:S(2)}) collective-permute-start(f32[24,8,128]{2,1,0:T(8,128)S(1)} %get-tuple-element.149), channel_id=1, source_target_pairs={{0,32},{32,0},{64,96},{96,64},{128,160},{160,128},{192,224},{224,1... | collective-permute-start | bytes 294920 | tf_op jit(solution)/shard_map/ppermute | solution.py:580
  107.3 4.7 %collective-permute-start.39 = (f32[12,2,8,128]{3,2,1,0:T(8,128)S(1)}, f32[12,2,8,128]{3,2,1,0:T(8,128)S(1)}, u32[]{:S(2)}, u32[]{:S(2)}) collective-permute-start(f32[12,2,8,128]{3,2,1,0:T(8,128)S(1)} %get-tuple-element.150), channel_id=1, source_target_pairs={{0,8},{8,0},{24,16},{16,24},{17,25},{25,17},{9,1},{1,9},{2,10},{10... | collective-permute-start | bytes 294920 | tf_op jit(solution)/shard_map/ppermute | solution.py:582
  112.3 26.5 %collective-permute-start.40 = (f32[24,8,128]{2,1,0:T(8,128)S(1)}, f32[24,8,128]{2,1,0:T(8,128)S(1)}, u32[]{:S(2)}, u32[]{:S(2)}) collective-permute-start(f32[24,8,128]{2,1,0:T(8,128)S(1)} %get-tuple-element.156), channel_id=1, source_target_pairs={{32,64},{64,32},{96,128},{128,96},{160,192},{192,160},{224,256},{2... | collective-permute-start | bytes 294920 | tf_op jit(solution)/shard_map/ppermute | solution.py:581
  116.9 21.9 %collective-permute-start.41 = (f32[12,2,8,128]{3,2,1,0:T(8,128)S(1)}, f32[12,2,8,128]{3,2,1,0:T(8,128)S(1)}, u32[]{:S(2)}, u32[]{:S(2)}) collective-permute-start(f32[12,2,8,128]{3,2,1,0:T(8,128)S(1)} %get-tuple-element.157), channel_id=1, source_target_pairs={{8,24},{24,8},{16,17},{17,16},{25,9},{9,25},{1,2},{2,1},{10,26},{2... | collective-permute-start | bytes 294920 | tf_op jit(solution)/shard_map/ppermute | solution.py:583
  120.1 18.6 %collective-permute-start.42 = (f32[24,8,128]{2,1,0:T(8,128)S(1)}, f32[24,8,128]{2,1,0:T(8,128)S(1)}, u32[]{:S(2)}, u32[]{:S(2)}) collective-permute-start(f32[24,8,128]{2,1,0:T(8,128)S(1)} %get-tuple-element.158), channel_id=1, source_target_pairs={{0,32},{32,0},{64,96},{96,64},{128,160},{160,128},{192,224},{224,1... | collective-permute-start | bytes 294920 | tf_op jit(solution)/shard_map/ppermute | solution.py:580
  122.1 16.7 %collective-permute-start.43 = (f32[12,2,8,128]{3,2,1,0:T(8,128)S(1)}, f32[12,2,8,128]{3,2,1,0:T(8,128)S(1)}, u32[]{:S(2)}, u32[]{:S(2)}) collective-permute-start(f32[12,2,8,128]{3,2,1,0:T(8,128)S(1)} %get-tuple-element.159), channel_id=1, source_target_pairs={{0,8},{8,0},{24,16},{16,24},{17,25},{25,17},{9,1},{1,9},{2,10},{10... | collective-permute-start | bytes 294920 | tf_op jit(solution)/shard_map/ppermute | solution.py:582
  128.3 10.5 %all-to-all-start.5 = ((f32[32,1,128]{2,1,0:T(1,128)}), f32[32,1,128]{2,1,0:T(1,128)S(1)}, u32[]{:S(2)}, u32[]{:S(2)}) async-start(f32[32,1,128]{2,1,0:T(1,128)} %bitcast.20), calls=%async_computation.5 | async-start | bytes 32768 | tf_op jit(solution)/shard_map/all_to_all | solution.py:347
  139.0 33.4 %collective-permute-start.44 = (f32[24,8,128]{2,1,0:T(8,128)S(1)}, f32[24,8,128]{2,1,0:T(8,128)S(1)}, u32[]{:S(2)}, u32[]{:S(2)}) collective-permute-start(f32[24,8,128]{2,1,0:T(8,128)S(1)} %get-tuple-element.161), channel_id=1, source_target_pairs={{32,64},{64,32},{96,128},{128,96},{160,192},{192,160},{224,256},{2... | collective-permute-start | bytes 294920 | tf_op jit(solution)/shard_map/ppermute | solution.py:581
  142.3 30.2 %collective-permute-start.45 = (f32[12,2,8,128]{3,2,1,0:T(8,128)S(1)}, f32[12,2,8,128]{3,2,1,0:T(8,128)S(1)}, u32[]{:S(2)}, u32[]{:S(2)}) collective-permute-start(f32[12,2,8,128]{3,2,1,0:T(8,128)S(1)} %get-tuple-element.162), channel_id=1, source_target_pairs={{8,24},{24,8},{16,17},{17,16},{25,9},{9,25},{1,2},{2,1},{10,26},{2... | collective-permute-start | bytes 294920 | tf_op jit(solution)/shard_map/ppermute | solution.py:583
  145.1 27.4 %collective-permute-start.46 = (f32[24,8,128]{2,1,0:T(8,128)S(1)}, f32[24,8,128]{2,1,0:T(8,128)S(1)}, u32[]{:S(2)}, u32[]{:S(2)}) collective-permute-start(f32[24,8,128]{2,1,0:T(8,128)S(1)} %get-tuple-element.163), channel_id=1, source_target_pairs={{0,32},{32,0},{64,96},{96,64},{128,160},{160,128},{192,224},{224,1... | collective-permute-start | bytes 294920 | tf_op jit(solution)/shard_map/ppermute | solution.py:580
  147.5 25.0 %collective-permute-start.47 = (f32[12,2,8,128]{3,2,1,0:T(8,128)S(1)}, f32[12,2,8,128]{3,2,1,0:T(8,128)S(1)}, u32[]{:S(2)}, u32[]{:S(2)}) collective-permute-start(f32[12,2,8,128]{3,2,1,0:T(8,128)S(1)} %get-tuple-element.164), channel_id=1, source_target_pairs={{0,8},{8,0},{24,16},{16,24},{17,25},{25,17},{9,1},{1,9},{2,10},{10... | collective-permute-start | bytes 294920 | tf_op jit(solution)/shard_map/ppermute | solution.py:582

commit v3 on v2

--- a/solution.py
+++ b/solution.py
@@ -21,15 +21,9 @@
 PIVOT_GUARD = 1e-3
 VMEM = pl.BlockSpec(memory_space=pltpu.VMEM)
 SMEM = pl.BlockSpec(memory_space=pltpu.SMEM)
-ANY = pl.BlockSpec(memory_space=pl.ANY)
-
-
-def call(body, outs, args, flops=10**6, after=(), scratch=(), flag=False):
-    count = len(args)
-
-    def without_after(*refs):
-        body(*refs[:count], *refs[count + len(after) :])
-
+
+
+def call(body, outs, args, flops=10**6, scratch=(), flag=False):
     shapes = [jax.ShapeDtypeStruct(s, F32) for s in outs]
     out_specs = [VMEM] * len(shapes)
     if flag:
@@ -37,14 +31,14 @@
         out_specs.append(SMEM)
     moved = 4 * sum(a.size for a in args)
     return pl.pallas_call(
-        without_after,
+        body,
         out_shape=shapes,
-        in_specs=[VMEM] * count + [ANY] * len(after),
+        in_specs=[VMEM] * len(args),
         out_specs=out_specs,
         scratch_shapes=scratch,
         compiler_params=pltpu.CompilerParams(vmem_limit_bytes=16 * 2**20),
         cost_estimate=pl.CostEstimate(flops=flops, bytes_accessed=moved, transcendentals=0),
-    )(*args, *after)
+    )(*args)
 
 
 def place():
@@ -292,19 +286,15 @@
     return acc
 
 
-def outer_body(parity, with_base, with_faces, *refs):
-    partial, links = refs[:2]
-    recv = in_face_order(refs[2:6])
-    base = refs[6] if with_base else None
-    out = refs[7] if with_base else refs[6]
-    faces = refs[-4:]
+def outer_body(parity, base, partial, links, recv, out, faces):
+    recv = in_face_order(recv)
     for t in range(2):
         acc = finished_spinor(partial, links, parity, t, recv, base)
         for p in range(2):
             for s in range(4):
                 for c in range(3):
                     out[(p * 4 + s) * 3 + c, t] = acc[p][s][c]
-    if with_faces:
+    if faces:
         write_faces(out, links, 1 - parity, faces)
 
 
@@ -320,11 +310,10 @@
     cell = lax.broadcasted_iota(jnp.int32, rows.shape, 1) % 32
     line = lax.broadcasted_iota(jnp.int32, rows.shape, 0)
     packed = jnp.sum(jnp.where(cell == line, rows, 0.0), axis=0, keepdims=True)
-    out[...] = jnp.broadcast_to(packed, out.shape)
-
-
-def moments_body(spinor, *refs):
-    given, out, scratch = refs[:-2], refs[-2], refs[-1]
+    out[...] = jnp.broadcast_to(packed[None], out.shape)
+
+
+def moments_body(spinor, given, out, scratch):
     scratch[...] = jnp.zeros(scratch.shape, F32)
     at = 0
     for total in [[m[i] for i in range(5)] for m in given] + [moment_tiles(spinor)]:
@@ -334,18 +323,24 @@
     pick_cells(scratch, out)
 
 
-def moments_call(spinor, given):
-    scratch = [pltpu.VMEM((24, 128), F32)]
-    return call(moments_body, [(32, 128)], (spinor, *given), 10**5, scratch=scratch)[0]
+MOMENT_SCRATCH = [pltpu.VMEM((24, 128), F32)]
+
+
+def moments_call(spinor):
+    def body(spinor, out, scratch):
+        moments_body(spinor, (), out, scratch)
+
+    return call(body, [(32, 8, 128)], (spinor,), 10**5, scratch=MOMENT_SCRATCH)[0]
 
 
 def row_sum_body(rows, out):
-    out[...] = jnp.broadcast_to(jnp.sum(rows[...], axis=0, keepdims=True), out.shape)
+    total = jnp.sum(rows[:, 0, :], axis=0, keepdims=True)
+    out[...] = jnp.broadcast_to(total[None], out.shape)
 
 
 def reduce_rows(rows):
     rows = lax.all_to_all(rows, ("gz", "gy"), 0, 0, tiled=True)
-    return call(row_sum_body, [(16, 128)], (rows,), 10**4)[0]
+    return call(row_sum_body, [(16, 16, 128)], (rows,), 10**4)[0]
 
 
 def reduce_devices(rows):
@@ -451,7 +446,7 @@
 
 
 def coefficients_body(rows, out, good_out):
-    total = jnp.sum(rows[...], axis=0, keepdims=True)
+    total = jnp.sum(rows[:, 0, :], axis=0, keepdims=True)
     mu = [read_matrix(total, f) for f in range(4)]
     line, group = sublanes(), group_of_lane()
     diagonal = (line == group) & (line < 4)
@@ -485,8 +480,8 @@
 
 
 def solve_body(which, c_rows, e_rows, out):
-    c = read_matrix(jnp.sum(c_rows[...], axis=0, keepdims=True), which[0])
-    e = read_matrix(jnp.sum(e_rows[...], axis=0, keepdims=True), which[1])
+    c = read_matrix(jnp.sum(c_rows[:, 0, :], axis=0, keepdims=True), which[0])
+    e = read_matrix(jnp.sum(e_rows[:, 0, :], axis=0, keepdims=True), which[1])
     solved, _ = solve(c, e, jnp.zeros(TILE, F32))
     write_coefficients(out, 0, solved)
 
@@ -593,24 +588,39 @@
     return call(body, outs, (spinor, links), 8 * 10**6)
 
 
-def hop_outer(partial, links, recv, parity, base=None, with_faces=True, after=()):
-    args = (partial, links, *in_start_order(recv)) + (() if base is None else (base,))
+def hop_outer(partial, links, recv, parity, base=None, with_faces=True, moments=(), rows=None):
+    outs = [SPINOR] + (FACES if with_faces else [])
+    args = (partial, links, *in_start_order(recv))
+    extra = moments if rows is None else (rows,)
+    if base is not None:
+        args += (base,)
+    used, made = len(args), len(outs)
 
     def body(*refs):
-        outer_body(parity, base is not None, with_faces, *refs)
-
-    outs = call(body, [SPINOR] + (FACES if with_faces else []), args, 4 * 10**6, after)
-    return outs[0], outs[1:]
-
-
-def half_normal(spinor, faces, links, with_moments=False, with_faces=True):
+        given, results = refs[: used + len(extra)], refs[used + len(extra) :]
+        old = None if base is None else given[6]
+        outer_body(parity, old, given[0], given[1], given[2:6], results[0], results[1:made])
+        if moments:
+            moments_body(results[0], given[used:], results[made], results[-1])
+        if rows is not None:
+            row_sum_body(given[used], results[made])
+
+    scratch = MOMENT_SCRATCH if moments else ()
+    more = [(32, 8, 128)] if moments else [] if rows is None else [(16, 16, 128)]
+    results = call(body, outs + more, args + tuple(extra), 4 * 10**6, scratch)
+    return results[0], results[1:made], results[made:]
+
+
+def half_normal(spinor, faces, links, with_moments=False, with_faces=True, moments=()):
     recv = exchange(faces)
-    partial, *moments = hop_inner(spinor, links, 1, with_moments)
-    odd, faces = hop_outer(partial, links, recv, 1)
+    partial, *made = hop_inner(spinor, links, 1, with_moments)
+    odd, faces, _ = hop_outer(partial, links, recv, 1)
     recv = exchange(faces)
     (partial,) = hop_inner(odd, links, 0)
-    out, faces = hop_outer(partial, links, recv, 0, spinor, with_faces)
-    return out, faces, moments
+    if moments:
+        moments = (*moments, *made)
+    out, faces, rows = hop_outer(partial, links, recv, 0, spinor, with_faces, moments)
+    return out, faces, rows or made
 
 
 def faces_only(spinor, links):
@@ -635,12 +645,12 @@
 
     alpha = solve_call(rows, rows, 1, 0)
     residual = combine(-1, first, image, alpha)
-    rho = reduce_devices(moments_call(residual, ()))
+    rho = reduce_devices(moments_call(residual))
     beta = solve_call(rows, rho, 0, 0)
     search = combine(1, residual, first, beta)
     faces = faces_only(search, links)
     halfway, faces, _ = half_normal(search, faces, links)
-    curvature = reduce_devices(moments_call(halfway, ()))
+    curvature = reduce_devices(moments_call(halfway))
     images, _, _ = half_normal(halfway, faces, links, with_faces=False)
     alpha1 = solve_call(curvature, rho, 0, 0)
     zero = jnp.zeros(SPINOR, F32)
@@ -656,13 +666,14 @@
     links, first, *faces = call(unpack_body, [(144, 2, 8, 128), SPINOR] + FACES, (received,))
     half1, faces, moments0 = half_normal(first, faces, links, True)
     image, faces, moments1 = half_normal(half1, faces, links, True)
-    half2, faces, moments2 = half_normal(image, faces, links, True)
-
-    rows = moments_call(half2, (*moments0, *moments1, *moments2))
+    half2, faces, (rows,) = half_normal(
+        image, faces, links, True, moments=(*moments0, *moments1)
+    )
+
+    rows = lax.all_to_all(rows, ("gz", "gy"), 0, 0, tiled=True)
     recv = exchange(faces)
     (partial,) = hop_inner(half2, links, 1)
-    rows = reduce_rows(rows)
-    odd, faces = hop_outer(partial, links, recv, 1, after=(rows,))
+    odd, faces, (rows,) = hop_outer(partial, links, recv, 1, rows=rows)
     rows = lax.all_to_all(rows, "ta", 0, 0, tiled=True)
     recv = exchange(faces)
     (partial,) = hop_inner(odd, links, 0)

time: 188 us -> 176 us (0.936)
  blocking collectives: 48.5 us -> 32.1 us
  starting transfers between devices: 111 us -> 121 us
  waiting for transfers between devices: 10.1 us -> 4.17 us
    all_to_all x1 -> x0, blocking collectives: 18.4 us -> none  [local(): rows = lax.all_to_all(rows, 'ta', 0, 0, tiled=True)]
    all_to_all x1 -> x2, starting transfers between devices: 3.62 us -> 13.1 us  [the longest x1 7.06 us: local(): rows = lax.all_to_all(rows, 'ta', 0, 0, tiled=True)]
    all_to_all x1 -> x2, waiting for transfers between devices: 6.56 us -> 0.01 us  [the longest x1 0.01 us: local(): rows = lax.all_to_all(rows, 'ta', 0, 0, tiled=True)]
    all_to_all x1, blocking collectives: 11.8 us -> 13.8 us  [local(): received = lax.all_to_all(out.reshape(4, 2, 96, 128), 'gz', 0, 0)]
    pallas_call x22 -> x20, Pallas kernels: 12.8 us -> 13.5 us  [call(): pl.pallas_call(body, out_shape=shapes, in_specs=[VMEM] * len(args), out_s...]
  transfers between devices with their start and end apart: 33 -> 34, of which waited for: 7 -> 7; matrix products, arithmetic and copies ran while one was open for 0% -> 0% of each run, Pallas kernels for 3% -> 3%
where the time goes in v3:
time: 176 us; the launch traced here: 175 us
  starting transfers between devices  121 us (69%)
  blocking collectives  32.1 us (18%)
  Pallas kernels  13.5 us (8%)
  waiting for transfers between devices  4.17 us (2%)
  local copies, waits for them, and re-layouts  1.88 us (1%)
  between operations  1.86 us (1%)
    ppermute x8, starting transfers between devices, exchange(): lax.ppermute(time_b, 'ta', make_pairs(times, 1))  35.8 us
    ppermute x8, starting transfers between devices, exchange(): lax.ppermute(row_a, ('gz', 'gy'), make_pairs(rows, 0))  34.8 us
    ppermute x8, starting transfers between devices, exchange(): lax.ppermute(row_b, ('gz', 'gy'), make_pairs(rows, 1))  21.6 us
    all_to_all x1, blocking collectives, local(): received = lax.all_to_all(packed, 'gz', 0, 0).reshape(960, 128)  18.3 us
    ppermute x8, starting transfers between devices, exchange(): lax.ppermute(time_a, 'ta', make_pairs(times, 0))  16.2 us
    all_to_all x1, blocking collectives, local(): received = lax.all_to_all(out.reshape(4, 2, 96, 128), 'gz', 0, 0)  13.8 us
    pallas_call x20, Pallas kernels, call(): pl.pallas_call(body, out_shape=shapes, in_specs=[VMEM] * len(args), out_s...  13.5 us
    all_to_all x1, starting transfers between devices, local(): rows = lax.all_to_all(rows, 'ta', 0, 0, tiled=True)  7.06 us
  transfers between devices with their start and end apart: 34, of which 7 were waited for; matrix products, arithmetic and copies ran while one was open for 0% of the time, Pallas kernels for 3%

profile of v3, /device:TPU:1, one launch (start us, length us, event | category | flops | bytes accessed | tf_op | source)
XLA Modules:
  0.0 175.2 jit_solution(7598498619289266634)
XLA Ops:
  0.6 1.0 copy-done
  1.6 0.9 copy-done.1
  2.5 1.3 shard_map.41
  3.8 18.3 %all_to_all.39 = f32[4,2,120,128]{3,2,1,0:T(8,128)S(1)} all-to-all(f32[4,2,120,128]{3,2,1,0:T(8,128)S(1)} %shard_map.41), channel_id=1, replica_groups=mesh['ta'=16,'gz'=4,'gy'=8] {'gz'}, dimensions={0} | all-to-all | bytes 983040 | tf_op jit(solution)/shard_map/all_to_all | solution.py:665
  22.1 2.0 %shard_map.42 = (f32[144,2,8,128]{3,2,1,0:T(8,128)S(1)}, f32[24,2,8,128]{3,2,1,0:T(8,128)S(1)}, f32[24,8,128]{2,1,0:T(8,128)S(1)}, f32[24,8,128]{2,1,0:T(8,128)S...) custom-call(f32[960,128]{1,0:T(8,128)S(1)} %bitcast.7), custom_call_target="tpu_custom_call" | custom-call | flops 1000000 | bytes 491520 | tf_op jit(solution)/shard_map/pallas_call | solution.py:33
  24.2 7.5 %collective-permute-start.16 = (f32[24,8,128]{2,1,0:T(8,128)S(1)}, f32[24,8,128]{2,1,0:T(8,128)S(1)}, u32[]{:S(2)}, u32[]{:S(2)}) collective-permute-start(f32[24,8,128]{2,1,0:T(8,128)S(1)} %get-tuple-element.122), channel_id=1, source_target_pairs={{32,64},{64,32},{96,128},{128,96},{160,192},{192,160},{224,256},{2... | collective-permute-start | bytes 294920 | tf_op jit(solution)/shard_map/ppermute | solution.py:576
  31.7 2.4 %collective-permute-start.17 = (f32[12,2,8,128]{3,2,1,0:T(8,128)S(1)}, f32[12,2,8,128]{3,2,1,0:T(8,128)S(1)}, u32[]{:S(2)}, u32[]{:S(2)}) collective-permute-start(f32[12,2,8,128]{3,2,1,0:T(8,128)S(1)} %get-tuple-element.123), channel_id=1, source_target_pairs={{8,24},{24,8},{16,17},{17,16},{25,9},{9,25},{1,2},{2,1},{10,26},{2... | collective-permute-start | bytes 294920 | tf_op jit(solution)/shard_map/ppermute | solution.py:578
  34.0 1.9 %collective-permute-start.18 = (f32[24,8,128]{2,1,0:T(8,128)S(1)}, f32[24,8,128]{2,1,0:T(8,128)S(1)}, u32[]{:S(2)}, u32[]{:S(2)}) collective-permute-start(f32[24,8,128]{2,1,0:T(8,128)S(1)} %get-tuple-element.124), channel_id=1, source_target_pairs={{0,32},{32,0},{64,96},{96,64},{128,160},{160,128},{192,224},{224,1... | collective-permute-start | bytes 294920 | tf_op jit(solution)/shard_map/ppermute | solution.py:575
  36.0 5.7 %collective-permute-start.19 = (f32[12,2,8,128]{3,2,1,0:T(8,128)S(1)}, f32[12,2,8,128]{3,2,1,0:T(8,128)S(1)}, u32[]{:S(2)}, u32[]{:S(2)}) collective-permute-start(f32[12,2,8,128]{3,2,1,0:T(8,128)S(1)} %get-tuple-element.125), channel_id=1, source_target_pairs={{0,8},{8,0},{24,16},{16,24},{17,25},{25,17},{9,1},{1,9},{2,10},{10... | collective-permute-start | bytes 294920 | tf_op jit(solution)/shard_map/ppermute | solution.py:577
  41.7 0.3 shard_map.43
  42.1 0.5 collective-permute-done.19.refs_5_
  42.6 0.2 shard_map.44
  42.8 3.6 %collective-permute-start.20 = (f32[24,8,128]{2,1,0:T(8,128)S(1)}, f32[24,8,128]{2,1,0:T(8,128)S(1)}, u32[]{:S(2)}, u32[]{:S(2)}) collective-permute-start(f32[24,8,128]{2,1,0:T(8,128)S(1)} %get-tuple-element.127), channel_id=1, source_target_pairs={{32,64},{64,32},{96,128},{128,96},{160,192},{192,160},{224,256},{2... | collective-permute-start | bytes 294920 | tf_op jit(solution)/shard_map/ppermute | solution.py:576
  46.5 1.9 %collective-permute-start.21 = (f32[12,2,8,128]{3,2,1,0:T(8,128)S(1)}, f32[12,2,8,128]{3,2,1,0:T(8,128)S(1)}, u32[]{:S(2)}, u32[]{:S(2)}) collective-permute-start(f32[12,2,8,128]{3,2,1,0:T(8,128)S(1)} %get-tuple-element.128), channel_id=1, source_target_pairs={{8,24},{24,8},{16,17},{17,16},{25,9},{9,25},{1,2},{2,1},{10,26},{2... | collective-permute-start | bytes 294920 | tf_op jit(solution)/shard_map/ppermute | solution.py:578
  48.4 1.9 %collective-permute-start.22 = (f32[24,8,128]{2,1,0:T(8,128)S(1)}, f32[24,8,128]{2,1,0:T(8,128)S(1)}, u32[]{:S(2)}, u32[]{:S(2)}) collective-permute-start(f32[24,8,128]{2,1,0:T(8,128)S(1)} %get-tuple-element.129), channel_id=1, source_target_pairs={{0,32},{32,0},{64,96},{96,64},{128,160},{160,128},{192,224},{224,1... | collective-permute-start | bytes 294920 | tf_op jit(solution)/shard_map/ppermute | solution.py:575
  50.3 3.6 %collective-permute-start.23 = (f32[12,2,8,128]{3,2,1,0:T(8,128)S(1)}, f32[12,2,8,128]{3,2,1,0:T(8,128)S(1)}, u32[]{:S(2)}, u32[]{:S(2)}) collective-permute-start(f32[12,2,8,128]{3,2,1,0:T(8,128)S(1)} %get-tuple-element.130), channel_id=1, source_target_pairs={{0,8},{8,0},{24,16},{16,24},{17,25},{25,17},{9,1},{1,9},{2,10},{10... | collective-permute-start | bytes 294920 | tf_op jit(solution)/shard_map/ppermute | solution.py:577
  54.0 0.3 shard_map.45.refs_0_
  54.3 0.6 collective-permute-done.23.refs_5_
  54.9 0.2 shard_map.46
  55.1 4.8 %collective-permute-start.24 = (f32[24,8,128]{2,1,0:T(8,128)S(1)}, f32[24,8,128]{2,1,0:T(8,128)S(1)}, u32[]{:S(2)}, u32[]{:S(2)}) collective-permute-start(f32[24,8,128]{2,1,0:T(8,128)S(1)} %get-tuple-element.133), channel_id=1, source_target_pairs={{32,64},{64,32},{96,128},{128,96},{160,192},{192,160},{224,256},{2... | collective-permute-start | bytes 294920 | tf_op jit(solution)/shard_map/ppermute | solution.py:576
  59.9 3.2 %collective-permute-start.25 = (f32[12,2,8,128]{3,2,1,0:T(8,128)S(1)}, f32[12,2,8,128]{3,2,1,0:T(8,128)S(1)}, u32[]{:S(2)}, u32[]{:S(2)}) collective-permute-start(f32[12,2,8,128]{3,2,1,0:T(8,128)S(1)} %get-tuple-element.134), channel_id=1, source_target_pairs={{8,24},{24,8},{16,17},{17,16},{25,9},{9,25},{1,2},{2,1},{10,26},{2... | collective-permute-start | bytes 294920 | tf_op jit(solution)/shard_map/ppermute | solution.py:578
  63.2 1.9 %collective-permute-start.26 = (f32[24,8,128]{2,1,0:T(8,128)S(1)}, f32[24,8,128]{2,1,0:T(8,128)S(1)}, u32[]{:S(2)}, u32[]{:S(2)}) collective-permute-start(f32[24,8,128]{2,1,0:T(8,128)S(1)} %get-tuple-element.135), channel_id=1, source_target_pairs={{0,32},{32,0},{64,96},{96,64},{128,160},{160,128},{192,224},{224,1... | collective-permute-start | bytes 294920 | tf_op jit(solution)/shard_map/ppermute | solution.py:575
  65.1 5.1 %collective-permute-start.27 = (f32[12,2,8,128]{3,2,1,0:T(8,128)S(1)}, f32[12,2,8,128]{3,2,1,0:T(8,128)S(1)}, u32[]{:S(2)}, u32[]{:S(2)}) collective-permute-start(f32[12,2,8,128]{3,2,1,0:T(8,128)S(1)} %get-tuple-element.136), channel_id=1, source_target_pairs={{0,8},{8,0},{24,16},{16,24},{17,25},{25,17},{9,1},{1,9},{2,10},{10... | collective-permute-start | bytes 294920 | tf_op jit(solution)/shard_map/ppermute | solution.py:577
  70.2 0.4 shard_map.47
  70.6 0.5 collective-permute-done.27.refs_5_
  71.3 3.2 %collective-permute-start.28 = (f32[24,8,128]{2,1,0:T(8,128)S(1)}, f32[24,8,128]{2,1,0:T(8,128)S(1)}, u32[]{:S(2)}, u32[]{:S(2)}) collective-permute-start(f32[24,8,128]{2,1,0:T(8,128)S(1)} %get-tuple-element.138), channel_id=1, source_target_pairs={{32,64},{64,32},{96,128},{128,96},{160,192},{192,160},{224,256},{2... | collective-permute-start | bytes 294920 | tf_op jit(solution)/shard_map/ppermute | solution.py:576
  74.6 1.9 %collective-permute-start.29 = (f32[12,2,8,128]{3,2,1,0:T(8,128)S(1)}, f32[12,2,8,128]{3,2,1,0:T(8,128)S(1)}, u32[]{:S(2)}, u32[]{:S(2)}) collective-permute-start(f32[12,2,8,128]{3,2,1,0:T(8,128)S(1)} %get-tuple-element.139), channel_id=1, source_target_pairs={{8,24},{24,8},{16,17},{17,16},{25,9},{9,25},{1,2},{2,1},{10,26},{2... | collective-permute-start | bytes 294920 | tf_op jit(solution)/shard_map/ppermute | solution.py:578
  76.5 2.3 %collective-permute-start.30 = (f32[24,8,128]{2,1,0:T(8,128)S(1)}, f32[24,8,128]{2,1,0:T(8,128)S(1)}, u32[]{:S(2)}, u32[]{:S(2)}) collective-permute-start(f32[24,8,128]{2,1,0:T(8,128)S(1)} %get-tuple-element.140), channel_id=1, source_target_pairs={{0,32},{32,0},{64,96},{96,64},{128,160},{160,128},{192,224},{224,1... | collective-permute-start | bytes 294920 | tf_op jit(solution)/shard_map/ppermute | solution.py:575
  78.8 3.8 %collective-permute-start.31 = (f32[12,2,8,128]{3,2,1,0:T(8,128)S(1)}, f32[12,2,8,128]{3,2,1,0:T(8,128)S(1)}, u32[]{:S(2)}, u32[]{:S(2)}) collective-permute-start(f32[12,2,8,128]{3,2,1,0:T(8,128)S(1)} %get-tuple-element.141), channel_id=1, source_target_pairs={{0,8},{8,0},{24,16},{16,24},{17,25},{25,17},{9,1},{1,9},{2,10},{10... | collective-permute-start | bytes 294920 | tf_op jit(solution)/shard_map/ppermute | solution.py:577
  82.6 0.3 shard_map.49.refs_0_
  83.0 0.6 collective-permute-done.31.refs_5_
  83.6 0.2 shard_map.50
  83.8 4.6 %collective-permute-start.32 = (f32[24,8,128]{2,1,0:T(8,128)S(1)}, f32[24,8,128]{2,1,0:T(8,128)S(1)}, u32[]{:S(2)}, u32[]{:S(2)}) collective-permute-start(f32[24,8,128]{2,1,0:T(8,128)S(1)} %get-tuple-element.144), channel_id=1, source_target_pairs={{32,64},{64,32},{96,128},{128,96},{160,192},{192,160},{224,256},{2... | collective-permute-start | bytes 294920 | tf_op jit(solution)/shard_map/ppermute | solution.py:576
  88.4 3.2 %collective-permute-start.33 = (f32[12,2,8,128]{3,2,1,0:T(8,128)S(1)}, f32[12,2,8,128]{3,2,1,0:T(8,128)S(1)}, u32[]{:S(2)}, u32[]{:S(2)}) collective-permute-start(f32[12,2,8,128]{3,2,1,0:T(8,128)S(1)} %get-tuple-element.145), channel_id=1, source_target_pairs={{8,24},{24,8},{16,17},{17,16},{25,9},{9,25},{1,2},{2,1},{10,26},{2... | collective-permute-start | bytes 294920 | tf_op jit(solution)/shard_map/ppermute | solution.py:578
  91.7 1.9 %collective-permute-start.34 = (f32[24,8,128]{2,1,0:T(8,128)S(1)}, f32[24,8,128]{2,1,0:T(8,128)S(1)}, u32[]{:S(2)}, u32[]{:S(2)}) collective-permute-start(f32[24,8,128]{2,1,0:T(8,128)S(1)} %get-tuple-element.146), channel_id=1, source_target_pairs={{0,32},{32,0},{64,96},{96,64},{128,160},{160,128},{192,224},{224,1... | collective-permute-start | bytes 294920 | tf_op jit(solution)/shard_map/ppermute | solution.py:575
  93.6 5.1 %collective-permute-start.35 = (f32[12,2,8,128]{3,2,1,0:T(8,128)S(1)}, f32[12,2,8,128]{3,2,1,0:T(8,128)S(1)}, u32[]{:S(2)}, u32[]{:S(2)}) collective-permute-start(f32[12,2,8,128]{3,2,1,0:T(8,128)S(1)} %get-tuple-element.147), channel_id=1, source_target_pairs={{0,8},{8,0},{24,16},{16,24},{17,25},{25,17},{9,1},{1,9},{2,10},{10... | collective-permute-start | bytes 294920 | tf_op jit(solution)/shard_map/ppermute | solution.py:577
  98.7 0.3 shard_map.51
  99.1 0.5 collective-permute-done.35.refs_5_
  99.8 3.2 %collective-permute-start.36 = (f32[24,8,128]{2,1,0:T(8,128)S(1)}, f32[24,8,128]{2,1,0:T(8,128)S(1)}, u32[]{:S(2)}, u32[]{:S(2)}) collective-permute-start(f32[24,8,128]{2,1,0:T(8,128)S(1)} %get-tuple-element.149), channel_id=1, source_target_pairs={{32,64},{64,32},{96,128},{128,96},{160,192},{192,160},{224,256},{2... | collective-permute-start | bytes 294920 | tf_op jit(solution)/shard_map/ppermute | solution.py:576
  103.1 1.9 %collective-permute-start.37 = (f32[12,2,8,128]{3,2,1,0:T(8,128)S(1)}, f32[12,2,8,128]{3,2,1,0:T(8,128)S(1)}, u32[]{:S(2)}, u32[]{:S(2)}) collective-permute-start(f32[12,2,8,128]{3,2,1,0:T(8,128)S(1)} %get-tuple-element.150), channel_id=1, source_target_pairs={{8,24},{24,8},{16,17},{17,16},{25,9},{9,25},{1,2},{2,1},{10,26},{2... | collective-permute-start | bytes 294920 | tf_op jit(solution)/shard_map/ppermute | solution.py:578
  105.0 2.3 %collective-permute-start.38 = (f32[24,8,128]{2,1,0:T(8,128)S(1)}, f32[24,8,128]{2,1,0:T(8,128)S(1)}, u32[]{:S(2)}, u32[]{:S(2)}) collective-permute-start(f32[24,8,128]{2,1,0:T(8,128)S(1)} %get-tuple-element.151), channel_id=1, source_target_pairs={{0,32},{32,0},{64,96},{96,64},{128,160},{160,128},{192,224},{224,1... | collective-permute-start | bytes 294920 | tf_op jit(solution)/shard_map/ppermute | solution.py:575
  107.3 3.8 %collective-permute-start.39 = (f32[12,2,8,128]{3,2,1,0:T(8,128)S(1)}, f32[12,2,8,128]{3,2,1,0:T(8,128)S(1)}, u32[]{:S(2)}, u32[]{:S(2)}) collective-permute-start(f32[12,2,8,128]{3,2,1,0:T(8,128)S(1)} %get-tuple-element.152), channel_id=1, source_target_pairs={{0,8},{8,0},{24,16},{16,24},{17,25},{25,17},{9,1},{1,9},{2,10},{10... | collective-permute-start | bytes 294920 | tf_op jit(solution)/shard_map/ppermute | solution.py:577
  111.1 0.3 shard_map.53.refs_0_
  111.4 0.6 collective-permute-done.39.refs_5_
  112.1 1.3 shard_map.54
  113.4 6.0 %all-to-all-start.5 = ((f32[32,8,128]{2,1,0:T(8,128)}), f32[32,8,128]{2,1,0:T(8,128)S(1)}, u32[]{:S(2)}, u32[]{:S(2)}) async-start(f32[32,8,128]{2,1,0:T(8,128)} %get-tuple-element.161), calls=%async_computation.5 | async-start | bytes 262144 | tf_op jit(solution)/shard_map/all_to_all | solution.py:673
  119.4 4.3 %collective-permute-start.40 = (f32[24,8,128]{2,1,0:T(8,128)S(1)}, f32[24,8,128]{2,1,0:T(8,128)S(1)}, u32[]{:S(2)}, u32[]{:S(2)}) collective-permute-start(f32[24,8,128]{2,1,0:T(8,128)S(1)} %get-tuple-element.157), channel_id=1, source_target_pairs={{32,64},{64,32},{96,128},{128,96},{160,192},{192,160},{224,256},{2... | collective-permute-start | bytes 294920 | tf_op jit(solution)/shard_map/ppermute | solution.py:576
  123.7 4.8 %collective-permute-start.41 = (f32[12,2,8,128]{3,2,1,0:T(8,128)S(1)}, f32[12,2,8,128]{3,2,1,0:T(8,128)S(1)}, u32[]{:S(2)}, u32[]{:S(2)}) collective-permute-start(f32[12,2,8,128]{3,2,1,0:T(8,128)S(1)} %get-tuple-element.158), channel_id=1, source_target_pairs={{8,24},{24,8},{16,17},{17,16},{25,9},{9,25},{1,2},{2,1},{10,26},{2... | collective-permute-start | bytes 294920 | tf_op jit(solution)/shard_map/ppermute | solution.py:578
  128.5 1.9 %collective-permute-start.42 = (f32[24,8,128]{2,1,0:T(8,128)S(1)}, f32[24,8,128]{2,1,0:T(8,128)S(1)}, u32[]{:S(2)}, u32[]{:S(2)}) collective-permute-start(f32[24,8,128]{2,1,0:T(8,128)S(1)} %get-tuple-element.159), channel_id=1, source_target_pairs={{0,32},{32,0},{64,96},{96,64},{128,160},{160,128},{192,224},{224,1... | collective-permute-start | bytes 294920 | tf_op jit(solution)/shard_map/ppermute | solution.py:575
  130.4 3.4 %collective-permute-start.43 = (f32[12,2,8,128]{3,2,1,0:T(8,128)S(1)}, f32[12,2,8,128]{3,2,1,0:T(8,128)S(1)}, u32[]{:S(2)}, u32[]{:S(2)}) collective-permute-start(f32[12,2,8,128]{3,2,1,0:T(8,128)S(1)} %get-tuple-element.160), channel_id=1, source_target_pairs={{0,8},{8,0},{24,16},{16,24},{17,25},{25,17},{9,1},{1,9},{2,10},{10... | collective-permute-start | bytes 294920 | tf_op jit(solution)/shard_map/ppermute | solution.py:577
  133.9 0.3 shard_map.55.refs_0_
  134.2 0.6 collective-permute-done.43.refs_5_
  134.8 0.9 shard_map.56
  135.7 7.1 %all-to-all-start.6 = ((f32[16,16,128]{2,1,0:T(8,128)}), f32[16,16,128]{2,1,0:T(8,128)S(1)}, u32[]{:S(2)}, u32[]{:S(2)}) async-start(f32[16,16,128]{2,1,0:T(8,128)} %get-tuple-element.162), calls=%async_computation.6 | async-start | bytes 262144 | tf_op jit(solution)/shard_map/all_to_all | solution.py:677
  142.7 4.5 %collective-permute-start.44 = (f32[24,8,128]{2,1,0:T(8,128)S(1)}, f32[24,8,128]{2,1,0:T(8,128)S(1)}, u32[]{:S(2)}, u32[]{:S(2)}) collective-permute-start(f32[24,8,128]{2,1,0:T(8,128)S(1)} %get-tuple-element.165), channel_id=1, source_target_pairs={{32,64},{64,32},{96,128},{128,96},{160,192},{192,160},{224,256},{2... | collective-permute-start | bytes 294920 | tf_op jit(solution)/shard_map/ppermute | solution.py:576
  147.2 2.2 %collective-permute-start.45 = (f32[12,2,8,128]{3,2,1,0:T(8,128)S(1)}, f32[12,2,8,128]{3,2,1,0:T(8,128)S(1)}, u32[]{:S(2)}, u32[]{:S(2)}) collective-permute-start(f32[12,2,8,128]{3,2,1,0:T(8,128)S(1)} %get-tuple-element.166), channel_id=1, source_target_pairs={{8,24},{24,8},{16,17},{17,16},{25,9},{9,25},{1,2},{2,1},{10,26},{2... | collective-permute-start | bytes 294920 | tf_op jit(solution)/shard_map/ppermute | solution.py:578
  149.4 1.9 %collective-permute-start.46 = (f32[24,8,128]{2,1,0:T(8,128)S(1)}, f32[24,8,128]{2,1,0:T(8,128)S(1)}, u32[]{:S(2)}, u32[]{:S(2)}) collective-permute-start(f32[24,8,128]{2,1,0:T(8,128)S(1)} %get-tuple-element.167), channel_id=1, source_target_pairs={{0,32},{32,0},{64,96},{96,64},{128,160},{160,128},{192,224},{224,1... | collective-permute-start | bytes 294920 | tf_op jit(solution)/shard_map/ppermute | solution.py:575
  151.3 4.3 %collective-permute-start.47 = (f32[12,2,8,128]{3,2,1,0:T(8,128)S(1)}, f32[12,2,8,128]{3,2,1,0:T(8,128)S(1)}, u32[]{:S(2)}, u32[]{:S(2)}) collective-permute-start(f32[12,2,8,128]{3,2,1,0:T(8,128)S(1)} %get-tuple-element.168), channel_id=1, source_target_pairs={{0,8},{8,0},{24,16},{16,24},{17,25},{25,17},{9,1},{1,9},{2,10},{10... | collective-permute-start | bytes 294920 | tf_op jit(solution)/shard_map/ppermute | solution.py:577
  155.6 0.3 shard_map.58
  155.9 2.4 %shard_map.57 = (f32[16,128]{1,0:T(8,128)S(1)}, s32[1]{0:T(128)}) custom-call(f32[16,16,128]{2,1,0:T(8,128)S(1)} %all-to-all-done.6.rows), custom_call_target="tpu_custom_call" | custom-call | flops 100000 | bytes 131072 | tf_op jit(solution)/shard_map/pallas_call | solution.py:33
  159.0 0.9 conditional.1
  159.3 0.7 branch_1_fun.1
  160.0 13.8 %all_to_all.40.received = f32[4,2,96,128]{3,2,1,0:T(8,128)S(1)} all-to-all(f32[4,2,96,128]{3,2,1,0:T(8,128)S(1)} %bitcast.10), channel_id=1, replica_groups=mesh['ta'=16,'gz'=4,'gy'=8] {'gz'}, dimensions={0} | all-to-all | bytes 786432 | tf_op jit(solution)/shard_map/all_to_all | solution.py:689
  173.8 1.4 shard_map.59
  (31 shorter events, 0.5 us)
Async XLA Ops:
  0.6 1.0 copy-start
  1.6 0.9 copy-start.1
  24.2 17.8 %collective-permute-start.16 = (f32[24,8,128]{2,1,0:T(8,128)S(1)}, f32[24,8,128]{2,1,0:T(8,128)S(1)}, u32[]{:S(2)}, u32[]{:S(2)}) collective-permute-start(f32[24,8,128]{2,1,0:T(8,128)S(1)} %get-tuple-element.122), channel_id=1, source_target_pairs={{32,64},{64,32},{96,128},{128,96},{160,192},{192,160},{224,256},{2... | collective-permute-start | bytes 294920 | tf_op jit(solution)/shard_map/ppermute | solution.py:576
  31.7 10.4 %collective-permute-start.17 = (f32[12,2,8,128]{3,2,1,0:T(8,128)S(1)}, f32[12,2,8,128]{3,2,1,0:T(8,128)S(1)}, u32[]{:S(2)}, u32[]{:S(2)}) collective-permute-start(f32[12,2,8,128]{3,2,1,0:T(8,128)S(1)} %get-tuple-element.123), channel_id=1, source_target_pairs={{8,24},{24,8},{16,17},{17,16},{25,9},{9,25},{1,2},{2,1},{10,26},{2... | collective-permute-start | bytes 294920 | tf_op jit(solution)/shard_map/ppermute | solution.py:578
  34.0 8.0 %collective-permute-start.18 = (f32[24,8,128]{2,1,0:T(8,128)S(1)}, f32[24,8,128]{2,1,0:T(8,128)S(1)}, u32[]{:S(2)}, u32[]{:S(2)}) collective-permute-start(f32[24,8,128]{2,1,0:T(8,128)S(1)} %get-tuple-element.124), channel_id=1, source_target_pairs={{0,32},{32,0},{64,96},{96,64},{128,160},{160,128},{192,224},{224,1... | collective-permute-start | bytes 294920 | tf_op jit(solution)/shard_map/ppermute | solution.py:575
  36.0 6.7 %collective-permute-start.19 = (f32[12,2,8,128]{3,2,1,0:T(8,128)S(1)}, f32[12,2,8,128]{3,2,1,0:T(8,128)S(1)}, u32[]{:S(2)}, u32[]{:S(2)}) collective-permute-start(f32[12,2,8,128]{3,2,1,0:T(8,128)S(1)} %get-tuple-element.125), channel_id=1, source_target_pairs={{0,8},{8,0},{24,16},{16,24},{17,25},{25,17},{9,1},{1,9},{2,10},{10... | collective-permute-start | bytes 294920 | tf_op jit(solution)/shard_map/ppermute | solution.py:577
  42.8 11.4 %collective-permute-start.20 = (f32[24,8,128]{2,1,0:T(8,128)S(1)}, f32[24,8,128]{2,1,0:T(8,128)S(1)}, u32[]{:S(2)}, u32[]{:S(2)}) collective-permute-start(f32[24,8,128]{2,1,0:T(8,128)S(1)} %get-tuple-element.127), channel_id=1, source_target_pairs={{32,64},{64,32},{96,128},{128,96},{160,192},{192,160},{224,256},{2... | collective-permute-start | bytes 294920 | tf_op jit(solution)/shard_map/ppermute | solution.py:576
  46.5 7.8 %collective-permute-start.21 = (f32[12,2,8,128]{3,2,1,0:T(8,128)S(1)}, f32[12,2,8,128]{3,2,1,0:T(8,128)S(1)}, u32[]{:S(2)}, u32[]{:S(2)}) collective-permute-start(f32[12,2,8,128]{3,2,1,0:T(8,128)S(1)} %get-tuple-element.128), channel_id=1, source_target_pairs={{8,24},{24,8},{16,17},{17,16},{25,9},{9,25},{1,2},{2,1},{10,26},{2... | collective-permute-start | bytes 294920 | tf_op jit(solution)/shard_map/ppermute | solution.py:578
  48.4 5.9 %collective-permute-start.22 = (f32[24,8,128]{2,1,0:T(8,128)S(1)}, f32[24,8,128]{2,1,0:T(8,128)S(1)}, u32[]{:S(2)}, u32[]{:S(2)}) collective-permute-start(f32[24,8,128]{2,1,0:T(8,128)S(1)} %get-tuple-element.129), channel_id=1, source_target_pairs={{0,32},{32,0},{64,96},{96,64},{128,160},{160,128},{192,224},{224,1... | collective-permute-start | bytes 294920 | tf_op jit(solution)/shard_map/ppermute | solution.py:575
  50.3 4.6 %collective-permute-start.23 = (f32[12,2,8,128]{3,2,1,0:T(8,128)S(1)}, f32[12,2,8,128]{3,2,1,0:T(8,128)S(1)}, u32[]{:S(2)}, u32[]{:S(2)}) collective-permute-start(f32[12,2,8,128]{3,2,1,0:T(8,128)S(1)} %get-tuple-element.130), channel_id=1, source_target_pairs={{0,8},{8,0},{24,16},{16,24},{17,25},{25,17},{9,1},{1,9},{2,10},{10... | collective-permute-start | bytes 294920 | tf_op jit(solution)/shard_map/ppermute | solution.py:577
  55.1 15.4 %collective-permute-start.24 = (f32[24,8,128]{2,1,0:T(8,128)S(1)}, f32[24,8,128]{2,1,0:T(8,128)S(1)}, u32[]{:S(2)}, u32[]{:S(2)}) collective-permute-start(f32[24,8,128]{2,1,0:T(8,128)S(1)} %get-tuple-element.133), channel_id=1, source_target_pairs={{32,64},{64,32},{96,128},{128,96},{160,192},{192,160},{224,256},{2... | collective-permute-start | bytes 294920 | tf_op jit(solution)/shard_map/ppermute | solution.py:576
  59.9 10.6 %collective-permute-start.25 = (f32[12,2,8,128]{3,2,1,0:T(8,128)S(1)}, f32[12,2,8,128]{3,2,1,0:T(8,128)S(1)}, u32[]{:S(2)}, u32[]{:S(2)}) collective-permute-start(f32[12,2,8,128]{3,2,1,0:T(8,128)S(1)} %get-tuple-element.134), channel_id=1, source_target_pairs={{8,24},{24,8},{16,17},{17,16},{25,9},{9,25},{1,2},{2,1},{10,26},{2... | collective-permute-start | bytes 294920 | tf_op jit(solution)/shard_map/ppermute | solution.py:578
  63.2 7.4 %collective-permute-start.26 = (f32[24,8,128]{2,1,0:T(8,128)S(1)}, f32[24,8,128]{2,1,0:T(8,128)S(1)}, u32[]{:S(2)}, u32[]{:S(2)}) collective-permute-start(f32[24,8,128]{2,1,0:T(8,128)S(1)} %get-tuple-element.135), channel_id=1, source_target_pairs={{0,32},{32,0},{64,96},{96,64},{128,160},{160,128},{192,224},{224,1... | collective-permute-start | bytes 294920 | tf_op jit(solution)/shard_map/ppermute | solution.py:575
  65.1 6.0 %collective-permute-start.27 = (f32[12,2,8,128]{3,2,1,0:T(8,128)S(1)}, f32[12,2,8,128]{3,2,1,0:T(8,128)S(1)}, u32[]{:S(2)}, u32[]{:S(2)}) collective-permute-start(f32[12,2,8,128]{3,2,1,0:T(8,128)S(1)} %get-tuple-element.136), channel_id=1, source_target_pairs={{0,8},{8,0},{24,16},{16,24},{17,25},{25,17},{9,1},{1,9},{2,10},{10... | collective-permute-start | bytes 294920 | tf_op jit(solution)/shard_map/ppermute | solution.py:577
  71.3 11.6 %collective-permute-start.28 = (f32[24,8,128]{2,1,0:T(8,128)S(1)}, f32[24,8,128]{2,1,0:T(8,128)S(1)}, u32[]{:S(2)}, u32[]{:S(2)}) collective-permute-start(f32[24,8,128]{2,1,0:T(8,128)S(1)} %get-tuple-element.138), channel_id=1, source_target_pairs={{32,64},{64,32},{96,128},{128,96},{160,192},{192,160},{224,256},{2... | collective-permute-start | bytes 294920 | tf_op jit(solution)/shard_map/ppermute | solution.py:576
  74.6 8.4 %collective-permute-start.29 = (f32[12,2,8,128]{3,2,1,0:T(8,128)S(1)}, f32[12,2,8,128]{3,2,1,0:T(8,128)S(1)}, u32[]{:S(2)}, u32[]{:S(2)}) collective-permute-start(f32[12,2,8,128]{3,2,1,0:T(8,128)S(1)} %get-tuple-element.139), channel_id=1, source_target_pairs={{8,24},{24,8},{16,17},{17,16},{25,9},{9,25},{1,2},{2,1},{10,26},{2... | collective-permute-start | bytes 294920 | tf_op jit(solution)/shard_map/ppermute | solution.py:578
  76.5 6.5 %collective-permute-start.30 = (f32[24,8,128]{2,1,0:T(8,128)S(1)}, f32[24,8,128]{2,1,0:T(8,128)S(1)}, u32[]{:S(2)}, u32[]{:S(2)}) collective-permute-start(f32[24,8,128]{2,1,0:T(8,128)S(1)} %get-tuple-element.140), channel_id=1, source_target_pairs={{0,32},{32,0},{64,96},{96,64},{128,160},{160,128},{192,224},{224,1... | collective-permute-start | bytes 294920 | tf_op jit(solution)/shard_map/ppermute | solution.py:575
  78.8 4.7 %collective-permute-start.31 = (f32[12,2,8,128]{3,2,1,0:T(8,128)S(1)}, f32[12,2,8,128]{3,2,1,0:T(8,128)S(1)}, u32[]{:S(2)}, u32[]{:S(2)}) collective-permute-start(f32[12,2,8,128]{3,2,1,0:T(8,128)S(1)} %get-tuple-element.141), channel_id=1, source_target_pairs={{0,8},{8,0},{24,16},{16,24},{17,25},{25,17},{9,1},{1,9},{2,10},{10... | collective-permute-start | bytes 294920 | tf_op jit(solution)/shard_map/ppermute | solution.py:577
  83.8 15.2 %collective-permute-start.32 = (f32[24,8,128]{2,1,0:T(8,128)S(1)}, f32[24,8,128]{2,1,0:T(8,128)S(1)}, u32[]{:S(2)}, u32[]{:S(2)}) collective-permute-start(f32[24,8,128]{2,1,0:T(8,128)S(1)} %get-tuple-element.144), channel_id=1, source_target_pairs={{32,64},{64,32},{96,128},{128,96},{160,192},{192,160},{224,256},{2... | collective-permute-start | bytes 294920 | tf_op jit(solution)/shard_map/ppermute | solution.py:576
  88.4 10.6 %collective-permute-start.33 = (f32[12,2,8,128]{3,2,1,0:T(8,128)S(1)}, f32[12,2,8,128]{3,2,1,0:T(8,128)S(1)}, u32[]{:S(2)}, u32[]{:S(2)}) collective-permute-start(f32[12,2,8,128]{3,2,1,0:T(8,128)S(1)} %get-tuple-element.145), channel_id=1, source_target_pairs={{8,24},{24,8},{16,17},{17,16},{25,9},{9,25},{1,2},{2,1},{10,26},{2... | collective-permute-start | bytes 294920 | tf_op jit(solution)/shard_map/ppermute | solution.py:578
  91.7 7.4 %collective-permute-start.34 = (f32[24,8,128]{2,1,0:T(8,128)S(1)}, f32[24,8,128]{2,1,0:T(8,128)S(1)}, u32[]{:S(2)}, u32[]{:S(2)}) collective-permute-start(f32[24,8,128]{2,1,0:T(8,128)S(1)} %get-tuple-element.146), channel_id=1, source_target_pairs={{0,32},{32,0},{64,96},{96,64},{128,160},{160,128},{192,224},{224,1... | collective-permute-start | bytes 294920 | tf_op jit(solution)/shard_map/ppermute | solution.py:575
  93.6 6.0 %collective-permute-start.35 = (f32[12,2,8,128]{3,2,1,0:T(8,128)S(1)}, f32[12,2,8,128]{3,2,1,0:T(8,128)S(1)}, u32[]{:S(2)}, u32[]{:S(2)}) collective-permute-start(f32[12,2,8,128]{3,2,1,0:T(8,128)S(1)} %get-tuple-element.147), channel_id=1, source_target_pairs={{0,8},{8,0},{24,16},{16,24},{17,25},{25,17},{9,1},{1,9},{2,10},{10... | collective-permute-start | bytes 294920 | tf_op jit(solution)/shard_map/ppermute | solution.py:577
  99.8 11.6 %collective-permute-start.36 = (f32[24,8,128]{2,1,0:T(8,128)S(1)}, f32[24,8,128]{2,1,0:T(8,128)S(1)}, u32[]{:S(2)}, u32[]{:S(2)}) collective-permute-start(f32[24,8,128]{2,1,0:T(8,128)S(1)} %get-tuple-element.149), channel_id=1, source_target_pairs={{32,64},{64,32},{96,128},{128,96},{160,192},{192,160},{224,256},{2... | collective-permute-start | bytes 294920 | tf_op jit(solution)/shard_map/ppermute | solution.py:576
  103.1 8.4 %collective-permute-start.37 = (f32[12,2,8,128]{3,2,1,0:T(8,128)S(1)}, f32[12,2,8,128]{3,2,1,0:T(8,128)S(1)}, u32[]{:S(2)}, u32[]{:S(2)}) collective-permute-start(f32[12,2,8,128]{3,2,1,0:T(8,128)S(1)} %get-tuple-element.150), channel_id=1, source_target_pairs={{8,24},{24,8},{16,17},{17,16},{25,9},{9,25},{1,2},{2,1},{10,26},{2... | collective-permute-start | bytes 294920 | tf_op jit(solution)/shard_map/ppermute | solution.py:578
  105.0 6.5 %collective-permute-start.38 = (f32[24,8,128]{2,1,0:T(8,128)S(1)}, f32[24,8,128]{2,1,0:T(8,128)S(1)}, u32[]{:S(2)}, u32[]{:S(2)}) collective-permute-start(f32[24,8,128]{2,1,0:T(8,128)S(1)} %get-tuple-element.151), channel_id=1, source_target_pairs={{0,32},{32,0},{64,96},{96,64},{128,160},{160,128},{192,224},{224,1... | collective-permute-start | bytes 294920 | tf_op jit(solution)/shard_map/ppermute | solution.py:575
  107.3 4.7 %collective-permute-start.39 = (f32[12,2,8,128]{3,2,1,0:T(8,128)S(1)}, f32[12,2,8,128]{3,2,1,0:T(8,128)S(1)}, u32[]{:S(2)}, u32[]{:S(2)}) collective-permute-start(f32[12,2,8,128]{3,2,1,0:T(8,128)S(1)} %get-tuple-element.152), channel_id=1, source_target_pairs={{0,8},{8,0},{24,16},{16,24},{17,25},{25,17},{9,1},{1,9},{2,10},{10... | collective-permute-start | bytes 294920 | tf_op jit(solution)/shard_map/ppermute | solution.py:577
  113.4 21.4 %all-to-all-start.5 = ((f32[32,8,128]{2,1,0:T(8,128)}), f32[32,8,128]{2,1,0:T(8,128)S(1)}, u32[]{:S(2)}, u32[]{:S(2)}) async-start(f32[32,8,128]{2,1,0:T(8,128)} %get-tuple-element.161), calls=%async_computation.5 | async-start | bytes 262144 | tf_op jit(solution)/shard_map/all_to_all | solution.py:673
  119.4 14.7 %collective-permute-start.40 = (f32[24,8,128]{2,1,0:T(8,128)S(1)}, f32[24,8,128]{2,1,0:T(8,128)S(1)}, u32[]{:S(2)}, u32[]{:S(2)}) collective-permute-start(f32[24,8,128]{2,1,0:T(8,128)S(1)} %get-tuple-element.157), channel_id=1, source_target_pairs={{32,64},{64,32},{96,128},{128,96},{160,192},{192,160},{224,256},{2... | collective-permute-start | bytes 294920 | tf_op jit(solution)/shard_map/ppermute | solution.py:576
  123.7 10.5 %collective-permute-start.41 = (f32[12,2,8,128]{3,2,1,0:T(8,128)S(1)}, f32[12,2,8,128]{3,2,1,0:T(8,128)S(1)}, u32[]{:S(2)}, u32[]{:S(2)}) collective-permute-start(f32[12,2,8,128]{3,2,1,0:T(8,128)S(1)} %get-tuple-element.158), channel_id=1, source_target_pairs={{8,24},{24,8},{16,17},{17,16},{25,9},{9,25},{1,2},{2,1},{10,26},{2... | collective-permute-start | bytes 294920 | tf_op jit(solution)/shard_map/ppermute | solution.py:578
  128.5 5.6 %collective-permute-start.42 = (f32[24,8,128]{2,1,0:T(8,128)S(1)}, f32[24,8,128]{2,1,0:T(8,128)S(1)}, u32[]{:S(2)}, u32[]{:S(2)}) collective-permute-start(f32[24,8,128]{2,1,0:T(8,128)S(1)} %get-tuple-element.159), channel_id=1, source_target_pairs={{0,32},{32,0},{64,96},{96,64},{128,160},{160,128},{192,224},{224,1... | collective-permute-start | bytes 294920 | tf_op jit(solution)/shard_map/ppermute | solution.py:575
  130.4 4.3 %collective-permute-start.43 = (f32[12,2,8,128]{3,2,1,0:T(8,128)S(1)}, f32[12,2,8,128]{3,2,1,0:T(8,128)S(1)}, u32[]{:S(2)}, u32[]{:S(2)}) collective-permute-start(f32[12,2,8,128]{3,2,1,0:T(8,128)S(1)} %get-tuple-element.160), channel_id=1, source_target_pairs={{0,8},{8,0},{24,16},{16,24},{17,25},{25,17},{9,1},{1,9},{2,10},{10... | collective-permute-start | bytes 294920 | tf_op jit(solution)/shard_map/ppermute | solution.py:577
  135.7 20.3 %all-to-all-start.6 = ((f32[16,16,128]{2,1,0:T(8,128)}), f32[16,16,128]{2,1,0:T(8,128)S(1)}, u32[]{:S(2)}, u32[]{:S(2)}) async-start(f32[16,16,128]{2,1,0:T(8,128)} %get-tuple-element.162), calls=%async_computation.6 | async-start | bytes 262144 | tf_op jit(solution)/shard_map/all_to_all | solution.py:677
  142.7 16.3 %collective-permute-start.44 = (f32[24,8,128]{2,1,0:T(8,128)S(1)}, f32[24,8,128]{2,1,0:T(8,128)S(1)}, u32[]{:S(2)}, u32[]{:S(2)}) collective-permute-start(f32[24,8,128]{2,1,0:T(8,128)S(1)} %get-tuple-element.165), channel_id=1, source_target_pairs={{32,64},{64,32},{96,128},{128,96},{160,192},{192,160},{224,256},{2... | collective-permute-start | bytes 294920 | tf_op jit(solution)/shard_map/ppermute | solution.py:576
  147.2 11.8 %collective-permute-start.45 = (f32[12,2,8,128]{3,2,1,0:T(8,128)S(1)}, f32[12,2,8,128]{3,2,1,0:T(8,128)S(1)}, u32[]{:S(2)}, u32[]{:S(2)}) collective-permute-start(f32[12,2,8,128]{3,2,1,0:T(8,128)S(1)} %get-tuple-element.166), channel_id=1, source_target_pairs={{8,24},{24,8},{16,17},{17,16},{25,9},{9,25},{1,2},{2,1},{10,26},{2... | collective-permute-start | bytes 294920 | tf_op jit(solution)/shard_map/ppermute | solution.py:578
  149.4 9.6 %collective-permute-start.46 = (f32[24,8,128]{2,1,0:T(8,128)S(1)}, f32[24,8,128]{2,1,0:T(8,128)S(1)}, u32[]{:S(2)}, u32[]{:S(2)}) collective-permute-start(f32[24,8,128]{2,1,0:T(8,128)S(1)} %get-tuple-element.167), channel_id=1, source_target_pairs={{0,32},{32,0},{64,96},{96,64},{128,160},{160,128},{192,224},{224,1... | collective-permute-start | bytes 294920 | tf_op jit(solution)/shard_map/ppermute | solution.py:575
  151.3 7.7 %collective-permute-start.47 = (f32[12,2,8,128]{3,2,1,0:T(8,128)S(1)}, f32[12,2,8,128]{3,2,1,0:T(8,128)S(1)}, u32[]{:S(2)}, u32[]{:S(2)}) collective-permute-start(f32[12,2,8,128]{3,2,1,0:T(8,128)S(1)} %get-tuple-element.168), channel_id=1, source_target_pairs={{0,8},{8,0},{24,16},{16,24},{17,25},{25,17},{9,1},{1,9},{2,10},{10... | collective-permute-start | bytes 294920 | tf_op jit(solution)/shard_map/ppermute | solution.py:577

commit v4 on v3

--- a/solution.py
+++ b/solution.py
@@ -21,9 +21,10 @@
 PIVOT_GUARD = 1e-3
 VMEM = pl.BlockSpec(memory_space=pltpu.VMEM)
 SMEM = pl.BlockSpec(memory_space=pltpu.SMEM)
-
-
-def call(body, outs, args, flops=10**6, scratch=(), flag=False):
+HBM = pl.BlockSpec(memory_space=pltpu.HBM)
+
+
+def call(body, outs, args, flops=10**6, scratch=(), flag=False, inputs=VMEM):
     shapes = [jax.ShapeDtypeStruct(s, F32) for s in outs]
     out_specs = [VMEM] * len(shapes)
     if flag:
@@ -33,7 +34,7 @@
     return pl.pallas_call(
         body,
         out_shape=shapes,
-        in_specs=[VMEM] * len(args),
+        in_specs=[inputs] * len(args),
         out_specs=out_specs,
         scratch_shapes=scratch,
         compiler_params=pltpu.CompilerParams(vmem_limit_bytes=16 * 2**20),
@@ -78,9 +79,17 @@
     return jnp.where(block_odd == 1, ROW_OWNER[1][row], ROW_OWNER[0][row])
 
 
-def pack_body(sources, links, out):
+def pack_body(sources, links, out, sources_here, links_here, done):
     block_odd = place()[4]
-    for ref, base, chunks in ((sources, 0, 6), (links, 48, 9)):
+    copies = [
+        pltpu.make_async_copy(sources, sources_here, done.at[0]),
+        pltpu.make_async_copy(links, links_here, done.at[1]),
+    ]
+    for copy in copies:
+        copy.start()
+    parts = ((sources_here, 0, 6), (links_here, 48, 9))
+    for copy, (ref, base, chunks) in zip(copies, parts):
+        copy.wait()
         for z in range(2):
             for i in range(chunks):
                 tiles = [ref[s, pl.ds(16 * i + z, 8, stride=2), :] for s in range(4)]
@@ -443,6 +452,15 @@
         for part in range(2):
             row = jnp.sum(jnp.where(here, c[part], 0.0), axis=0, keepdims=True)
             out[base + 2 * d + part : base + 2 * d + part + 1, :] = row
+
+
+def write_table(out, base, c):
+    group = group_of_lane()
+    for part in range(2):
+        for j in range(4):
+            x = jnp.where(group == j, c[part], 0.0)
+            x = x + roll_lanes(x, 64)
+            out[base + 4 * part + j] = x + roll_lanes(x, 32)
 
 
 def coefficients_body(rows, out, good_out):
@@ -469,8 +487,8 @@
     _, good3 = solve(rho, unit_pair(unit), GUARD * rho_size)
     q = matmul(alpha, alpha1)
     k = add(alpha, matmul(p, alpha1))
-    write_coefficients(out, 0, k)
-    write_coefficients(out, 8, q)
+    write_table(out, 0, k)
+    write_table(out, 8, q)
     good = good0 & good1 & good2 & good3
     good_out[0] = jnp.min(jnp.where(good, 1, 0))
 
@@ -506,24 +524,52 @@
             out[12 + c, t] = signed_add(x[12 + c, t], im, sign)
 
 
-def final_body(partial, links, *refs):
+def send_body(partial, links, *refs):
     recv = in_face_order(refs[:4])
-    base, first, image, rows, out = refs[4:]
+    base, image, out = refs[4:]
     for t in range(2):
+        for c in range(24):
+            out[pl.ds(2 * c + t, 8, stride=96), :] = image[c, t]
         b = finished_spinor(partial, links, 0, t, recv, base)
-        for s in range(4):
-            for c in range(3):
-                at = s * 3 + c
-                re, im = first[at, t], first[12 + at, t]
-                image_re, image_im = image[at, t], image[12 + at, t]
-                rk = mix(re, im, rows, 0)
-                ak = mix(image_re, image_im, rows, 0)
-                aq = mix(image_re, image_im, rows, 8)
-                bq = mix(b[0][s][c], b[1][s][c], rows, 8)
-                out[pl.ds(2 * at + t, 8, stride=96), :] = rk[0] - aq[0]
-                out[pl.ds(2 * (12 + at) + t, 8, stride=96), :] = rk[1] - aq[1]
-                out[pl.ds(48 + 2 * at + t, 8, stride=96), :] = re - ak[0] + bq[0]
-                out[pl.ds(48 + 2 * (12 + at) + t, 8, stride=96), :] = im - ak[1] + bq[1]
+        for p in range(2):
+            for s in range(4):
+                for c in range(3):
+                    at = (p * 4 + s) * 3 + c
+                    out[pl.ds(48 + 2 * at + t, 8, stride=96), :] = b[p][s][c]
+
+
+def returned(received, block_odd, z, at):
+    return swap_groups([received[owner(block_odd, r), z, at : at + 8, :] for r in range(4)])
+
+
+def weighted(total, re, im, table, base, j, sign):
+    for i in range(4):
+        cr = table[base + j, i : i + 1, :]
+        ci = table[base + 4 + j, i : i + 1, :]
+        real, imag = re[i] * cr - im[i] * ci, re[i] * ci + im[i] * cr
+        if total is None:
+            total = (real, imag)
+        else:
+            total = (signed_add(total[0], real, sign), signed_add(total[1], imag, sign))
+    return total
+
+
+def final_body(sources, received, table, solution_ref, residual_ref):
+    block_odd = place()[4]
+    for z in range(2):
+        for n in range(3):
+            rows = [pl.ds(16 * (n + 3 * part) + z, 8, stride=2) for part in range(2)]
+            r = [[sources[s, rows[part], :] for s in range(4)] for part in range(2)]
+            a = [returned(received, block_odd, z, 8 * (n + 3 * part)) for part in range(2)]
+            b = [returned(received, block_odd, z, 48 + 8 * (n + 3 * part)) for part in range(2)]
+            for j in range(4):
+                x = weighted(None, r[0], r[1], table, 0, j, 1)
+                x = weighted(x, a[0], a[1], table, 8, j, -1)
+                y = weighted((r[0][j], r[1][j]), a[0], a[1], table, 0, j, -1)
+                y = weighted(y, b[0], b[1], table, 8, j, 1)
+                for part in range(2):
+                    solution_ref[j, rows[part], :] = x[part]
+                    residual_ref[j, rows[part], :] = y[part]
 
 
 def send_order_body(solution_ref, residual_ref, out):
@@ -538,15 +584,14 @@
     for i, ref in enumerate((solution_ref, residual_ref)):
         for z in range(2):
             for n in range(6):
-                at = 48 * i + 8 * n
-                tiles = [received[owner(block_odd, row), z, at : at + 8, :] for row in range(4)]
-                for s, tile in enumerate(swap_groups(tiles)):
+                for s, tile in enumerate(returned(received, block_odd, z, 48 * i + 8 * n)):
                     ref[s, pl.ds(16 * n + z, 8, stride=2), :] = tile
 
 
 SPINOR = (24, 2, 8, 128)
+ORIGINAL = (4, 96, 128)
 FACES = [(24, 8, 128), (24, 8, 128), (12, 2, 8, 128), (12, 2, 8, 128)]
-START_ORDER = (1, 3, 0, 2)
+START_ORDER = (3, 1, 0, 2)
 
 
 def in_start_order(faces):
@@ -628,6 +673,10 @@
         write_faces(spinor, links, 1, faces)
 
     return call(body, FACES, (spinor, links))
+
+
+def give_back(out):
+    return lax.all_to_all(out.reshape(4, 2, 96, 128), "gz", 0, 0)
 
 
 def direct_branch(links, first, image, rows):
@@ -656,12 +705,15 @@
     zero = jnp.zeros(SPINOR, F32)
     solution_field = combine(1, combine(1, zero, first, alpha), search, alpha1)
     residual = combine(-1, residual, images, alpha1)
-    return call(send_order_body, [(768, 128)], (solution_field, residual))[0]
+    (out,) = call(send_order_body, [(768, 128)], (solution_field, residual))
+    return tuple(call(deliver_body, [ORIGINAL] * 2, (give_back(out),)))
 
 
 def local(sources, gauge_links):
-    args = (sources.reshape(4, 96, 128), gauge_links.reshape(4, 144, 128))
-    (packed,) = call(pack_body, [(4, 2, 120, 128)], args)
+    flat = sources.reshape(ORIGINAL)
+    here = [pltpu.VMEM(ORIGINAL, F32), pltpu.VMEM((4, 144, 128), F32), pltpu.SemaphoreType.DMA((2,))]
+    args = (flat, gauge_links.reshape(4, 144, 128))
+    (packed,) = call(pack_body, [(4, 2, 120, 128)], args, scratch=here, inputs=HBM)
     received = lax.all_to_all(packed, "gz", 0, 0).reshape(960, 128)
     links, first, *faces = call(unpack_body, [(144, 2, 8, 128), SPINOR] + FACES, (received,))
     half1, faces, moments0 = half_normal(first, faces, links, True)
@@ -677,17 +729,14 @@
     rows = lax.all_to_all(rows, "ta", 0, 0, tiled=True)
     recv = exchange(faces)
     (partial,) = hop_inner(odd, links, 0)
-    table, good = call(coefficients_body, [(16, 128)], (rows,), 10**5, flag=True)
-
-    def moment_branch():
-        given = (partial, links, *in_start_order(recv), half2, first, image, table)
-        return call(final_body, [(768, 128)], given, 10**7)[0]
-
-    out = lax.cond(
-        good[0] == 1, moment_branch, lambda: direct_branch(links, first, image, rows)
+    given = (partial, links, *in_start_order(recv), half2, image)
+    received = give_back(call(send_body, [(768, 128)], given, 10**7)[0])
+    table, good = call(coefficients_body, [(16, 8, 128)], (rows,), 10**5, flag=True)
+    done = lax.cond(
+        good[0] == 1,
+        lambda: tuple(call(final_body, [ORIGINAL] * 2, (flat, received, table))),
+        lambda: direct_branch(links, first, image, rows),
     )
-    received = lax.all_to_all(out.reshape(4, 2, 96, 128), "gz", 0, 0)
-    done = call(deliver_body, [(4, 96, 128)] * 2, (received,))
     return tuple(x.reshape(sources.shape) for x in done)
 
 

time: 176 us -> 173 us (0.983)
  blocking collectives: 32.1 us -> 18.3 us
  waiting for transfers between devices: 4.17 us -> 9.79 us
  starting transfers between devices: 121 us -> 126 us
    all_to_all x1 -> x0, blocking collectives: 13.8 us -> none  [local(): received = lax.all_to_all(out.reshape(4, 2, 96, 128), 'gz', 0, 0)]
    all_to_all x0 -> x1, waiting for transfers between devices: none -> 5 us  [give_back(): return lax.all_to_all(out.reshape(4, 2, 96, 128), 'gz', 0, 0)]
    all_to_all x0 -> x1, starting transfers between devices: none -> 4.94 us  [give_back(): return lax.all_to_all(out.reshape(4, 2, 96, 128), 'gz', 0, 0)]
  transfers between devices with their start and end apart: 34 -> 35, of which waited for: 7 -> 9; matrix products, arithmetic and copies ran while one was open for 0% -> 0% of each run, Pallas kernels for 3% -> 3%
where the time goes in v4:
time: 173 us; the launch traced here: 171 us
  starting transfers between devices  126 us (73%)
  blocking collectives  18.3 us (11%)
  Pallas kernels  14.1 us (8%)
  waiting for transfers between devices  9.79 us (6%)
  between operations  1.86 us (1%)
    ppermute x8, starting transfers between devices, exchange(): lax.ppermute(row_a, ('gz', 'gy'), make_pairs(rows, 0))  34.8 us
    ppermute x8, starting transfers between devices, exchange(): lax.ppermute(time_b, 'ta', make_pairs(times, 1))  34.3 us
    ppermute x8, starting transfers between devices, exchange(): lax.ppermute(row_b, ('gz', 'gy'), make_pairs(rows, 1))  23 us
    all_to_all x1, blocking collectives, local(): received = lax.all_to_all(packed, 'gz', 0, 0).reshape(960, 128)  18.3 us
    ppermute x8, starting transfers between devices, exchange(): lax.ppermute(time_a, 'ta', make_pairs(times, 0))  16.2 us
    pallas_call x20, Pallas kernels, call(): pl.pallas_call(body, out_shape=shapes, in_specs=[inputs] * len(args), out...  14.1 us
    all_to_all x1, starting transfers between devices, local(): rows = lax.all_to_all(rows, 'ta', 0, 0, tiled=True)  7.06 us
    all_to_all x1, starting transfers between devices, local(): rows = lax.all_to_all(rows, ('gz', 'gy'), 0, 0, tiled=True)  6.03 us
  transfers between devices with their start and end apart: 35, of which 9 were waited for; matrix products, arithmetic and copies ran while one was open for 0% of the time, Pallas kernels for 3%

profile of v4, /device:TPU:1, one launch (start us, length us, event | category | flops | bytes accessed | tf_op | source)
XLA Modules:
  0.0 171.4 jit_solution(10782014962374739450)
XLA Ops:
  0.6 1.0 copy-done
  1.6 1.5 shard_map.41
  3.1 18.3 %all_to_all.44 = f32[4,2,120,128]{3,2,1,0:T(8,128)S(1)} all-to-all(f32[4,2,120,128]{3,2,1,0:T(8,128)S(1)} %shard_map.41), channel_id=1, replica_groups=mesh['ta'=16,'gz'=4,'gy'=8] {'gz'}, dimensions={0} | all-to-all | bytes 983040 | tf_op jit(solution)/shard_map/all_to_all | solution.py:717
  21.4 2.0 %shard_map.42 = (f32[144,2,8,128]{3,2,1,0:T(8,128)S(1)}, f32[24,2,8,128]{3,2,1,0:T(8,128)S(1)}, f32[24,8,128]{2,1,0:T(8,128)S(1)}, f32[24,8,128]{2,1,0:T(8,128)S...) custom-call(f32[960,128]{1,0:T(8,128)S(1)} %bitcast.8), custom_call_target="tpu_custom_call" | custom-call | flops 1000000 | bytes 491520 | tf_op jit(solution)/shard_map/pallas_call | solution.py:34
  23.4 2.3 %collective-permute-start.16 = (f32[12,2,8,128]{3,2,1,0:T(8,128)S(1)}, f32[12,2,8,128]{3,2,1,0:T(8,128)S(1)}, u32[]{:S(2)}, u32[]{:S(2)}) collective-permute-start(f32[12,2,8,128]{3,2,1,0:T(8,128)S(1)} %get-tuple-element.106), channel_id=1, source_target_pairs={{8,24},{24,8},{16,17},{17,16},{25,9},{9,25},{1,2},{2,1},{10,26},{2... | collective-permute-start | bytes 294920 | tf_op jit(solution)/shard_map/ppermute | solution.py:623
  25.8 7.5 %collective-permute-start.17 = (f32[24,8,128]{2,1,0:T(8,128)S(1)}, f32[24,8,128]{2,1,0:T(8,128)S(1)}, u32[]{:S(2)}, u32[]{:S(2)}) collective-permute-start(f32[24,8,128]{2,1,0:T(8,128)S(1)} %get-tuple-element.107), channel_id=1, source_target_pairs={{32,64},{64,32},{96,128},{128,96},{160,192},{192,160},{224,256},{2... | collective-permute-start | bytes 294920 | tf_op jit(solution)/shard_map/ppermute | solution.py:621
  33.3 1.9 %collective-permute-start.18 = (f32[24,8,128]{2,1,0:T(8,128)S(1)}, f32[24,8,128]{2,1,0:T(8,128)S(1)}, u32[]{:S(2)}, u32[]{:S(2)}) collective-permute-start(f32[24,8,128]{2,1,0:T(8,128)S(1)} %get-tuple-element.108), channel_id=1, source_target_pairs={{0,32},{32,0},{64,96},{96,64},{128,160},{160,128},{192,224},{224,1... | collective-permute-start | bytes 294920 | tf_op jit(solution)/shard_map/ppermute | solution.py:620
  35.2 5.7 %collective-permute-start.19 = (f32[12,2,8,128]{3,2,1,0:T(8,128)S(1)}, f32[12,2,8,128]{3,2,1,0:T(8,128)S(1)}, u32[]{:S(2)}, u32[]{:S(2)}) collective-permute-start(f32[12,2,8,128]{3,2,1,0:T(8,128)S(1)} %get-tuple-element.109), channel_id=1, source_target_pairs={{0,8},{8,0},{24,16},{16,24},{17,25},{25,17},{9,1},{1,9},{2,10},{10... | collective-permute-start | bytes 294920 | tf_op jit(solution)/shard_map/ppermute | solution.py:622
  40.9 0.3 shard_map.43
  41.3 0.5 collective-permute-done.19.refs_5_
  42.1 2.5 %collective-permute-start.20 = (f32[12,2,8,128]{3,2,1,0:T(8,128)S(1)}, f32[12,2,8,128]{3,2,1,0:T(8,128)S(1)}, u32[]{:S(2)}, u32[]{:S(2)}) collective-permute-start(f32[12,2,8,128]{3,2,1,0:T(8,128)S(1)} %get-tuple-element.111), channel_id=1, source_target_pairs={{8,24},{24,8},{16,17},{17,16},{25,9},{9,25},{1,2},{2,1},{10,26},{2... | collective-permute-start | bytes 294920 | tf_op jit(solution)/shard_map/ppermute | solution.py:623
  44.6 3.0 %collective-permute-start.21 = (f32[24,8,128]{2,1,0:T(8,128)S(1)}, f32[24,8,128]{2,1,0:T(8,128)S(1)}, u32[]{:S(2)}, u32[]{:S(2)}) collective-permute-start(f32[24,8,128]{2,1,0:T(8,128)S(1)} %get-tuple-element.112), channel_id=1, source_target_pairs={{32,64},{64,32},{96,128},{128,96},{160,192},{192,160},{224,256},{2... | collective-permute-start | bytes 294920 | tf_op jit(solution)/shard_map/ppermute | solution.py:621
  47.6 1.9 %collective-permute-start.22 = (f32[24,8,128]{2,1,0:T(8,128)S(1)}, f32[24,8,128]{2,1,0:T(8,128)S(1)}, u32[]{:S(2)}, u32[]{:S(2)}) collective-permute-start(f32[24,8,128]{2,1,0:T(8,128)S(1)} %get-tuple-element.113), channel_id=1, source_target_pairs={{0,32},{32,0},{64,96},{96,64},{128,160},{160,128},{192,224},{224,1... | collective-permute-start | bytes 294920 | tf_op jit(solution)/shard_map/ppermute | solution.py:620
  49.6 3.6 %collective-permute-start.23 = (f32[12,2,8,128]{3,2,1,0:T(8,128)S(1)}, f32[12,2,8,128]{3,2,1,0:T(8,128)S(1)}, u32[]{:S(2)}, u32[]{:S(2)}) collective-permute-start(f32[12,2,8,128]{3,2,1,0:T(8,128)S(1)} %get-tuple-element.114), channel_id=1, source_target_pairs={{0,8},{8,0},{24,16},{16,24},{17,25},{25,17},{9,1},{1,9},{2,10},{10... | collective-permute-start | bytes 294920 | tf_op jit(solution)/shard_map/ppermute | solution.py:622
  53.2 0.3 shard_map.45.refs_0_
  53.5 0.6 collective-permute-done.23.refs_5_
  54.1 0.2 shard_map.46
  54.4 3.7 %collective-permute-start.24 = (f32[12,2,8,128]{3,2,1,0:T(8,128)S(1)}, f32[12,2,8,128]{3,2,1,0:T(8,128)S(1)}, u32[]{:S(2)}, u32[]{:S(2)}) collective-permute-start(f32[12,2,8,128]{3,2,1,0:T(8,128)S(1)} %get-tuple-element.117), channel_id=1, source_target_pairs={{8,24},{24,8},{16,17},{17,16},{25,9},{9,25},{1,2},{2,1},{10,26},{2... | collective-permute-start | bytes 294920 | tf_op jit(solution)/shard_map/ppermute | solution.py:623
  58.1 4.3 %collective-permute-start.25 = (f32[24,8,128]{2,1,0:T(8,128)S(1)}, f32[24,8,128]{2,1,0:T(8,128)S(1)}, u32[]{:S(2)}, u32[]{:S(2)}) collective-permute-start(f32[24,8,128]{2,1,0:T(8,128)S(1)} %get-tuple-element.118), channel_id=1, source_target_pairs={{32,64},{64,32},{96,128},{128,96},{160,192},{192,160},{224,256},{2... | collective-permute-start | bytes 294920 | tf_op jit(solution)/shard_map/ppermute | solution.py:621
  62.4 1.9 %collective-permute-start.26 = (f32[24,8,128]{2,1,0:T(8,128)S(1)}, f32[24,8,128]{2,1,0:T(8,128)S(1)}, u32[]{:S(2)}, u32[]{:S(2)}) collective-permute-start(f32[24,8,128]{2,1,0:T(8,128)S(1)} %get-tuple-element.119), channel_id=1, source_target_pairs={{0,32},{32,0},{64,96},{96,64},{128,160},{160,128},{192,224},{224,1... | collective-permute-start | bytes 294920 | tf_op jit(solution)/shard_map/ppermute | solution.py:620
  64.4 5.1 %collective-permute-start.27 = (f32[12,2,8,128]{3,2,1,0:T(8,128)S(1)}, f32[12,2,8,128]{3,2,1,0:T(8,128)S(1)}, u32[]{:S(2)}, u32[]{:S(2)}) collective-permute-start(f32[12,2,8,128]{3,2,1,0:T(8,128)S(1)} %get-tuple-element.120), channel_id=1, source_target_pairs={{0,8},{8,0},{24,16},{16,24},{17,25},{25,17},{9,1},{1,9},{2,10},{10... | collective-permute-start | bytes 294920 | tf_op jit(solution)/shard_map/ppermute | solution.py:622
  69.4 0.3 shard_map.47
  69.8 0.5 collective-permute-done.27.refs_5_
  70.6 2.2 %collective-permute-start.28 = (f32[12,2,8,128]{3,2,1,0:T(8,128)S(1)}, f32[12,2,8,128]{3,2,1,0:T(8,128)S(1)}, u32[]{:S(2)}, u32[]{:S(2)}) collective-permute-start(f32[12,2,8,128]{3,2,1,0:T(8,128)S(1)} %get-tuple-element.122), channel_id=1, source_target_pairs={{8,24},{24,8},{16,17},{17,16},{25,9},{9,25},{1,2},{2,1},{10,26},{2... | collective-permute-start | bytes 294920 | tf_op jit(solution)/shard_map/ppermute | solution.py:623
  72.7 3.0 %collective-permute-start.29 = (f32[24,8,128]{2,1,0:T(8,128)S(1)}, f32[24,8,128]{2,1,0:T(8,128)S(1)}, u32[]{:S(2)}, u32[]{:S(2)}) collective-permute-start(f32[24,8,128]{2,1,0:T(8,128)S(1)} %get-tuple-element.123), channel_id=1, source_target_pairs={{32,64},{64,32},{96,128},{128,96},{160,192},{192,160},{224,256},{2... | collective-permute-start | bytes 294920 | tf_op jit(solution)/shard_map/ppermute | solution.py:621
  75.7 2.3 %collective-permute-start.30 = (f32[24,8,128]{2,1,0:T(8,128)S(1)}, f32[24,8,128]{2,1,0:T(8,128)S(1)}, u32[]{:S(2)}, u32[]{:S(2)}) collective-permute-start(f32[24,8,128]{2,1,0:T(8,128)S(1)} %get-tuple-element.124), channel_id=1, source_target_pairs={{0,32},{32,0},{64,96},{96,64},{128,160},{160,128},{192,224},{224,1... | collective-permute-start | bytes 294920 | tf_op jit(solution)/shard_map/ppermute | solution.py:620
  78.1 3.8 %collective-permute-start.31 = (f32[12,2,8,128]{3,2,1,0:T(8,128)S(1)}, f32[12,2,8,128]{3,2,1,0:T(8,128)S(1)}, u32[]{:S(2)}, u32[]{:S(2)}) collective-permute-start(f32[12,2,8,128]{3,2,1,0:T(8,128)S(1)} %get-tuple-element.125), channel_id=1, source_target_pairs={{0,8},{8,0},{24,16},{16,24},{17,25},{25,17},{9,1},{1,9},{2,10},{10... | collective-permute-start | bytes 294920 | tf_op jit(solution)/shard_map/ppermute | solution.py:622
  81.9 0.3 shard_map.49.refs_0_
  82.2 0.6 collective-permute-done.31.refs_5_
  82.8 0.2 shard_map.50
  83.0 3.3 %collective-permute-start.32 = (f32[12,2,8,128]{3,2,1,0:T(8,128)S(1)}, f32[12,2,8,128]{3,2,1,0:T(8,128)S(1)}, u32[]{:S(2)}, u32[]{:S(2)}) collective-permute-start(f32[12,2,8,128]{3,2,1,0:T(8,128)S(1)} %get-tuple-element.128), channel_id=1, source_target_pairs={{8,24},{24,8},{16,17},{17,16},{25,9},{9,25},{1,2},{2,1},{10,26},{2... | collective-permute-start | bytes 294920 | tf_op jit(solution)/shard_map/ppermute | solution.py:623
  86.3 4.6 %collective-permute-start.33 = (f32[24,8,128]{2,1,0:T(8,128)S(1)}, f32[24,8,128]{2,1,0:T(8,128)S(1)}, u32[]{:S(2)}, u32[]{:S(2)}) collective-permute-start(f32[24,8,128]{2,1,0:T(8,128)S(1)} %get-tuple-element.129), channel_id=1, source_target_pairs={{32,64},{64,32},{96,128},{128,96},{160,192},{192,160},{224,256},{2... | collective-permute-start | bytes 294920 | tf_op jit(solution)/shard_map/ppermute | solution.py:621
  90.9 1.9 %collective-permute-start.34 = (f32[24,8,128]{2,1,0:T(8,128)S(1)}, f32[24,8,128]{2,1,0:T(8,128)S(1)}, u32[]{:S(2)}, u32[]{:S(2)}) collective-permute-start(f32[24,8,128]{2,1,0:T(8,128)S(1)} %get-tuple-element.130), channel_id=1, source_target_pairs={{0,32},{32,0},{64,96},{96,64},{128,160},{160,128},{192,224},{224,1... | collective-permute-start | bytes 294920 | tf_op jit(solution)/shard_map/ppermute | solution.py:620
  92.8 5.1 %collective-permute-start.35 = (f32[12,2,8,128]{3,2,1,0:T(8,128)S(1)}, f32[12,2,8,128]{3,2,1,0:T(8,128)S(1)}, u32[]{:S(2)}, u32[]{:S(2)}) collective-permute-start(f32[12,2,8,128]{3,2,1,0:T(8,128)S(1)} %get-tuple-element.131), channel_id=1, source_target_pairs={{0,8},{8,0},{24,16},{16,24},{17,25},{25,17},{9,1},{1,9},{2,10},{10... | collective-permute-start | bytes 294920 | tf_op jit(solution)/shard_map/ppermute | solution.py:622
  97.9 0.3 shard_map.51
  98.3 0.5 collective-permute-done.35.refs_5_
  99.0 1.9 %collective-permute-start.36 = (f32[12,2,8,128]{3,2,1,0:T(8,128)S(1)}, f32[12,2,8,128]{3,2,1,0:T(8,128)S(1)}, u32[]{:S(2)}, u32[]{:S(2)}) collective-permute-start(f32[12,2,8,128]{3,2,1,0:T(8,128)S(1)} %get-tuple-element.133), channel_id=1, source_target_pairs={{8,24},{24,8},{16,17},{17,16},{25,9},{9,25},{1,2},{2,1},{10,26},{2... | collective-permute-start | bytes 294920 | tf_op jit(solution)/shard_map/ppermute | solution.py:623
  101.0 3.2 %collective-permute-start.37 = (f32[24,8,128]{2,1,0:T(8,128)S(1)}, f32[24,8,128]{2,1,0:T(8,128)S(1)}, u32[]{:S(2)}, u32[]{:S(2)}) collective-permute-start(f32[24,8,128]{2,1,0:T(8,128)S(1)} %get-tuple-element.134), channel_id=1, source_target_pairs={{32,64},{64,32},{96,128},{128,96},{160,192},{192,160},{224,256},{2... | collective-permute-start | bytes 294920 | tf_op jit(solution)/shard_map/ppermute | solution.py:621
  104.2 2.3 %collective-permute-start.38 = (f32[24,8,128]{2,1,0:T(8,128)S(1)}, f32[24,8,128]{2,1,0:T(8,128)S(1)}, u32[]{:S(2)}, u32[]{:S(2)}) collective-permute-start(f32[24,8,128]{2,1,0:T(8,128)S(1)} %get-tuple-element.135), channel_id=1, source_target_pairs={{0,32},{32,0},{64,96},{96,64},{128,160},{160,128},{192,224},{224,1... | collective-permute-start | bytes 294920 | tf_op jit(solution)/shard_map/ppermute | solution.py:620
  106.6 3.8 %collective-permute-start.39 = (f32[12,2,8,128]{3,2,1,0:T(8,128)S(1)}, f32[12,2,8,128]{3,2,1,0:T(8,128)S(1)}, u32[]{:S(2)}, u32[]{:S(2)}) collective-permute-start(f32[12,2,8,128]{3,2,1,0:T(8,128)S(1)} %get-tuple-element.136), channel_id=1, source_target_pairs={{0,8},{8,0},{24,16},{16,24},{17,25},{25,17},{9,1},{1,9},{2,10},{10... | collective-permute-start | bytes 294920 | tf_op jit(solution)/shard_map/ppermute | solution.py:622
  110.4 0.3 shard_map.53.refs_0_
  110.7 0.6 collective-permute-done.39.refs_5_
  111.3 1.3 shard_map.54
  112.6 6.0 %all-to-all-start.6 = ((f32[32,8,128]{2,1,0:T(8,128)}), f32[32,8,128]{2,1,0:T(8,128)S(1)}, u32[]{:S(2)}, u32[]{:S(2)}) async-start(f32[32,8,128]{2,1,0:T(8,128)} %get-tuple-element.145), calls=%async_computation.6 | async-start | bytes 262144 | tf_op jit(solution)/shard_map/all_to_all | solution.py:725
  118.6 4.8 %collective-permute-start.40 = (f32[12,2,8,128]{3,2,1,0:T(8,128)S(1)}, f32[12,2,8,128]{3,2,1,0:T(8,128)S(1)}, u32[]{:S(2)}, u32[]{:S(2)}) collective-permute-start(f32[12,2,8,128]{3,2,1,0:T(8,128)S(1)} %get-tuple-element.141), channel_id=1, source_target_pairs={{8,24},{24,8},{16,17},{17,16},{25,9},{9,25},{1,2},{2,1},{10,26},{2... | collective-permute-start | bytes 294920 | tf_op jit(solution)/shard_map/ppermute | solution.py:623
  123.5 4.3 %collective-permute-start.41 = (f32[24,8,128]{2,1,0:T(8,128)S(1)}, f32[24,8,128]{2,1,0:T(8,128)S(1)}, u32[]{:S(2)}, u32[]{:S(2)}) collective-permute-start(f32[24,8,128]{2,1,0:T(8,128)S(1)} %get-tuple-element.142), channel_id=1, source_target_pairs={{32,64},{64,32},{96,128},{128,96},{160,192},{192,160},{224,256},{2... | collective-permute-start | bytes 294920 | tf_op jit(solution)/shard_map/ppermute | solution.py:621
  127.7 1.9 %collective-permute-start.42 = (f32[24,8,128]{2,1,0:T(8,128)S(1)}, f32[24,8,128]{2,1,0:T(8,128)S(1)}, u32[]{:S(2)}, u32[]{:S(2)}) collective-permute-start(f32[24,8,128]{2,1,0:T(8,128)S(1)} %get-tuple-element.143), channel_id=1, source_target_pairs={{0,32},{32,0},{64,96},{96,64},{128,160},{160,128},{192,224},{224,1... | collective-permute-start | bytes 294920 | tf_op jit(solution)/shard_map/ppermute | solution.py:620
  129.7 3.4 %collective-permute-start.43 = (f32[12,2,8,128]{3,2,1,0:T(8,128)S(1)}, f32[12,2,8,128]{3,2,1,0:T(8,128)S(1)}, u32[]{:S(2)}, u32[]{:S(2)}) collective-permute-start(f32[12,2,8,128]{3,2,1,0:T(8,128)S(1)} %get-tuple-element.144), channel_id=1, source_target_pairs={{0,8},{8,0},{24,16},{16,24},{17,25},{25,17},{9,1},{1,9},{2,10},{10... | collective-permute-start | bytes 294920 | tf_op jit(solution)/shard_map/ppermute | solution.py:622
  133.1 0.3 shard_map.55.refs_0_
  133.4 0.6 collective-permute-done.43.refs_5_
  134.0 0.9 shard_map.56
  134.9 7.1 %all-to-all-start.7 = ((f32[16,16,128]{2,1,0:T(8,128)}), f32[16,16,128]{2,1,0:T(8,128)S(1)}, u32[]{:S(2)}, u32[]{:S(2)}) async-start(f32[16,16,128]{2,1,0:T(8,128)} %get-tuple-element.146), calls=%async_computation.7 | async-start | bytes 262144 | tf_op jit(solution)/shard_map/all_to_all | solution.py:729
  142.0 2.2 %collective-permute-start.44 = (f32[12,2,8,128]{3,2,1,0:T(8,128)S(1)}, f32[12,2,8,128]{3,2,1,0:T(8,128)S(1)}, u32[]{:S(2)}, u32[]{:S(2)}) collective-permute-start(f32[12,2,8,128]{3,2,1,0:T(8,128)S(1)} %get-tuple-element.149), channel_id=1, source_target_pairs={{8,24},{24,8},{16,17},{17,16},{25,9},{9,25},{1,2},{2,1},{10,26},{2... | collective-permute-start | bytes 294920 | tf_op jit(solution)/shard_map/ppermute | solution.py:623
  144.2 4.5 %collective-permute-start.45 = (f32[24,8,128]{2,1,0:T(8,128)S(1)}, f32[24,8,128]{2,1,0:T(8,128)S(1)}, u32[]{:S(2)}, u32[]{:S(2)}) collective-permute-start(f32[24,8,128]{2,1,0:T(8,128)S(1)} %get-tuple-element.150), channel_id=1, source_target_pairs={{32,64},{64,32},{96,128},{128,96},{160,192},{192,160},{224,256},{2... | collective-permute-start | bytes 294920 | tf_op jit(solution)/shard_map/ppermute | solution.py:621
  148.6 1.9 %collective-permute-start.46 = (f32[24,8,128]{2,1,0:T(8,128)S(1)}, f32[24,8,128]{2,1,0:T(8,128)S(1)}, u32[]{:S(2)}, u32[]{:S(2)}) collective-permute-start(f32[24,8,128]{2,1,0:T(8,128)S(1)} %get-tuple-element.151), channel_id=1, source_target_pairs={{0,32},{32,0},{64,96},{96,64},{128,160},{160,128},{192,224},{224,1... | collective-permute-start | bytes 294920 | tf_op jit(solution)/shard_map/ppermute | solution.py:620
  150.6 4.3 %collective-permute-start.47 = (f32[12,2,8,128]{3,2,1,0:T(8,128)S(1)}, f32[12,2,8,128]{3,2,1,0:T(8,128)S(1)}, u32[]{:S(2)}, u32[]{:S(2)}) collective-permute-start(f32[12,2,8,128]{3,2,1,0:T(8,128)S(1)} %get-tuple-element.152), channel_id=1, source_target_pairs={{0,8},{8,0},{24,16},{16,24},{17,25},{25,17},{9,1},{1,9},{2,10},{10... | collective-permute-start | bytes 294920 | tf_op jit(solution)/shard_map/ppermute | solution.py:622
  154.9 0.3 shard_map.58.partial
  155.2 0.6 collective-permute-done.47.refs_3_
  155.8 1.1 shard_map.59
  156.9 4.9 %all-to-all-start.8 = ((f32[4,2,96,128]{3,2,1,0:T(8,128)}), f32[4,2,96,128]{3,2,1,0:T(8,128)S(1)}, u32[]{:S(2)}, u32[]{:S(2)}) async-start(f32[4,2,96,128]{3,2,1,0:T(8,128)} %bitcast.5), calls=%async_computation.8 | async-start | bytes 786432 | tf_op jit(solution)/shard_map/all_to_all | solution.py:679
  161.8 2.4 %shard_map.57 = (f32[16,8,128]{2,1,0:T(8,128)S(1)}, s32[1]{0:T(128)}) custom-call(f32[16,16,128]{2,1,0:T(8,128)S(1)} %all-to-all-done.7.rows), custom_call_target="tpu_custom_call" | custom-call | flops 100000 | bytes 131072 | tf_op jit(solution)/shard_map/pallas_call | solution.py:34
  164.9 5.0 %all-to-all-done.8 = f32[4,2,96,128]{3,2,1,0:T(8,128)S(1)} async-done(((f32[4,2,96,128]{3,2,1,0:T(8,128)}), f32[4,2,96,128]{3,2,1,0:T(8,128)S(1)}, u32[]{:S(2)}, u32[]{:S(2)}) %all-to-all-start.8) | async-done | bytes 393248 | tf_op jit(solution)/shard_map/all_to_all | solution.py:679
  169.9 1.5 conditional.1
  169.9 1.5 branch_1_fun.1
  (32 shorter events, 0.7 us)
Async XLA Ops:
  0.6 1.0 copy-start
  23.4 17.8 %collective-permute-start.16 = (f32[12,2,8,128]{3,2,1,0:T(8,128)S(1)}, f32[12,2,8,128]{3,2,1,0:T(8,128)S(1)}, u32[]{:S(2)}, u32[]{:S(2)}) collective-permute-start(f32[12,2,8,128]{3,2,1,0:T(8,128)S(1)} %get-tuple-element.106), channel_id=1, source_target_pairs={{8,24},{24,8},{16,17},{17,16},{25,9},{9,25},{1,2},{2,1},{10,26},{2... | collective-permute-start | bytes 294920 | tf_op jit(solution)/shard_map/ppermute | solution.py:623
  25.8 15.5 %collective-permute-start.17 = (f32[24,8,128]{2,1,0:T(8,128)S(1)}, f32[24,8,128]{2,1,0:T(8,128)S(1)}, u32[]{:S(2)}, u32[]{:S(2)}) collective-permute-start(f32[24,8,128]{2,1,0:T(8,128)S(1)} %get-tuple-element.107), channel_id=1, source_target_pairs={{32,64},{64,32},{96,128},{128,96},{160,192},{192,160},{224,256},{2... | collective-permute-start | bytes 294920 | tf_op jit(solution)/shard_map/ppermute | solution.py:621
  33.3 8.0 %collective-permute-start.18 = (f32[24,8,128]{2,1,0:T(8,128)S(1)}, f32[24,8,128]{2,1,0:T(8,128)S(1)}, u32[]{:S(2)}, u32[]{:S(2)}) collective-permute-start(f32[24,8,128]{2,1,0:T(8,128)S(1)} %get-tuple-element.108), channel_id=1, source_target_pairs={{0,32},{32,0},{64,96},{96,64},{128,160},{160,128},{192,224},{224,1... | collective-permute-start | bytes 294920 | tf_op jit(solution)/shard_map/ppermute | solution.py:620
  35.2 6.7 %collective-permute-start.19 = (f32[12,2,8,128]{3,2,1,0:T(8,128)S(1)}, f32[12,2,8,128]{3,2,1,0:T(8,128)S(1)}, u32[]{:S(2)}, u32[]{:S(2)}) collective-permute-start(f32[12,2,8,128]{3,2,1,0:T(8,128)S(1)} %get-tuple-element.109), channel_id=1, source_target_pairs={{0,8},{8,0},{24,16},{16,24},{17,25},{25,17},{9,1},{1,9},{2,10},{10... | collective-permute-start | bytes 294920 | tf_op jit(solution)/shard_map/ppermute | solution.py:622
  42.1 11.4 %collective-permute-start.20 = (f32[12,2,8,128]{3,2,1,0:T(8,128)S(1)}, f32[12,2,8,128]{3,2,1,0:T(8,128)S(1)}, u32[]{:S(2)}, u32[]{:S(2)}) collective-permute-start(f32[12,2,8,128]{3,2,1,0:T(8,128)S(1)} %get-tuple-element.111), channel_id=1, source_target_pairs={{8,24},{24,8},{16,17},{17,16},{25,9},{9,25},{1,2},{2,1},{10,26},{2... | collective-permute-start | bytes 294920 | tf_op jit(solution)/shard_map/ppermute | solution.py:623
  44.6 8.9 %collective-permute-start.21 = (f32[24,8,128]{2,1,0:T(8,128)S(1)}, f32[24,8,128]{2,1,0:T(8,128)S(1)}, u32[]{:S(2)}, u32[]{:S(2)}) collective-permute-start(f32[24,8,128]{2,1,0:T(8,128)S(1)} %get-tuple-element.112), channel_id=1, source_target_pairs={{32,64},{64,32},{96,128},{128,96},{160,192},{192,160},{224,256},{2... | collective-permute-start | bytes 294920 | tf_op jit(solution)/shard_map/ppermute | solution.py:621
  47.6 5.9 %collective-permute-start.22 = (f32[24,8,128]{2,1,0:T(8,128)S(1)}, f32[24,8,128]{2,1,0:T(8,128)S(1)}, u32[]{:S(2)}, u32[]{:S(2)}) collective-permute-start(f32[24,8,128]{2,1,0:T(8,128)S(1)} %get-tuple-element.113), channel_id=1, source_target_pairs={{0,32},{32,0},{64,96},{96,64},{128,160},{160,128},{192,224},{224,1... | collective-permute-start | bytes 294920 | tf_op jit(solution)/shard_map/ppermute | solution.py:620
  49.6 4.6 %collective-permute-start.23 = (f32[12,2,8,128]{3,2,1,0:T(8,128)S(1)}, f32[12,2,8,128]{3,2,1,0:T(8,128)S(1)}, u32[]{:S(2)}, u32[]{:S(2)}) collective-permute-start(f32[12,2,8,128]{3,2,1,0:T(8,128)S(1)} %get-tuple-element.114), channel_id=1, source_target_pairs={{0,8},{8,0},{24,16},{16,24},{17,25},{25,17},{9,1},{1,9},{2,10},{10... | collective-permute-start | bytes 294920 | tf_op jit(solution)/shard_map/ppermute | solution.py:622
  54.4 15.4 %collective-permute-start.24 = (f32[12,2,8,128]{3,2,1,0:T(8,128)S(1)}, f32[12,2,8,128]{3,2,1,0:T(8,128)S(1)}, u32[]{:S(2)}, u32[]{:S(2)}) collective-permute-start(f32[12,2,8,128]{3,2,1,0:T(8,128)S(1)} %get-tuple-element.117), channel_id=1, source_target_pairs={{8,24},{24,8},{16,17},{17,16},{25,9},{9,25},{1,2},{2,1},{10,26},{2... | collective-permute-start | bytes 294920 | tf_op jit(solution)/shard_map/ppermute | solution.py:623
  58.1 11.7 %collective-permute-start.25 = (f32[24,8,128]{2,1,0:T(8,128)S(1)}, f32[24,8,128]{2,1,0:T(8,128)S(1)}, u32[]{:S(2)}, u32[]{:S(2)}) collective-permute-start(f32[24,8,128]{2,1,0:T(8,128)S(1)} %get-tuple-element.118), channel_id=1, source_target_pairs={{32,64},{64,32},{96,128},{128,96},{160,192},{192,160},{224,256},{2... | collective-permute-start | bytes 294920 | tf_op jit(solution)/shard_map/ppermute | solution.py:621
  62.4 7.4 %collective-permute-start.26 = (f32[24,8,128]{2,1,0:T(8,128)S(1)}, f32[24,8,128]{2,1,0:T(8,128)S(1)}, u32[]{:S(2)}, u32[]{:S(2)}) collective-permute-start(f32[24,8,128]{2,1,0:T(8,128)S(1)} %get-tuple-element.119), channel_id=1, source_target_pairs={{0,32},{32,0},{64,96},{96,64},{128,160},{160,128},{192,224},{224,1... | collective-permute-start | bytes 294920 | tf_op jit(solution)/shard_map/ppermute | solution.py:620
  64.4 6.0 %collective-permute-start.27 = (f32[12,2,8,128]{3,2,1,0:T(8,128)S(1)}, f32[12,2,8,128]{3,2,1,0:T(8,128)S(1)}, u32[]{:S(2)}, u32[]{:S(2)}) collective-permute-start(f32[12,2,8,128]{3,2,1,0:T(8,128)S(1)} %get-tuple-element.120), channel_id=1, source_target_pairs={{0,8},{8,0},{24,16},{16,24},{17,25},{25,17},{9,1},{1,9},{2,10},{10... | collective-permute-start | bytes 294920 | tf_op jit(solution)/shard_map/ppermute | solution.py:622
  70.6 11.6 %collective-permute-start.28 = (f32[12,2,8,128]{3,2,1,0:T(8,128)S(1)}, f32[12,2,8,128]{3,2,1,0:T(8,128)S(1)}, u32[]{:S(2)}, u32[]{:S(2)}) collective-permute-start(f32[12,2,8,128]{3,2,1,0:T(8,128)S(1)} %get-tuple-element.122), channel_id=1, source_target_pairs={{8,24},{24,8},{16,17},{17,16},{25,9},{9,25},{1,2},{2,1},{10,26},{2... | collective-permute-start | bytes 294920 | tf_op jit(solution)/shard_map/ppermute | solution.py:623
  72.7 9.4 %collective-permute-start.29 = (f32[24,8,128]{2,1,0:T(8,128)S(1)}, f32[24,8,128]{2,1,0:T(8,128)S(1)}, u32[]{:S(2)}, u32[]{:S(2)}) collective-permute-start(f32[24,8,128]{2,1,0:T(8,128)S(1)} %get-tuple-element.123), channel_id=1, source_target_pairs={{32,64},{64,32},{96,128},{128,96},{160,192},{192,160},{224,256},{2... | collective-permute-start | bytes 294920 | tf_op jit(solution)/shard_map/ppermute | solution.py:621
  75.7 6.5 %collective-permute-start.30 = (f32[24,8,128]{2,1,0:T(8,128)S(1)}, f32[24,8,128]{2,1,0:T(8,128)S(1)}, u32[]{:S(2)}, u32[]{:S(2)}) collective-permute-start(f32[24,8,128]{2,1,0:T(8,128)S(1)} %get-tuple-element.124), channel_id=1, source_target_pairs={{0,32},{32,0},{64,96},{96,64},{128,160},{160,128},{192,224},{224,1... | collective-permute-start | bytes 294920 | tf_op jit(solution)/shard_map/ppermute | solution.py:620
  78.1 4.7 %collective-permute-start.31 = (f32[12,2,8,128]{3,2,1,0:T(8,128)S(1)}, f32[12,2,8,128]{3,2,1,0:T(8,128)S(1)}, u32[]{:S(2)}, u32[]{:S(2)}) collective-permute-start(f32[12,2,8,128]{3,2,1,0:T(8,128)S(1)} %get-tuple-element.125), channel_id=1, source_target_pairs={{0,8},{8,0},{24,16},{16,24},{17,25},{25,17},{9,1},{1,9},{2,10},{10... | collective-permute-start | bytes 294920 | tf_op jit(solution)/shard_map/ppermute | solution.py:622
  83.0 15.2 %collective-permute-start.32 = (f32[12,2,8,128]{3,2,1,0:T(8,128)S(1)}, f32[12,2,8,128]{3,2,1,0:T(8,128)S(1)}, u32[]{:S(2)}, u32[]{:S(2)}) collective-permute-start(f32[12,2,8,128]{3,2,1,0:T(8,128)S(1)} %get-tuple-element.128), channel_id=1, source_target_pairs={{8,24},{24,8},{16,17},{17,16},{25,9},{9,25},{1,2},{2,1},{10,26},{2... | collective-permute-start | bytes 294920 | tf_op jit(solution)/shard_map/ppermute | solution.py:623
  86.3 11.9 %collective-permute-start.33 = (f32[24,8,128]{2,1,0:T(8,128)S(1)}, f32[24,8,128]{2,1,0:T(8,128)S(1)}, u32[]{:S(2)}, u32[]{:S(2)}) collective-permute-start(f32[24,8,128]{2,1,0:T(8,128)S(1)} %get-tuple-element.129), channel_id=1, source_target_pairs={{32,64},{64,32},{96,128},{128,96},{160,192},{192,160},{224,256},{2... | collective-permute-start | bytes 294920 | tf_op jit(solution)/shard_map/ppermute | solution.py:621
  90.9 7.4 %collective-permute-start.34 = (f32[24,8,128]{2,1,0:T(8,128)S(1)}, f32[24,8,128]{2,1,0:T(8,128)S(1)}, u32[]{:S(2)}, u32[]{:S(2)}) collective-permute-start(f32[24,8,128]{2,1,0:T(8,128)S(1)} %get-tuple-element.130), channel_id=1, source_target_pairs={{0,32},{32,0},{64,96},{96,64},{128,160},{160,128},{192,224},{224,1... | collective-permute-start | bytes 294920 | tf_op jit(solution)/shard_map/ppermute | solution.py:620
  92.8 6.0 %collective-permute-start.35 = (f32[12,2,8,128]{3,2,1,0:T(8,128)S(1)}, f32[12,2,8,128]{3,2,1,0:T(8,128)S(1)}, u32[]{:S(2)}, u32[]{:S(2)}) collective-permute-start(f32[12,2,8,128]{3,2,1,0:T(8,128)S(1)} %get-tuple-element.131), channel_id=1, source_target_pairs={{0,8},{8,0},{24,16},{16,24},{17,25},{25,17},{9,1},{1,9},{2,10},{10... | collective-permute-start | bytes 294920 | tf_op jit(solution)/shard_map/ppermute | solution.py:622
  99.0 11.6 %collective-permute-start.36 = (f32[12,2,8,128]{3,2,1,0:T(8,128)S(1)}, f32[12,2,8,128]{3,2,1,0:T(8,128)S(1)}, u32[]{:S(2)}, u32[]{:S(2)}) collective-permute-start(f32[12,2,8,128]{3,2,1,0:T(8,128)S(1)} %get-tuple-element.133), channel_id=1, source_target_pairs={{8,24},{24,8},{16,17},{17,16},{25,9},{9,25},{1,2},{2,1},{10,26},{2... | collective-permute-start | bytes 294920 | tf_op jit(solution)/shard_map/ppermute | solution.py:623
  101.0 9.7 %collective-permute-start.37 = (f32[24,8,128]{2,1,0:T(8,128)S(1)}, f32[24,8,128]{2,1,0:T(8,128)S(1)}, u32[]{:S(2)}, u32[]{:S(2)}) collective-permute-start(f32[24,8,128]{2,1,0:T(8,128)S(1)} %get-tuple-element.134), channel_id=1, source_target_pairs={{32,64},{64,32},{96,128},{128,96},{160,192},{192,160},{224,256},{2... | collective-permute-start | bytes 294920 | tf_op jit(solution)/shard_map/ppermute | solution.py:621
  104.2 6.5 %collective-permute-start.38 = (f32[24,8,128]{2,1,0:T(8,128)S(1)}, f32[24,8,128]{2,1,0:T(8,128)S(1)}, u32[]{:S(2)}, u32[]{:S(2)}) collective-permute-start(f32[24,8,128]{2,1,0:T(8,128)S(1)} %get-tuple-element.135), channel_id=1, source_target_pairs={{0,32},{32,0},{64,96},{96,64},{128,160},{160,128},{192,224},{224,1... | collective-permute-start | bytes 294920 | tf_op jit(solution)/shard_map/ppermute | solution.py:620
  106.6 4.7 %collective-permute-start.39 = (f32[12,2,8,128]{3,2,1,0:T(8,128)S(1)}, f32[12,2,8,128]{3,2,1,0:T(8,128)S(1)}, u32[]{:S(2)}, u32[]{:S(2)}) collective-permute-start(f32[12,2,8,128]{3,2,1,0:T(8,128)S(1)} %get-tuple-element.136), channel_id=1, source_target_pairs={{0,8},{8,0},{24,16},{16,24},{17,25},{25,17},{9,1},{1,9},{2,10},{10... | collective-permute-start | bytes 294920 | tf_op jit(solution)/shard_map/ppermute | solution.py:622
  112.6 21.4 %all-to-all-start.6 = ((f32[32,8,128]{2,1,0:T(8,128)}), f32[32,8,128]{2,1,0:T(8,128)S(1)}, u32[]{:S(2)}, u32[]{:S(2)}) async-start(f32[32,8,128]{2,1,0:T(8,128)} %get-tuple-element.145), calls=%async_computation.6 | async-start | bytes 262144 | tf_op jit(solution)/shard_map/all_to_all | solution.py:725
  118.6 14.7 %collective-permute-start.40 = (f32[12,2,8,128]{3,2,1,0:T(8,128)S(1)}, f32[12,2,8,128]{3,2,1,0:T(8,128)S(1)}, u32[]{:S(2)}, u32[]{:S(2)}) collective-permute-start(f32[12,2,8,128]{3,2,1,0:T(8,128)S(1)} %get-tuple-element.141), channel_id=1, source_target_pairs={{8,24},{24,8},{16,17},{17,16},{25,9},{9,25},{1,2},{2,1},{10,26},{2... | collective-permute-start | bytes 294920 | tf_op jit(solution)/shard_map/ppermute | solution.py:623
  123.5 9.9 %collective-permute-start.41 = (f32[24,8,128]{2,1,0:T(8,128)S(1)}, f32[24,8,128]{2,1,0:T(8,128)S(1)}, u32[]{:S(2)}, u32[]{:S(2)}) collective-permute-start(f32[24,8,128]{2,1,0:T(8,128)S(1)} %get-tuple-element.142), channel_id=1, source_target_pairs={{32,64},{64,32},{96,128},{128,96},{160,192},{192,160},{224,256},{2... | collective-permute-start | bytes 294920 | tf_op jit(solution)/shard_map/ppermute | solution.py:621
  127.7 5.6 %collective-permute-start.42 = (f32[24,8,128]{2,1,0:T(8,128)S(1)}, f32[24,8,128]{2,1,0:T(8,128)S(1)}, u32[]{:S(2)}, u32[]{:S(2)}) collective-permute-start(f32[24,8,128]{2,1,0:T(8,128)S(1)} %get-tuple-element.143), channel_id=1, source_target_pairs={{0,32},{32,0},{64,96},{96,64},{128,160},{160,128},{192,224},{224,1... | collective-permute-start | bytes 294920 | tf_op jit(solution)/shard_map/ppermute | solution.py:620
  129.7 4.3 %collective-permute-start.43 = (f32[12,2,8,128]{3,2,1,0:T(8,128)S(1)}, f32[12,2,8,128]{3,2,1,0:T(8,128)S(1)}, u32[]{:S(2)}, u32[]{:S(2)}) collective-permute-start(f32[12,2,8,128]{3,2,1,0:T(8,128)S(1)} %get-tuple-element.144), channel_id=1, source_target_pairs={{0,8},{8,0},{24,16},{16,24},{17,25},{25,17},{9,1},{1,9},{2,10},{10... | collective-permute-start | bytes 294920 | tf_op jit(solution)/shard_map/ppermute | solution.py:622
  134.9 22.0 %all-to-all-start.7 = ((f32[16,16,128]{2,1,0:T(8,128)}), f32[16,16,128]{2,1,0:T(8,128)S(1)}, u32[]{:S(2)}, u32[]{:S(2)}) async-start(f32[16,16,128]{2,1,0:T(8,128)} %get-tuple-element.146), calls=%async_computation.7 | async-start | bytes 262144 | tf_op jit(solution)/shard_map/all_to_all | solution.py:729
  142.0 13.2 %collective-permute-start.44 = (f32[12,2,8,128]{3,2,1,0:T(8,128)S(1)}, f32[12,2,8,128]{3,2,1,0:T(8,128)S(1)}, u32[]{:S(2)}, u32[]{:S(2)}) collective-permute-start(f32[12,2,8,128]{3,2,1,0:T(8,128)S(1)} %get-tuple-element.149), channel_id=1, source_target_pairs={{8,24},{24,8},{16,17},{17,16},{25,9},{9,25},{1,2},{2,1},{10,26},{2... | collective-permute-start | bytes 294920 | tf_op jit(solution)/shard_map/ppermute | solution.py:623
  144.2 11.0 %collective-permute-start.45 = (f32[24,8,128]{2,1,0:T(8,128)S(1)}, f32[24,8,128]{2,1,0:T(8,128)S(1)}, u32[]{:S(2)}, u32[]{:S(2)}) collective-permute-start(f32[24,8,128]{2,1,0:T(8,128)S(1)} %get-tuple-element.150), channel_id=1, source_target_pairs={{32,64},{64,32},{96,128},{128,96},{160,192},{192,160},{224,256},{2... | collective-permute-start | bytes 294920 | tf_op jit(solution)/shard_map/ppermute | solution.py:621
  148.6 6.5 %collective-permute-start.46 = (f32[24,8,128]{2,1,0:T(8,128)S(1)}, f32[24,8,128]{2,1,0:T(8,128)S(1)}, u32[]{:S(2)}, u32[]{:S(2)}) collective-permute-start(f32[24,8,128]{2,1,0:T(8,128)S(1)} %get-tuple-element.151), channel_id=1, source_target_pairs={{0,32},{32,0},{64,96},{96,64},{128,160},{160,128},{192,224},{224,1... | collective-permute-start | bytes 294920 | tf_op jit(solution)/shard_map/ppermute | solution.py:620
  150.6 5.2 %collective-permute-start.47 = (f32[12,2,8,128]{3,2,1,0:T(8,128)S(1)}, f32[12,2,8,128]{3,2,1,0:T(8,128)S(1)}, u32[]{:S(2)}, u32[]{:S(2)}) collective-permute-start(f32[12,2,8,128]{3,2,1,0:T(8,128)S(1)} %get-tuple-element.152), channel_id=1, source_target_pairs={{0,8},{8,0},{24,16},{16,24},{17,25},{25,17},{9,1},{1,9},{2,10},{10... | collective-permute-start | bytes 294920 | tf_op jit(solution)/shard_map/ppermute | solution.py:622
  155.1 14.7 %copy-start.1 = (f32[4,2,4,3,2,2,128]{6,5,4,3,2,1,0:T(2,128)S(1)}, f32[4,2,4,3,2,2,128]{6,5,4,3,2,1,0:T(2,128)}, u32[]{:S(2)}) copy-start(f32[4,2,4,3,2,2,128]{6,5,4,3,2,1,0:T(2,128)} %param.4) | copy-start | bytes 589828
  156.9 13.0 %all-to-all-start.8 = ((f32[4,2,96,128]{3,2,1,0:T(8,128)}), f32[4,2,96,128]{3,2,1,0:T(8,128)S(1)}, u32[]{:S(2)}, u32[]{:S(2)}) async-start(f32[4,2,96,128]{3,2,1,0:T(8,128)} %bitcast.5), calls=%async_computation.8 | async-start | bytes 786432 | tf_op jit(solution)/shard_map/all_to_all | solution.py:679
